TPU v7x, 128 devices: a whole 4x4x4 slice. The times are simulated.
128 devices in a mesh: batch: 8 (over z, y_lo), head: 4 (over x), blk: 4 (over y_hi, core).
Axes of the slice: x: 4, y: 4 (y_hi: 2, y_lo: 2; y = y_hi * 2 + y_lo), z: 4, core: 2. Of those that a mesh axis runs over, the one named last changes fastest.
Arguments:
- inputs: bfloat16 [8, 2048, 768], P('batch', ('head', 'blk')), may hold values from -4 to 4
- lengths: int32 [8], P('batch'), may hold values from 1025 to 2048, as said below
- joint_weight: bfloat16 [2, 768, 2304], P(None, ('batch', 'blk')), may hold values from -0.21875 to 0.21875
- query_bias: bfloat16 [2, 768], P(None, ('batch', 'blk')), may hold values from -1.1953125 to 1.1953125
- value_bias: bfloat16 [2, 768], P(None, ('batch', 'blk')), may hold values from -0.3984375 to 0.3984375
- output_weight: bfloat16 [2, 768, 768], P(None, ('batch', 'blk')), may hold values from -0.75 to 0.75
- output_bias: bfloat16 [2, 768], P(None, ('batch', 'blk')), may hold values from -0.3984375 to 0.3984375
- first_gain: bfloat16 [2, 768], P(None, ('batch', 'blk')), may hold values from 0.5 to 1.5
- first_shift: bfloat16 [2, 768], P(None, ('batch', 'blk')), may hold values from -0.3984375 to 0.3984375
- up_weight: bfloat16 [2, 768, 3072], P(None, ('batch', 'blk')), may hold values from -0.21875 to 0.21875
- up_bias: bfloat16 [2, 3072], P(None, ('batch', 'blk')), may hold values from -1.1953125 to 1.1953125
- down_weight: bfloat16 [2, 3072, 768], P(None, ('batch', 'blk')), may hold values from -0.15625 to 0.15625
- down_bias: bfloat16 [2, 768], P(None, ('batch', 'blk')), may hold values from -0.3984375 to 0.3984375
- second_gain: bfloat16 [2, 768], P(None, ('batch', 'blk')), may hold values from 0.5 to 1.5
- second_shift: bfloat16 [2, 768], P(None, ('batch', 'blk')), may hold values from -0.3984375 to 0.3984375
- cotangent: bfloat16 [8, 2048, 768], P('batch', ('head', 'blk')), may hold values from -4 to 4
Outputs:
- activations: bfloat16 [2, 8, 2048, 768], P(None, 'batch', ('head', 'blk'))
- input_grad: float32 [8, 2048, 768], P('batch', ('head', 'blk'))
- joint_weight_grad: float32 [2, 768, 2304], P(None, ('batch', 'blk'))
- query_bias_grad: float32 [2, 768], P(None, ('batch', 'blk'))
- value_bias_grad: float32 [2, 768], P(None, ('batch', 'blk'))
- output_weight_grad: float32 [2, 768, 768], P(None, ('batch', 'blk'))
- output_bias_grad: float32 [2, 768], P(None, ('batch', 'blk'))
- first_gain_grad: float32 [2, 768], P(None, ('batch', 'blk'))
- first_shift_grad: float32 [2, 768], P(None, ('batch', 'blk'))
- up_weight_grad: float32 [2, 768, 3072], P(None, ('batch', 'blk'))
- up_bias_grad: float32 [2, 3072], P(None, ('batch', 'blk'))
- down_weight_grad: float32 [2, 3072, 768], P(None, ('batch', 'blk'))
- down_bias_grad: float32 [2, 768], P(None, ('batch', 'blk'))
- second_gain_grad: float32 [2, 768], P(None, ('batch', 'blk'))
- second_shift_grad: float32 [2, 768], P(None, ('batch', 'blk'))
Inputs may be any that keep to these rules, and one draw needn't show every extreme that they name: Positions lengths[b] and later of sequence b are padding, whose keys are masked.
All inputs are finite; a program needn't handle non-finite values.
Results may differ from a plain program's by a relative error of at most 0.025.
Values may be sent and summed in bfloat16 or wider, within the bound.
A program may use at most 256 MiB of HBM per device.

v0:
```python
import jax
import jax.numpy as jnp
from jax import lax
from jax.sharding import PartitionSpec as P

HEADS = 12
HD = 64
LAYERS = 2


EPSILON = 1e-12
MASKED = -1e30


def in_one_piece(arrays, axis, dim, along):
    columns = [a.reshape(*a.shape[:along], -1) for a in arrays]
    both = jnp.concatenate(columns, axis=along)
    whole, at, outs = (lax.all_gather(both, axis, axis=dim, tiled=True), 0, [])
    for a, column in zip(arrays, columns):
        share = whole[..., at : at + column.shape[along]]
        outs.append(share.reshape(*share.shape[:along], *a.shape[along:]))
        at += column.shape[along]
    return tuple(outs)


def sent_together(arrays, axis, split_dim, concat_dim, along):
    widths = [a.shape[along] for a in arrays]
    both = jnp.concatenate(arrays, axis=along)
    whole = lax.all_to_all(both, axis, split_axis=split_dim, concat_axis=concat_dim, tiled=True)
    return tuple(jnp.split(whole, [sum(widths[:k]) for k in range(1, len(widths))], axis=along))


def sent_together_2(arrays, axis, dim, along):
    widths = [a.shape[along] for a in arrays]
    both = jnp.concatenate(arrays, axis=along)
    whole = lax.all_gather(both, axis, axis=dim, tiled=True)
    return tuple(jnp.split(whole, [sum(widths[:k]) for k in range(1, len(widths))], axis=along))


def cut_along(array, dim, length):
    dims = array.shape
    blocks = array.reshape(*dims[:dim], length, dims[dim] // length, *dims[dim + 1 :])
    return jnp.moveaxis(blocks, dim, 0)


def sum_at_owner(array, axis, dim):
    length = lax.axis_size(axis)
    blocks = lax.all_to_all(cut_along(array, dim, length), axis, 0, 0, tiled=True)
    return jnp.sum(blocks.astype(jnp.float32), axis=0)


def side_by_side(arrays, axis, dim, along):
    columns = [a.reshape(*a.shape[:along], -1) for a in arrays]
    both = jnp.concatenate(columns, axis=along)
    whole, at, outs = (lax.psum_scatter(both, axis, scatter_dimension=dim, tiled=True), 0, [])
    for a, column in zip(arrays, columns):
        share = whole[..., at : at + column.shape[along]]
        outs.append(share.reshape(*share.shape[:along], *a.shape[along:]))
        at += column.shape[along]
    return tuple(outs)


def sent_to_all(array, axis):
    length = lax.axis_size(axis)
    return lax.all_to_all(
        jnp.broadcast_to(array[None], (length, *array.shape)), axis, 0, 0, tiled=True
    )


def of_everyone(array, axis):
    return sent_to_all(array, axis).astype(jnp.float32).sum(axis=0)


def layer_norm(values, gain, shift):
    average = jnp.mean(values, axis=-1, keepdims=True)
    centered = values - average
    variance = jnp.mean(centered * centered, axis=-1, keepdims=True)
    return centered * lax.rsqrt(variance + EPSILON) * gain + shift


def exact_gelu(values):
    return jax.nn.gelu(values, approximate=False)


def row_product(operand, matrix):
    return jnp.dot(operand, matrix, preferred_element_type=jnp.float32)


def inner_rows(operand, other):
    return lax.dot_general(
        operand, other, (((0,), (0,)), ((), ())), preferred_element_type=jnp.float32
    )


def times_transposed(operand, matrix):
    return lax.dot_general(
        operand, matrix, (((1,), (1,)), ((), ())), preferred_element_type=jnp.float32
    )


def gather_forward(parts):
    return (
        *in_one_piece(
            (parts[0], parts[1], parts[2], parts[3], parts[4], parts[5], parts[6], parts[7]),
            ("batch", "blk"),
            0,
            1,
        ),
        *in_one_piece((parts[8], parts[9]), ("batch", "blk"), 0, 1),
        lax.all_gather(parts[10], ("batch", "blk"), axis=0, tiled=True),
        lax.all_gather(parts[11], ("batch", "blk"), axis=0, tiled=True),
        lax.all_gather(parts[12], ("batch", "blk"), axis=0, tiled=True),
    )


def gather_backward(parts):
    return (
        *in_one_piece(
            (parts[0], parts[1], parts[2], parts[3], parts[4], parts[5], parts[6], parts[7]),
            ("batch", "blk"),
            0,
            1,
        ),
        *in_one_piece((parts[8], parts[9]), ("batch", "blk"), 0, 1),
        lax.all_gather(parts[10], ("batch", "blk"), axis=0, tiled=True),
        lax.all_gather(parts[11], ("batch", "blk"), axis=0, tiled=True),
        lax.all_gather(parts[12], ("batch", "blk"), axis=0, tiled=True),
    )


def column_sums(values):
    return jnp.sum(values.astype(jnp.float32), axis=tuple(range(values.ndim - 1)))


def body(
    inputs,
    lengths,
    joint_weight,
    query_bias,
    value_bias,
    output_weight,
    output_bias,
    first_gain,
    first_shift,
    up_weight,
    up_bias,
    down_weight,
    down_bias,
    second_gain,
    second_shift,
    cotangent,
):
    shards = (
        joint_weight,
        query_bias,
        value_bias,
        output_weight,
        output_bias,
        first_gain,
        first_shift,
        up_weight,
        up_bias,
        down_weight,
        down_bias,
        second_gain,
        second_shift,
    )
    seq_count, tok_count, width = inputs.shape
    row_count = seq_count * tok_count
    head_devices = lax.axis_size("head")
    blk_devices = lax.axis_size("blk")
    group_heads = HEADS // head_devices
    score_scale = HD ** (-0.5)
    block_rows = head_devices * tok_count
    places = jnp.arange(blk_devices * block_rows, dtype=jnp.int32)
    block_index = places // block_rows
    within = places % block_rows
    key_places = (within // tok_count * blk_devices + block_index) * tok_count + within % tok_count

    def masked_scores(query, key_rows, length):
        query_heads = query.reshape(query.shape[0], group_heads, HD)
        key_heads = key_rows.reshape(key_rows.shape[0], group_heads, HD)
        raw_scores = jnp.einsum(
            "qhe,khe->hqk", query_heads, key_heads, preferred_element_type=jnp.float32
        )
        key_valid = key_places < length
        return jnp.where(key_valid[None, None, :], raw_scores * score_scale, MASKED)

    def attend_forward(sequence_items):
        query, key_rows, value_rows, length = sequence_items
        scores = masked_scores(query, key_rows, length)
        row_peak = jnp.max(scores, axis=-1, keepdims=True)
        shifted = jnp.exp(scores - row_peak)
        row_total = jnp.sum(shifted, axis=-1, keepdims=True)
        probabilities = (shifted / row_total).astype(jnp.bfloat16)
        value_heads = value_rows.reshape(value_rows.shape[0], group_heads, HD)
        mixed_heads = jnp.einsum(
            "hqk,khe->qhe", probabilities, value_heads, preferred_element_type=jnp.float32
        )
        log_total = row_peak[..., 0] + jnp.log(row_total[..., 0])
        return (mixed_heads.reshape(query.shape[0], -1).astype(jnp.bfloat16), log_total)

    def attend_backward(sequence_items):
        query, key_rows, value_rows, length, log_total, grad_mixed = sequence_items
        scores = masked_scores(query, key_rows, length)
        probabilities = jnp.exp(scores - log_total[..., None])
        query_heads = query.reshape(query.shape[0], group_heads, HD)
        key_heads = key_rows.reshape(key_rows.shape[0], group_heads, HD)
        value_heads = value_rows.reshape(value_rows.shape[0], group_heads, HD)
        grad_heads = grad_mixed.reshape(grad_mixed.shape[0], group_heads, HD)
        grad_probs = jnp.einsum(
            "qhe,khe->hqk", grad_heads, value_heads, preferred_element_type=jnp.float32
        )
        row_inner = jnp.sum(probabilities * grad_probs, axis=-1, keepdims=True)
        grad_scores = (probabilities * (grad_probs - row_inner) * score_scale).astype(jnp.bfloat16)
        grad_query = jnp.einsum(
            "hqk,khe->qhe", grad_scores, key_heads, preferred_element_type=jnp.float32
        )
        key_term = jnp.einsum(
            "hqk,qhe->khe", grad_scores, query_heads, preferred_element_type=jnp.float32
        )
        value_term = jnp.einsum(
            "hqk,qhe->khe",
            probabilities.astype(jnp.bfloat16),
            grad_heads,
            preferred_element_type=jnp.float32,
        )
        key_total = key_rows.shape[0]
        pair_term = jnp.concatenate(
            [key_term.reshape(key_total, -1), value_term.reshape(key_total, -1)], axis=-1
        )
        return (grad_query.reshape(query.shape[0], -1).astype(jnp.bfloat16), pair_term)

    hidden = inputs.reshape(row_count, width)
    kept = []
    outputs = []
    for layer_index in range(LAYERS):
        weights = gather_forward(tuple((shard[layer_index] for shard in shards)))
        (
            joint_full,
            query_add,
            value_add,
            out_full,
            out_add,
            gain_first,
            shift_first,
            up_full,
            up_add,
            down_full,
            down_add,
            gain_second,
            shift_second,
        ) = weights
        projected = row_product(hidden, joint_full)
        query = (
            (projected[:, :width] + query_add)
            .astype(jnp.bfloat16)
            .reshape(seq_count, tok_count, width)
        )
        key_rows = (
            projected[:, width : 2 * width]
            .astype(jnp.bfloat16)
            .reshape(seq_count, tok_count, width)
        )
        value_rows = (
            (projected[:, 2 * width :] + value_add)
            .astype(jnp.bfloat16)
            .reshape(seq_count, tok_count, width)
        )
        query_group, key_group, value_group = sent_together(
            (query, key_rows, value_rows), "head", 2, 1, 0
        )
        key_all, value_all = sent_together_2((key_group, value_group), "blk", 1, 0)
        mixed_group, log_total = lax.map(attend_forward, (query_group, key_all, value_all, lengths))
        mixed_rows = lax.all_to_all(
            mixed_group, "head", split_axis=1, concat_axis=2, tiled=True
        ).reshape(row_count, width)
        branch = row_product(mixed_rows, out_full) + out_add
        before_first = hidden.astype(jnp.float32) + branch
        first_norm = layer_norm(before_first, gain_first, shift_first)
        first_low = first_norm.astype(jnp.bfloat16)
        upward = row_product(first_low, up_full) + up_add
        activated = exact_gelu(upward).astype(jnp.bfloat16)
        before_second = first_norm + (row_product(activated, down_full) + down_add)
        result = layer_norm(before_second, gain_second, shift_second)
        result_low = result.astype(jnp.bfloat16)
        outputs.append(result_low.reshape(seq_count, tok_count, width))
        kept.append(
            (
                hidden,
                query_group,
                key_all,
                value_all,
                log_total,
                mixed_rows,
                before_first,
                first_low,
                upward,
                activated,
                before_second,
            )
        )
        hidden = result_low
    grad_rows = cotangent.reshape(row_count, width).astype(jnp.float32)
    layer_grads = [None] * LAYERS
    for layer_index in reversed(range(LAYERS)):
        (
            hidden,
            query_group,
            key_all,
            value_all,
            log_total,
            mixed_rows,
            before_first,
            first_low,
            upward,
            activated,
            before_second,
        ) = kept[layer_index]
        weights = gather_backward(tuple((shard[layer_index] for shard in shards)))
        (
            joint_full,
            query_add,
            value_add,
            out_full,
            out_add,
            gain_first,
            shift_first,
            up_full,
            up_add,
            down_full,
            down_add,
            gain_second,
            shift_second,
        ) = weights
        _, second_pull = jax.vjp(
            layer_norm,
            before_second,
            gain_second.astype(jnp.float32),
            shift_second.astype(jnp.float32),
        )
        grad_second, grad_gain_second, grad_shift_second = second_pull(grad_rows)
        grad_down = grad_second.astype(jnp.bfloat16)
        grad_down_full = inner_rows(activated, grad_down)
        grad_down_add = column_sums(grad_down)
        _, gelu_pull = jax.vjp(exact_gelu, upward)
        grad_up = gelu_pull(times_transposed(grad_down, down_full))[0].astype(jnp.bfloat16)
        grad_up_full = inner_rows(first_low, grad_up)
        grad_up_add = column_sums(grad_up)
        grad_first = grad_second + times_transposed(grad_up, up_full)
        _, first_pull = jax.vjp(
            layer_norm,
            before_first,
            gain_first.astype(jnp.float32),
            shift_first.astype(jnp.float32),
        )
        grad_before, grad_gain_first, grad_shift_first = first_pull(grad_first)
        grad_branch = grad_before.astype(jnp.bfloat16)
        grad_out_full = inner_rows(mixed_rows, grad_branch)
        grad_out_add = column_sums(grad_branch)
        grad_mixed = (
            times_transposed(grad_branch, out_full)
            .astype(jnp.bfloat16)
            .reshape(seq_count, tok_count, width)
        )
        grad_group = lax.all_to_all(grad_mixed, "head", split_axis=2, concat_axis=1, tiled=True)
        grad_query_group, pair_terms = lax.map(
            attend_backward, (query_group, key_all, value_all, lengths, log_total, grad_group)
        )
        pair_sums = sum_at_owner(pair_terms.astype(jnp.bfloat16), "blk", 1).astype(jnp.bfloat16)
        group_width = pair_sums.shape[-1] // 2
        grad_query, grad_key, grad_value = sent_together(
            (grad_query_group, pair_sums[..., :group_width], pair_sums[..., group_width:]),
            "head",
            1,
            2,
            0,
        )
        grad_joint_rows = jnp.concatenate([grad_query, grad_key, grad_value], axis=-1).reshape(
            row_count, 3 * width
        )
        grad_joint_full = inner_rows(hidden, grad_joint_rows)
        grad_query_add = column_sums(grad_query)
        grad_value_add = column_sums(grad_value)
        grad_rows = grad_before + times_transposed(grad_joint_rows, joint_full)
        summed = (
            *tuple(
                (
                    part.astype(jnp.float32)
                    for part in side_by_side(
                        (
                            grad_joint_full.astype(jnp.bfloat16),
                            grad_query_add.astype(jnp.bfloat16),
                            grad_value_add.astype(jnp.bfloat16),
                            grad_out_full.astype(jnp.bfloat16),
                            grad_out_add.astype(jnp.bfloat16),
                            grad_gain_first.astype(jnp.bfloat16),
                            grad_shift_first.astype(jnp.bfloat16),
                            grad_up_full.astype(jnp.bfloat16),
                        ),
                        ("batch", "blk"),
                        0,
                        1,
                    )
                )
            ),
            *tuple(
                (
                    part.astype(jnp.float32)
                    for part in side_by_side(
                        (grad_up_add.astype(jnp.bfloat16), grad_down_full.astype(jnp.bfloat16)),
                        ("batch", "blk"),
                        0,
                        1,
                    )
                )
            ),
            lax.psum_scatter(
                grad_down_add.astype(jnp.bfloat16),
                ("batch", "blk"),
                scatter_dimension=0,
                tiled=True,
            ).astype(jnp.float32),
            lax.psum_scatter(
                grad_gain_second.astype(jnp.bfloat16),
                ("batch", "blk"),
                scatter_dimension=0,
                tiled=True,
            ).astype(jnp.float32),
            lax.psum_scatter(
                grad_shift_second.astype(jnp.bfloat16),
                ("batch", "blk"),
                scatter_dimension=0,
                tiled=True,
            ).astype(jnp.float32),
        )
        layer_grads[layer_index] = (
            of_everyone(summed[0].astype(jnp.bfloat16), "head").astype(jnp.float32),
            of_everyone(summed[1].astype(jnp.bfloat16), "head").astype(jnp.float32),
            of_everyone(summed[2].astype(jnp.bfloat16), "head").astype(jnp.float32),
            of_everyone(summed[3].astype(jnp.bfloat16), "head").astype(jnp.float32),
            of_everyone(summed[4].astype(jnp.bfloat16), "head").astype(jnp.float32),
            of_everyone(summed[5].astype(jnp.bfloat16), "head").astype(jnp.float32),
            of_everyone(summed[6].astype(jnp.bfloat16), "head").astype(jnp.float32),
            of_everyone(summed[7].astype(jnp.bfloat16), "head").astype(jnp.float32),
            of_everyone(summed[8].astype(jnp.bfloat16), "head").astype(jnp.float32),
            of_everyone(summed[9].astype(jnp.bfloat16), "head").astype(jnp.float32),
            of_everyone(summed[10].astype(jnp.bfloat16), "head").astype(jnp.float32),
            of_everyone(summed[11].astype(jnp.bfloat16), "head").astype(jnp.float32),
            of_everyone(summed[12].astype(jnp.bfloat16), "head").astype(jnp.float32),
        )
    stacked = tuple(
        (
            jnp.stack([layer_grads[layer_slot][member_slot] for layer_slot in range(LAYERS)])
            for member_slot in range(13)
        )
    )
    activations = jnp.stack(outputs)
    input_grad = grad_rows.reshape(seq_count, tok_count, width)
    return (
        activations,
        input_grad,
        stacked[0],
        stacked[1],
        stacked[2],
        stacked[3],
        stacked[4],
        stacked[5],
        stacked[6],
        stacked[7],
        stacked[8],
        stacked[9],
        stacked[10],
        stacked[11],
        stacked[12],
    )


def solution(mesh):
    placed = (
        P("batch", ("head", "blk"), None),
        P("batch"),
        P(None, ("batch", "blk"), None),
        P(None, ("batch", "blk")),
        P(None, ("batch", "blk")),
        P(None, ("batch", "blk"), None),
        P(None, ("batch", "blk")),
        P(None, ("batch", "blk")),
        P(None, ("batch", "blk")),
        P(None, ("batch", "blk"), None),
        P(None, ("batch", "blk")),
        P(None, ("batch", "blk"), None),
        P(None, ("batch", "blk")),
        P(None, ("batch", "blk")),
        P(None, ("batch", "blk")),
        P("batch", ("head", "blk"), None),
    )
    return jax.shard_map(
        body,
        mesh=mesh,
        in_specs=placed,
        out_specs=(
            P(None, "batch", ("head", "blk"), None),
            P("batch", ("head", "blk"), None),
            P(None, ("batch", "blk"), None),
            P(None, ("batch", "blk")),
            P(None, ("batch", "blk")),
            P(None, ("batch", "blk"), None),
            P(None, ("batch", "blk")),
            P(None, ("batch", "blk")),
            P(None, ("batch", "blk")),
            P(None, ("batch", "blk"), None),
            P(None, ("batch", "blk")),
            P(None, ("batch", "blk"), None),
            P(None, ("batch", "blk")),
            P(None, ("batch", "blk")),
            P(None, ("batch", "blk")),
        ),
        check_vma=False,
    )
```

profile of v0, /device:TPU:0, one launch (start us, length us, event | category | flops | bytes accessed | tf_op | source)
XLA Modules:
  0.0 1151.4 jit_solution(13663937285352128930)
XLA Ops:
  15.2 70.6 %all-gather.13.cloned.1.call-done = bf16[768,6149]{1,0:T(8,128)(2,1)} async-done(((bf16[24,6149]{1,0:T(8,128)(2,1)}), bf16[768,6149]{1,0:T(8,128)(2,1)}) %all-gather.13.cloned.1.call-update) | async-done | bytes 9444880 | tf_op jit(solution)/shard_map/all_gather | solution.py:18
  91.8 17.0 %all_to_all.278 = bf16[3,128,768]{1,0,2:T(4,128)(2,1)S(1)} all-to-all(bf16[3,128,768]{1,0,2:T(4,128)(2,1)S(1)} %copy.479), channel_id=1, replica_groups=mesh['batch'=8,'head'=4,'blk'=4] {'head'}, dimensions={2} | all-to-all | bytes 1179648 | tf_op jit(solution)/shard_map/all_to_all | solution.py:29
  117.8 126.0 %all-reduce.15 = (bf16[768]{0:T(1024)(128)(2,1)S(1)}, bf16[768]{0:T(1024)(128)(2,1)S(1)}, bf16[768]{0:T(1024)(128)(2,1)S(1)}, bf16[768]{0:T(1024)(128)(2,1)}, bf16[768]{0:T(1024)(128)(2,1)}) all-reduce(bf16[768]{0:T(1024)(128)(2,1)S(1)} %dynamic-update-slice, ...), channel_id=2, replica_groups=mesh['batch'=8,'head'=4,'blk'=4] {'batch','blk'}, use_global_device_ids=true, to_apply=%add | all-reduce | flops 3840 | bytes 15360
  273.3 9.3 multiply_convert_fusion.3
  288.3 15.6 %all_to_all.279 = bf16[3,128,768]{1,0,2:T(4,128)(2,1)S(1)} all-to-all(bf16[3,128,768]{1,0,2:T(4,128)(2,1)S(1)} %copy.490), channel_id=1, replica_groups=mesh['batch'=8,'head'=4,'blk'=4] {'head'}, dimensions={2} | all-to-all | bytes 1179648 | tf_op jit(solution)/shard_map/all_to_all | solution.py:29
  307.8 18.0 %all-gather.21.cloned.1.call-done = bf16[2,2048,192]{1,2,0:T(8,128)(2,1)} async-done(((bf16[2,512,192]{1,2,0:T(8,128)(2,1)}), bf16[2,2048,192]{1,2,0:T(8,128)(2,1)}) %all-gather.21.cloned.1.call-update) | async-done | bytes 1572880 | tf_op jit(solution)/shard_map/all_gather | solution.py:36
  346.7 43.3 %all-gather.23.cloned.1.call-done = bf16[3072,769]{1,0:T(8,128)(2,1)} async-done(((bf16[96,769]{1,0:T(8,128)(2,1)}), bf16[3072,769]{1,0:T(8,128)(2,1)}) %all-gather.23.cloned.1.call-update) | async-done | bytes 4724752 | tf_op jit(solution)/shard_map/all_gather | solution.py:18
  394.8 7.2 multiply_convert_fusion.2
  414.1 7.8 copy.562
  451.6 25.3 %fusion.108 = bf16[2048,3,64]{0,2,1:T(8,128)(2,1)S(1)} fusion(bf16[512,3,64]{0,2,1:T(8,128)(2,1)S(1)} %copy-done.24, f32[3,512,2048]{2,1,0:T(8,128)} %fusion.280, f32[3,512,2048]{2,1,0:T(8,128)} %copy-done.1, f32[3,512]{1,0:T(4,128)} %log_add_fusion.1, pred[2048]{0:T(1024)(128)(4,1)} %copy-done.50), kind=kOutput, calls=%fused_computation.87 | convolution fusion | flops 437652992 | bytes 26157056 | tf_op jit(solution)/shard_map/while/body/eval_jaxpr/hqk,qhe->khe/dot_general | solution.py:219
  477.6 8.2 fusion.117
  493.1 25.0 %fusion.170 = bf16[3,64,512]{2,1,0:T(8,128)(2,1)} fusion(bf16[2048,3,64]{0,2,1:T(8,128)(2,1)} %bitcast.270, f32[3,512,2048]{2,1,0:T(8,128)} %fusion.280, f32[3,512,2048]{2,1,0:T(8,128)} %copy-done.1, f32[3,512]{1,0:T(4,128)} %log_add_fusion.1, pred[2048]{0:T(1024)(128)(4,1)} %copy-done.50), kind=kOutput, calls=%fused_computation.153 | convolution fusion | flops 437358080 | bytes 26157056 | tf_op jit(solution)/shard_map/while/body/eval_jaxpr/hqk,khe->qhe/dot_general | solution.py:216
  524.3 19.3 %all_to_all.280 = bf16[3,512,192]{2,0,1:T(4,128)(2,1)} all-to-all(bf16[3,512,192]{2,0,1:T(4,128)(2,1)S(1)} %copy.505), channel_id=1, replica_groups=mesh['batch'=8,'head'=4,'blk'=4] {'head'}, dimensions={1} | all-to-all | bytes 1179648 | tf_op jit(solution)/shard_map/all_to_all | solution.py:29
  563.0 7.6 copy.560
  599.8 20.7 %fusion.111 = bf16[2048,3,64]{0,2,1:T(8,128)(2,1)S(1)} fusion(bf16[512,3,64]{0,2,1:T(8,128)(2,1)S(1)} %copy-done.22, f32[3,512,2048]{2,1,0:T(8,128)} %fusion.281, f32[3,512,2048]{2,1,0:T(8,128)} %copy-done, f32[3,512]{1,0:T(4,128)S(1)} %log_add_fusion, pred[2048]{0:T(1024)(128)(4,1)S(1)} %copy-done.52), kind=kOutput, calls=%fused_computation.88 | convolution fusion | flops 437652992 | bytes 26157056 | tf_op jit(solution)/shard_map/while/body/eval_jaxpr/hqk,qhe->khe/dot_general | solution.py:219
  643.9 24.6 %fusion.167 = bf16[3,64,512]{2,1,0:T(8,128)(2,1)} fusion(bf16[2048,3,64]{0,2,1:T(8,128)(2,1)} %bitcast.266, f32[3,512,2048]{2,1,0:T(8,128)} %fusion.281, f32[3,512,2048]{2,1,0:T(8,128)} %copy-done, f32[3,512]{1,0:T(4,128)} %copy-done.88, pred[2048]{0:T(1024)(128)(4,1)S(1)} %copy-done.54), kind=kOutput, calls=%fused_computation.152 | convolution fusion | flops 437358080 | bytes 26157056 | tf_op jit(solution)/shard_map/while/body/eval_jaxpr/hqk,khe->qhe/dot_general | solution.py:216
  695.3 16.8 %concatenate.105 = bf16[768,6149]{1,0:T(8,128)(2,1)} concatenate(bf16[768,2304]{1,0:T(8,128)(2,1)S(1)} %convolution_convert_fusion.3, bf16[768,1]{1,0:T(8,128)(2,1)} %reshape.926, bf16[768,1]{1,0:T(8,128)(2,1)} %reshape.927, bf16[768,768]{1,0:T(8,128)(2,1)} %copy.534, bf16[768,1]{1,0:T(8,128)(2,1)} %reshape.928, bf16[768,1]{1,0:T(8,128)(2,1)} %convert_element_type.726, ...), dimensions={1} | concatenate | bytes 18889728 | tf_op jit(solution)/shard_map/concatenate | solution.py:54
  732.4 16.8 %concatenate.104 = bf16[768,6149]{1,0:T(8,128)(2,1)} concatenate(bf16[768,2304]{1,0:T(8,128)(2,1)S(1)} %copy.523, bf16[768,1]{1,0:T(8,128)(2,1)} %reshape.923, bf16[768,1]{1,0:T(8,128)(2,1)} %reshape.924, bf16[768,768]{1,0:T(8,128)(2,1)} %copy.526, bf16[768,1]{1,0:T(8,128)(2,1)} %reshape.925, bf16[768,1]{1,0:T(8,128)(2,1)} %convert_element_type.724, ...), dimensions={1} | concatenate | bytes 18889728 | tf_op jit(solution)/shard_map/concatenate | solution.py:54
  751.3 129.8 %all-reduce.14 = (bf16[768]{0:T(1024)(128)(2,1)S(1)}, bf16[768]{0:T(1024)(128)(2,1)S(1)}, bf16[768]{0:T(1024)(128)(2,1)S(1)}, bf16[768]{0:T(1024)(128)(2,1)S(1)}...) all-reduce(bf16[768]{0:T(1024)(128)(2,1)S(1)} %dynamic-update-slice, ...), channel_id=7, replica_groups=mesh['batch'=8,'head'=4,'blk'=4] {'batch','blk'}, use_global_device_ids=true, to_apply=%add.5 | all-reduce | flops 5376 | bytes 21504
  972.1 7.8 all-to-all-done.28
  1099.3 7.0 all-to-all-done.10
  1111.7 6.4 all-to-all-done.11
  1123.4 7.6 all-to-all-done.24
  1136.2 7.5 all-to-all-done.25
  (647 shorter events, 487.7 us)
Async XLA Ops:
  7.2 78.6 %all-gather.13.cloned.1.call-start = ((), (), s32[]{:S(2)}) async-start(), calls=%async_computation.38 | async-start | bytes 9934848 | tf_op jit(solution)/shard_map/all_gather | solution.py:18
  15.1 228.9 %all-gather.15.cloned.1.call-start = ((), (), s32[]{:S(2)}) async-start(), calls=%async_computation.39 | async-start | bytes 1966080 | tf_op jit(solution)/shard_map/all_gather | solution.py:36
  110.6 153.4 %all-gather.17.cloned.1.call-start = ((), (), s32[]{:S(2)}) async-start(), calls=%async_computation.40 | async-start | bytes 5677056 | tf_op jit(solution)/shard_map/all_gather | solution.py:18
  112.8 153.1 %all-gather.19.cloned.1.call-start = ((), (), s32[]{:S(2)}) async-start(), calls=%async_computation.41 | async-start | bytes 9934848 | tf_op jit(solution)/shard_map/all_gather | solution.py:18
  260.3 9.7 all-to-all-start.1
  263.7 62.1 %all-gather.21.cloned.1.call-start = ((), (), s32[]{:S(2)}) async-start(), calls=%async_computation.42 | async-start | bytes 1966080 | tf_op jit(solution)/shard_map/all_gather | solution.py:36
  304.9 85.1 %all-gather.23.cloned.1.call-start = ((), (), s32[]{:S(2)}) async-start(), calls=%async_computation.43 | async-start | bytes 5677056 | tf_op jit(solution)/shard_map/all_gather | solution.py:18
  342.3 49.2 %all-to-all-start.3 = ((bf16[4,2,12288]{2,1,0:T(2,128)(2,1)}), bf16[4,2,12288]{2,1,0:T(2,128)(2,1)S(1)}, u32[]{:S(2)}, u32[]{:S(2)}) async-start(bf16[4,2,12288]{2,1,0:T(2,128)(2,1)} %reshape.965), calls=%async_computation.3 | async-start | bytes 393216 | tf_op jit(solution)/shard_map/all_to_all | solution.py:275
  346.5 584.4 %reduce-scatter.9.cloned.1.call-start = ((), (), s32[]{:S(2)}) async-start(), calls=%async_computation.45 | async-start | bytes 5677056
  434.0 10.7 all-to-all-start.4
  489.5 30.4 %all-to-all-start.5 = ((bf16[4,1,512,384]{2,3,1,0:T(8,128)(2,1)}), bf16[4,1,512,384]{2,3,1,0:T(8,128)(2,1)S(1)}, u32[]{:S(2)}, u32[]{:S(2)}) async-start(bf16[4,1,512,384]{2,3,1,0:T(8,128)(2,1)} %pad_maximum_fusion.2), calls=%async_computation.5 | async-start | bytes 3145728 | tf_op jit(solution)/shard_map/all_to_all | solution.py:48
  493.1 457.4 %reduce-scatter.7.cloned.1.call-start = ((), (), s32[]{:S(2)}) async-start(), calls=%async_computation.44 | async-start | bytes 5677056
  582.9 10.1 all-to-all-start.7
  629.5 40.7 %all-to-all-start.8 = ((bf16[4,1,512,384]{2,3,1,0:T(8,128)(2,1)}), bf16[4,1,512,384]{2,3,1,0:T(8,128)(2,1)}, u32[]{:S(2)}, u32[]{:S(2)}) async-start(bf16[4,1,512,384]{2,3,1,0:T(8,128)(2,1)} %pad_maximum_fusion.3), calls=%async_computation.8 | async-start | bytes 3145728 | tf_op jit(solution)/shard_map/all_to_all | solution.py:48
  678.6 38.4 %all-to-all-start.9 = ((bf16[3,512,192]{2,0,1:T(4,128)(2,1)}), bf16[3,512,192]{2,0,1:T(4,128)(2,1)}, u32[]{:S(2)}, u32[]{:S(2)}) async-start(bf16[3,512,192]{2,0,1:T(4,128)(2,1)} %copy.516), calls=%async_computation.9 | async-start | bytes 2097152 | tf_op jit(solution)/shard_map/all_to_all | solution.py:29
  683.0 297.8 %all-reduce.19.cloned.1.call-start = ((), (), s32[]{:S(2)}) async-start(), calls=%async_computation.46 | async-start | bytes 38535168
  881.8 9.5 all-to-all-start.30
  945.9 11.9 %all-to-all-start.29 = ((bf16[4,96,768]{2,1,0:T(8,128)(2,1)}), bf16[4,96,768]{2,1,0:T(8,128)(2,1)S(1)}, u32[]{:S(2)}, u32[]{:S(2)}) async-start(bf16[4,96,768]{2,1,0:T(8,128)(2,1)} %broadcast_in_dim.366), calls=%async_computation.29 | async-start | bytes 1179648 | tf_op jit(solution)/shard_map/all_to_all | solution.py:65
  967.5 12.3 %all-to-all-start.28 = ((bf16[4,96,768]{2,1,0:T(8,128)(2,1)}), bf16[4,96,768]{2,1,0:T(8,128)(2,1)S(1)}, u32[]{:S(2)}, u32[]{:S(2)}) async-start(bf16[4,96,768]{2,1,0:T(8,128)(2,1)} %broadcast_in_dim.365), calls=%async_computation.28 | async-start | bytes 1179648 | tf_op jit(solution)/shard_map/all_to_all | solution.py:65
  1075.0 9.4 all-to-all-start.16
  1095.2 11.1 all-to-all-start.10
  1107.1 11.1 all-to-all-start.11
  1119.1 11.9 %all-to-all-start.24 = ((bf16[4,24,3072]{2,1,0:T(8,128)(2,1)}), bf16[4,24,3072]{2,1,0:T(8,128)(2,1)S(1)}, u32[]{:S(2)}, u32[]{:S(2)}) async-start(bf16[4,24,3072]{2,1,0:T(8,128)(2,1)} %broadcast_in_dim.359), calls=%async_computation.24 | async-start | bytes 1179648 | tf_op jit(solution)/shard_map/all_to_all | solution.py:65
  1131.8 11.9 %all-to-all-start.25 = ((bf16[4,24,3072]{2,1,0:T(8,128)(2,1)}), bf16[4,24,3072]{2,1,0:T(8,128)(2,1)S(1)}, u32[]{:S(2)}, u32[]{:S(2)}) async-start(bf16[4,24,3072]{2,1,0:T(8,128)(2,1)} %broadcast_in_dim.360), calls=%async_computation.25 | async-start | bytes 1179648 | tf_op jit(solution)/shard_map/all_to_all | solution.py:65
  (144 other events, 3628.8 us)
Sparse Core Ops, SparseCore 0:
  15.2 70.4 all-gather.12
  110.7 21.2 all-gather.14
  134.3 61.7 all-gather.16
  198.2 67.5 all-gather.18
  305.0 20.7 all-gather.20
  328.0 61.9 all-gather.22
  422.0 161.2 reduce-scatter.8
  585.8 161.6 reduce-scatter.6
  751.4 186.1 all-reduce.18
where the time goes:
time: 1160 us; the launch traced here: 1150 us
  blocking collectives  308 us (27%)
  waiting for transfers between devices  280 us (24%)
  matrix products  216 us (19%)
  local copies, waits for them, and re-layouts  152 us (13%)
  starting transfers between devices  117 us (10%)
  other arithmetic  61.2 us (5%)
  between operations  18.6 us (2%)
    unnamed x2, blocking collectives  256 us
    all_to_all x26, waiting for transfers between devices, sent_to_all(): lax.all_to_all(jnp.broadcast_to(array[None], (length, *array.shape)), axi...  134 us
    all_gather x4, waiting for transfers between devices, in_one_piece(): whole, at, outs = (lax.all_gather(both, axis, axis=dim, tiled=True), 0, [])  114 us
    all_to_all x26, starting transfers between devices, sent_to_all(): lax.all_to_all(jnp.broadcast_to(array[None], (length, *array.shape)), axi...  87 us
    all_to_all x3, blocking collectives, sent_together(): lax.all_to_all(both, axis, split_axis=split_dim, concat_axis=concat_dim,...  51.8 us
    dot_general x2, matrix products, attend_backward(): jnp.einsum('hqk,khe->qhe', grad_scores, key_heads, preferred_element_type...  49.7 us
    dot_general x2, matrix products, attend_backward(): jnp.einsum('hqk,qhe->khe', grad_scores, query_heads, preferred_element_ty...  46 us
    concatenate x2, local copies, waits for them, and re-layouts, side_by_side(): both = jnp.concatenate(columns, axis=along)  33.6 us
  transfers between devices with their start and end apart: 42, of which 33 were waited for; matrix products, arithmetic and copies ran while one was open for 30% of the time, Pallas kernels for 0%

commit v1 on v0

--- a/solution.py
+++ b/solution.py
@@ -1,6 +1,8 @@
 import jax
 import jax.numpy as jnp
 from jax import lax
+from jax.experimental import pallas as pl
+from jax.experimental.pallas import tpu as pltpu
 from jax.sharding import PartitionSpec as P
 
 HEADS = 12
@@ -10,17 +12,6 @@
 
 EPSILON = 1e-12
 MASKED = -1e30
-
-
-def in_one_piece(arrays, axis, dim, along):
-    columns = [a.reshape(*a.shape[:along], -1) for a in arrays]
-    both = jnp.concatenate(columns, axis=along)
-    whole, at, outs = (lax.all_gather(both, axis, axis=dim, tiled=True), 0, [])
-    for a, column in zip(arrays, columns):
-        share = whole[..., at : at + column.shape[along]]
-        outs.append(share.reshape(*share.shape[:along], *a.shape[along:]))
-        at += column.shape[along]
-    return tuple(outs)
 
 
 def sent_together(arrays, axis, split_dim, concat_dim, along):
@@ -49,28 +40,6 @@
     return jnp.sum(blocks.astype(jnp.float32), axis=0)
 
 
-def side_by_side(arrays, axis, dim, along):
-    columns = [a.reshape(*a.shape[:along], -1) for a in arrays]
-    both = jnp.concatenate(columns, axis=along)
-    whole, at, outs = (lax.psum_scatter(both, axis, scatter_dimension=dim, tiled=True), 0, [])
-    for a, column in zip(arrays, columns):
-        share = whole[..., at : at + column.shape[along]]
-        outs.append(share.reshape(*share.shape[:along], *a.shape[along:]))
-        at += column.shape[along]
-    return tuple(outs)
-
-
-def sent_to_all(array, axis):
-    length = lax.axis_size(axis)
-    return lax.all_to_all(
-        jnp.broadcast_to(array[None], (length, *array.shape)), axis, 0, 0, tiled=True
-    )
-
-
-def of_everyone(array, axis):
-    return sent_to_all(array, axis).astype(jnp.float32).sum(axis=0)
-
-
 def layer_norm(values, gain, shift):
     average = jnp.mean(values, axis=-1, keepdims=True)
     centered = values - average
@@ -98,34 +67,417 @@
     )
 
 
-def gather_forward(parts):
+MESH = pl.DeviceIdType.MESH
+ALL = slice(None)
+
+
+def my_place():
+    b, x, k = lax.axis_index("batch"), lax.axis_index("head"), lax.axis_index("blk")
+    return {"z": b // 2, "y": (k // 2) * 2 + b % 2, "x": x, "c": k % 2}
+
+
+def device_of(place):
     return (
-        *in_one_piece(
-            (parts[0], parts[1], parts[2], parts[3], parts[4], parts[5], parts[6], parts[7]),
-            ("batch", "blk"),
-            0,
-            1,
+        place["z"] * 2 + place["y"] % 2,
+        place["x"],
+        (place["y"] // 2) * 2 + place["c"],
+    )
+
+
+def peer_of(place, axis, step):
+    other = dict(place)
+    other[axis] = (place[axis] + step) % (2 if axis == "c" else 4)
+    return other
+
+
+def greet_all(place):
+    barrier = pltpu.get_barrier_semaphore()
+    peers = [peer_of(place, a, s) for a in ("x", "y", "z") for s in (1, 2, 3)]
+    peers.append(peer_of(place, "c", 1))
+    for p in peers:
+        pl.semaphore_signal(barrier, inc=1, device_id=device_of(p), device_id_type=MESH)
+    pl.semaphore_wait(barrier, len(peers))
+
+
+def remote(src, dst, send, recv, place):
+    return pltpu.make_async_remote_copy(
+        src_ref=src,
+        dst_ref=dst,
+        send_sem=send,
+        recv_sem=recv,
+        device_id=device_of(place),
+        device_id_type=MESH,
+    )
+
+
+PIECES = (
+    (0, ("z", "y", "x")),
+    (1, ("z", "y")),
+    (2, ("y", "z")),
+    (3, ("z", "y", "x")),
+    (4, ("z", "y")),
+    (5, ("y", "z")),
+    (6, ("y", "z")),
+)
+
+
+def gather_kernel(*refs):
+    n = len(PIECES)
+    ins, outs = refs[:n], refs[n : 2 * n]
+    send, recv, fsend, frecv, local = refs[2 * n :]
+    me = my_place()
+    partner = peer_of(me, "c", 1)
+
+    def region(i, phase, place):
+        array, order = PIECES[i]
+        done = order[:phase]
+        z = ALL if "z" in done else place["z"]
+        y = (ALL, ALL) if "y" in done else (place["y"] % 2, place["y"] // 2)
+        cols = ALL
+        if "x" in order and "x" not in done:
+            cols = pl.ds(pl.multiple_of(place["x"] * 768, 128), 768)
+        return outs[i].at[z, y[0], y[1], place["c"], ALL, cols]
+
+    def own(i):
+        if "x" in PIECES[i][1]:
+            return ins[i].at[ALL, pl.ds(pl.multiple_of(me["x"] * 768, 128), 768)]
+        return ins[i]
+
+    def step(i, phase, s):
+        axis = PIECES[i][1][phase]
+        src = own(i) if phase == 0 else region(i, phase, me)
+        return remote(
+            src,
+            region(i, phase, me),
+            send.at[i, phase, s - 1],
+            recv.at[i, phase, s - 1],
+            peer_of(me, axis, s),
+        )
+
+    def landed(i, phase, s):
+        axis = PIECES[i][1][phase]
+        place = peer_of(me, axis, 4 - s)
+        r = region(i, phase, place)
+        return remote(r, r, send.at[i, phase, s - 1], recv.at[i, phase, s - 1], place)
+
+    def forward(i, phase, s):
+        axis = PIECES[i][1][phase]
+        r = region(i, phase, peer_of(me, axis, 4 - s))
+        return remote(r, r, fsend.at[i, phase, s - 1], frecv.at[i, phase, s - 1], partner)
+
+    def forwarded(i, phase, s):
+        axis = PIECES[i][1][phase]
+        r = region(i, phase, peer_of(partner, axis, 4 - s))
+        return remote(r, r, fsend.at[i, phase, s - 1], frecv.at[i, phase, s - 1], partner)
+
+    greet_all(me)
+    copies, sends, fwds = [], [], []
+    for i in range(n):
+        for s in (2, 1, 3):
+            c = step(i, 0, s)
+            c.start()
+            sends.append(c)
+        c = pltpu.make_async_copy(own(i), region(i, 0, me), local.at[i])
+        c.start()
+        copies.append(c)
+        c = remote(own(i), region(i, 0, me), fsend.at[i, 3, 0], frecv.at[i, 3, 0], partner)
+        c.start()
+        fwds.append(c)
+    for c in copies:
+        c.wait()
+    for phase in range(3):
+        for i in range(n):
+            order = PIECES[i][1]
+            if phase >= len(order):
+                continue
+            for s in (1, 3, 2):
+                landed(i, phase, s).wait_recv()
+                c = forward(i, phase, s)
+                c.start()
+                fwds.append(c)
+            if phase + 1 < len(order):
+                for s in (2, 1, 3):
+                    c = step(i, phase + 1, s)
+                    c.start()
+                    sends.append(c)
+    for i in range(n):
+        r = region(i, 0, partner)
+        remote(r, r, fsend.at[i, 3, 0], frecv.at[i, 3, 0], partner).wait_recv()
+        for phase in range(len(PIECES[i][1])):
+            for s in (1, 2, 3):
+                forwarded(i, phase, s).wait_recv()
+    for c in sends + fwds:
+        c.wait_send()
+
+
+def gather_weights(pieces):
+    n = len(pieces)
+    anyspace = pl.BlockSpec(memory_space=pl.ANY)
+    return pl.pallas_call(
+        gather_kernel,
+        out_shape=[jax.ShapeDtypeStruct((4, 2, 2, 2, *p.shape), p.dtype) for p in pieces],
+        in_specs=[anyspace] * n,
+        out_specs=[anyspace] * n,
+        scratch_shapes=[
+            pltpu.SemaphoreType.DMA((n, 3, 3)),
+            pltpu.SemaphoreType.DMA((n, 3, 3)),
+            pltpu.SemaphoreType.DMA((n, 4, 3)),
+            pltpu.SemaphoreType.DMA((n, 4, 3)),
+            pltpu.SemaphoreType.DMA((n,)),
+        ],
+        compiler_params=pltpu.CompilerParams(collective_id=0, has_side_effects=True),
+        name="gather_weights",
+    )(*pieces)
+
+
+THIRDS = (("x", "y", "z"), ("y", "z", "x"), ("z", "x", "y"))
+
+
+def reduce_kernel(*refs):
+    ins = refs[:11]
+    joint_out, out_out, up_out, down_out, vec_out = refs[11:16]
+    lhs, rhs, g, r1, s1, r2, s2, r3, last, vc, va = refs[16:27]
+    csend, crecv, lsem, ps, pr, vs, vr = refs[27:]
+    vec_in = ins[10]
+    me = my_place()
+    partner = peer_of(me, "c", 1)
+    c = me["c"]
+    greet_all(me)
+    half = pl.ds(pl.multiple_of(c * 128, 128), 128)
+    other_half = pl.ds(pl.multiple_of((1 - c) * 128, 128), 128)
+    starts = (0, 3072, 3840, 6144)
+    widths = (3072, 768, 2304, 768)
+    layers = (1, 0)
+
+    def exchanges(l):
+        lhs_in, rhs_in = ins[5 * l], ins[5 * l + 1 : 5 * l + 5]
+        away = [
+            remote(
+                lhs_in.at[1 - c],
+                lhs.at[l, ALL, half],
+                csend.at[l, 0],
+                crecv.at[l, 0],
+                partner,
+            )
+        ]
+        here = [pltpu.make_async_copy(lhs_in.at[c], lhs.at[l, ALL, half], lsem.at[l, 0])]
+        for j in range(4):
+            dst = rhs.at[l, half, pl.ds(starts[j], widths[j])]
+            away.append(remote(rhs_in[j], dst, csend.at[l, j + 1], crecv.at[l, j + 1], partner))
+            here.append(pltpu.make_async_copy(rhs_in[j], dst, lsem.at[l, j + 1]))
+        return away, here
+
+    exchanged = {}
+    for l in layers:
+        exchanged[l] = exchanges(l)
+        for copy in exchanged[l][0] + exchanged[l][1]:
+            copy.start()
+
+    vec_axes = ("c", "x", "y", "z")
+    vec_sends = []
+
+    def vec_slot(phase, place):
+        if phase == 0:
+            return vc.at[place["c"]]
+        return va.at[phase - 1, place[vec_axes[phase]]]
+
+    def vec_start(phase, value):
+        vec_slot(phase, me)[...] = value.astype(jnp.bfloat16)
+        for s in range(1, 2 if phase == 0 else 4):
+            copy = remote(
+                vec_slot(phase, me),
+                vec_slot(phase, me),
+                vs.at[phase, s - 1],
+                vr.at[phase, s - 1],
+                peer_of(me, vec_axes[phase], s),
+            )
+            copy.start()
+            vec_sends.append(copy)
+
+    def vec_finish(phase):
+        count = 2 if phase == 0 else 4
+        for s in range(1, count):
+            src = peer_of(me, vec_axes[phase], count - s)
+            slot = vec_slot(phase, src)
+            remote(slot, slot, vs.at[phase, s - 1], vr.at[phase, s - 1], src).wait_recv()
+        total = None
+        for j in range(count):
+            part = (vc[j] if phase == 0 else va[phase - 1, j]).astype(jnp.float32)
+            total = part if total is None else total + part
+        return total
+
+    vec_start(0, vec_in[...])
+
+    sends = []
+
+    def send_chunks(phase, t, l, source, target):
+        axis = THIRDS[t][phase] if phase < 3 else "x"
+        for s in (2, 1, 3):
+            peer = peer_of(me, axis, s)
+            copy = remote(
+                source(peer[axis]),
+                target(s),
+                ps.at[phase, t, l, s - 1],
+                pr.at[phase, t, l, s - 1],
+                peer,
+            )
+            copy.start()
+            sends.append(copy)
+
+    def await_chunks(phase, t, l, target):
+        axis = THIRDS[t][phase] if phase < 3 else "x"
+        for s in (1, 3, 2):
+            slot = target(s)
+            remote(
+                slot,
+                slot,
+                ps.at[phase, t, l, s - 1],
+                pr.at[phase, t, l, s - 1],
+                peer_of(me, axis, s),
+            ).wait_recv()
+
+    dims = (((0,), (0,)), ((), ()))
+    for l in layers:
+        away, here = exchanged[l]
+        for copy in here:
+            copy.wait()
+        for copy in away:
+            copy.wait_recv()
+        for t in range(3):
+            for q in range(4):
+                unit = (0, 1 + q, 5 if q < 3 else 6)[t]
+                col = (q * 768, 3072, 3840 + q * 768)[t]
+                block = jnp.dot(
+                    lhs[l, 384 * unit : 384 * unit + 384, :],
+                    rhs[l, :, col : col + 768],
+                    preferred_element_type=jnp.float32,
+                )
+                for i in range(16):
+                    z, y = i // 4, (i % 2) * 2 + (i // 2) % 2
+                    at = ((q, y, z), (y, z, q), (z, q, y))[t]
+                    g[t, l, at[0], at[1], at[2]] = block[24 * i : 24 * i + 24].astype(jnp.bfloat16)
+            send_chunks(
+                0, t, l, lambda a, t=t, l=l: g.at[t, l, a], lambda s, t=t, l=l: r1.at[t, l, s - 1]
+            )
+    vec_start(1, vec_finish(0))
+    f32 = jnp.float32
+    for l in layers:
+        for t in range(3):
+            mine = me[THIRDS[t][0]]
+            await_chunks(0, t, l, lambda s, t=t, l=l: r1.at[t, l, s - 1])
+
+            def add1(i, carry, t=t, l=l, mine=mine):
+                a, b = i // 4, i % 4
+                total = g[t, l, mine, a, b].astype(f32)
+                for s in range(3):
+                    total = total + r1[t, l, s, a, b].astype(f32)
+                s1[t, l, a, b] = total.astype(jnp.bfloat16)
+                return carry
+
+            lax.fori_loop(0, 16, add1, 0)
+            send_chunks(
+                1, t, l, lambda a, t=t, l=l: s1.at[t, l, a], lambda s, t=t, l=l: r2.at[t, l, s - 1]
+            )
+    vec_start(2, vec_finish(1))
+    for l in layers:
+        for t in range(3):
+            mine = me[THIRDS[t][1]]
+            await_chunks(1, t, l, lambda s, t=t, l=l: r2.at[t, l, s - 1])
+            for a in range(4):
+                total = s1[t, l, mine, a].astype(f32)
+                for s in range(3):
+                    total = total + r2[t, l, s, a].astype(f32)
+                s2[t, l, a] = total.astype(jnp.bfloat16)
+            send_chunks(
+                2, t, l, lambda a, t=t, l=l: s2.at[t, l, a], lambda s, t=t, l=l: r3.at[t, l, s - 1]
+            )
+    vec_start(3, vec_finish(2))
+    for l in layers:
+        for t in range(3):
+            mine = me[THIRDS[t][2]]
+            await_chunks(2, t, l, lambda s, t=t, l=l: r3.at[t, l, s - 1])
+            total = s2[t, l, mine].astype(f32)
+            for s in range(3):
+                total = total + r3[t, l, s].astype(f32)
+            last[t, l, me["x"]] = total.astype(jnp.bfloat16)
+            send_chunks(
+                3,
+                t,
+                l,
+                lambda a, t=t, l=l: last.at[t, l, me["x"]],
+                lambda s, t=t, l=l: last.at[t, l, me["x"]],
+            )
+    vec_out[...] = vec_finish(3)
+    for l in layers:
+        for t in range(3):
+            await_chunks(3, t, l, lambda s, t=t, l=l: last.at[t, l, (me["x"] + 4 - s) % 4])
+            for q in range(4):
+                part = last[t, l, q].astype(f32)
+                if t == 0:
+                    up_out[l, :, 768 * q : 768 * q + 768] = part
+                elif t == 1:
+                    down_out[l, 24 * q : 24 * q + 24, :] = part
+                elif q < 3:
+                    joint_out[l, :, 768 * q : 768 * q + 768] = part
+                else:
+                    out_out[l] = part
+    for copy in sends + vec_sends + [a for l in layers for a in exchanged[l][0]]:
+        copy.wait_send()
+
+
+def for_owner_cores(array):
+    tokens, width = array.shape
+    n = width // 768
+    t = array.T.reshape(16, 2, n, 24, tokens).transpose(1, 2, 0, 3, 4)
+    return t.reshape(2, n * 384, tokens)
+
+
+def reduce_grads(per_layer, vectors):
+    operands = []
+    for hidden, mixed, first, acts, d_joint, d_branch, d_up, d_down in per_layer:
+        operands.append(
+            jnp.concatenate([for_owner_cores(a) for a in (first, acts, hidden, mixed)], axis=1)
+        )
+        operands += [d_up, d_down, d_joint, d_branch]
+    anyspace = pl.BlockSpec(memory_space=pl.ANY)
+    vmem = pl.BlockSpec(memory_space=pltpu.VMEM)
+    bf, dma = jnp.bfloat16, pltpu.SemaphoreType.DMA
+    return pl.pallas_call(
+        reduce_kernel,
+        out_shape=[
+            jax.ShapeDtypeStruct((2, 24, 2304), jnp.float32),
+            jax.ShapeDtypeStruct((2, 24, 768), jnp.float32),
+            jax.ShapeDtypeStruct((2, 24, 3072), jnp.float32),
+            jax.ShapeDtypeStruct((2, 96, 768), jnp.float32),
+            jax.ShapeDtypeStruct((32, 768), jnp.float32),
+        ],
+        in_specs=[anyspace] * 10 + [vmem],
+        out_specs=[vmem] * 5,
+        scratch_shapes=[
+            pltpu.VMEM((2, 2688, 256), bf),
+            pltpu.VMEM((2, 256, 6912), bf),
+            pltpu.VMEM((3, 2, 4, 4, 4, 24, 768), bf),
+            pltpu.VMEM((3, 2, 3, 4, 4, 24, 768), bf),
+            pltpu.VMEM((3, 2, 4, 4, 24, 768), bf),
+            pltpu.VMEM((3, 2, 3, 4, 24, 768), bf),
+            pltpu.VMEM((3, 2, 4, 24, 768), bf),
+            pltpu.VMEM((3, 2, 3, 24, 768), bf),
+            pltpu.VMEM((3, 2, 4, 24, 768), bf),
+            pltpu.VMEM((2, 32, 768), bf),
+            pltpu.VMEM((3, 4, 32, 768), bf),
+            dma((2, 5)),
+            dma((2, 5)),
+            dma((2, 5)),
+            dma((4, 3, 2, 3)),
+            dma((4, 3, 2, 3)),
+            dma((4, 3)),
+            dma((4, 3)),
+        ],
+        compiler_params=pltpu.CompilerParams(
+            collective_id=1, has_side_effects=True, vmem_limit_bytes=62 * 1024 * 1024
         ),
-        *in_one_piece((parts[8], parts[9]), ("batch", "blk"), 0, 1),
-        lax.all_gather(parts[10], ("batch", "blk"), axis=0, tiled=True),
-        lax.all_gather(parts[11], ("batch", "blk"), axis=0, tiled=True),
-        lax.all_gather(parts[12], ("batch", "blk"), axis=0, tiled=True),
-    )
-
-
-def gather_backward(parts):
-    return (
-        *in_one_piece(
-            (parts[0], parts[1], parts[2], parts[3], parts[4], parts[5], parts[6], parts[7]),
-            ("batch", "blk"),
-            0,
-            1,
-        ),
-        *in_one_piece((parts[8], parts[9]), ("batch", "blk"), 0, 1),
-        lax.all_gather(parts[10], ("batch", "blk"), axis=0, tiled=True),
-        lax.all_gather(parts[11], ("batch", "blk"), axis=0, tiled=True),
-        lax.all_gather(parts[12], ("batch", "blk"), axis=0, tiled=True),
-    )
+        name="reduce_grads",
+    )(*operands, vectors)
 
 
 def column_sums(values):
@@ -150,21 +502,53 @@
     second_shift,
     cotangent,
 ):
-    shards = (
-        joint_weight,
-        query_bias,
-        value_bias,
-        output_weight,
-        output_bias,
-        first_gain,
-        first_shift,
-        up_weight,
-        up_bias,
-        down_weight,
-        down_bias,
-        second_gain,
-        second_shift,
-    )
+    vectors = jnp.stack(
+        (
+            query_bias,
+            value_bias,
+            output_bias,
+            first_gain,
+            first_shift,
+            down_bias,
+            second_gain,
+            second_shift,
+        ),
+        axis=1,
+    )
+    vectors = jnp.concatenate([vectors, up_bias.reshape(LAYERS, 4, 24)], axis=1)
+    vectors = jnp.pad(vectors.reshape(24, 24), ((0, 8), (0, 104)))
+    joint_and_out = jnp.concatenate([joint_weight, output_weight], axis=-1)
+    pieces = []
+    for layer_index in range(LAYERS):
+        pieces += [up_weight[layer_index], down_weight[layer_index], joint_and_out[layer_index]]
+    *gathered, vectors_all = gather_weights((*pieces, vectors))
+    vectors_all = vectors_all.reshape(32, 32, 128)[:, :24, :24].reshape(32, LAYERS, 12, 24)
+    rows_all = vectors_all[:, :, :8].transpose(1, 2, 0, 3).reshape(LAYERS, 8, 768)
+    up_adds = vectors_all[:, :, 8:].transpose(1, 0, 2, 3).reshape(LAYERS, 3072)
+    weights_of = []
+    for layer_index in range(LAYERS):
+        up_full, down_full, joint_out = gathered[3 * layer_index : 3 * layer_index + 3]
+        up_full = up_full.reshape(768, 3072)
+        down_full = down_full.reshape(3072, 768)
+        joint_out = joint_out.reshape(768, 3072)
+        rows = rows_all[layer_index]
+        weights_of.append(
+            (
+                joint_out[:, :2304],
+                rows[0],
+                rows[1],
+                joint_out[:, 2304:],
+                rows[2],
+                rows[3],
+                rows[4],
+                up_full,
+                up_adds[layer_index],
+                down_full,
+                rows[5],
+                rows[6],
+                rows[7],
+            )
+        )
     seq_count, tok_count, width = inputs.shape
     row_count = seq_count * tok_count
     head_devices = lax.axis_size("head")
@@ -235,7 +619,7 @@
     kept = []
     outputs = []
     for layer_index in range(LAYERS):
-        weights = gather_forward(tuple((shard[layer_index] for shard in shards)))
+        weights = weights_of[layer_index]
         (
             joint_full,
             query_add,
@@ -303,6 +687,7 @@
         hidden = result_low
     grad_rows = cotangent.reshape(row_count, width).astype(jnp.float32)
     layer_grads = [None] * LAYERS
+    vector_grads = [None] * LAYERS
     for layer_index in reversed(range(LAYERS)):
         (
             hidden,
@@ -317,7 +702,7 @@
             activated,
             before_second,
         ) = kept[layer_index]
-        weights = gather_backward(tuple((shard[layer_index] for shard in shards)))
+        weights = weights_of[layer_index]
         (
             joint_full,
             query_add,
@@ -341,11 +726,9 @@
         )
         grad_second, grad_gain_second, grad_shift_second = second_pull(grad_rows)
         grad_down = grad_second.astype(jnp.bfloat16)
-        grad_down_full = inner_rows(activated, grad_down)
         grad_down_add = column_sums(grad_down)
         _, gelu_pull = jax.vjp(exact_gelu, upward)
         grad_up = gelu_pull(times_transposed(grad_down, down_full))[0].astype(jnp.bfloat16)
-        grad_up_full = inner_rows(first_low, grad_up)
         grad_up_add = column_sums(grad_up)
         grad_first = grad_second + times_transposed(grad_up, up_full)
         _, first_pull = jax.vjp(
@@ -356,7 +739,6 @@
         )
         grad_before, grad_gain_first, grad_shift_first = first_pull(grad_first)
         grad_branch = grad_before.astype(jnp.bfloat16)
-        grad_out_full = inner_rows(mixed_rows, grad_branch)
         grad_out_add = column_sums(grad_branch)
         grad_mixed = (
             times_transposed(grad_branch, out_full)
@@ -379,81 +761,52 @@
         grad_joint_rows = jnp.concatenate([grad_query, grad_key, grad_value], axis=-1).reshape(
             row_count, 3 * width
         )
-        grad_joint_full = inner_rows(hidden, grad_joint_rows)
         grad_query_add = column_sums(grad_query)
         grad_value_add = column_sums(grad_value)
         grad_rows = grad_before + times_transposed(grad_joint_rows, joint_full)
-        summed = (
-            *tuple(
-                (
-                    part.astype(jnp.float32)
-                    for part in side_by_side(
-                        (
-                            grad_joint_full.astype(jnp.bfloat16),
-                            grad_query_add.astype(jnp.bfloat16),
-                            grad_value_add.astype(jnp.bfloat16),
-                            grad_out_full.astype(jnp.bfloat16),
-                            grad_out_add.astype(jnp.bfloat16),
-                            grad_gain_first.astype(jnp.bfloat16),
-                            grad_shift_first.astype(jnp.bfloat16),
-                            grad_up_full.astype(jnp.bfloat16),
-                        ),
-                        ("batch", "blk"),
-                        0,
-                        1,
-                    )
-                )
-            ),
-            *tuple(
-                (
-                    part.astype(jnp.float32)
-                    for part in side_by_side(
-                        (grad_up_add.astype(jnp.bfloat16), grad_down_full.astype(jnp.bfloat16)),
-                        ("batch", "blk"),
-                        0,
-                        1,
-                    )
-                )
-            ),
-            lax.psum_scatter(
-                grad_down_add.astype(jnp.bfloat16),
-                ("batch", "blk"),
-                scatter_dimension=0,
-                tiled=True,
-            ).astype(jnp.float32),
-            lax.psum_scatter(
-                grad_gain_second.astype(jnp.bfloat16),
-                ("batch", "blk"),
-                scatter_dimension=0,
-                tiled=True,
-            ).astype(jnp.float32),
-            lax.psum_scatter(
-                grad_shift_second.astype(jnp.bfloat16),
-                ("batch", "blk"),
-                scatter_dimension=0,
-                tiled=True,
-            ).astype(jnp.float32),
-        )
         layer_grads[layer_index] = (
-            of_everyone(summed[0].astype(jnp.bfloat16), "head").astype(jnp.float32),
-            of_everyone(summed[1].astype(jnp.bfloat16), "head").astype(jnp.float32),
-            of_everyone(summed[2].astype(jnp.bfloat16), "head").astype(jnp.float32),
-            of_everyone(summed[3].astype(jnp.bfloat16), "head").astype(jnp.float32),
-            of_everyone(summed[4].astype(jnp.bfloat16), "head").astype(jnp.float32),
-            of_everyone(summed[5].astype(jnp.bfloat16), "head").astype(jnp.float32),
-            of_everyone(summed[6].astype(jnp.bfloat16), "head").astype(jnp.float32),
-            of_everyone(summed[7].astype(jnp.bfloat16), "head").astype(jnp.float32),
-            of_everyone(summed[8].astype(jnp.bfloat16), "head").astype(jnp.float32),
-            of_everyone(summed[9].astype(jnp.bfloat16), "head").astype(jnp.float32),
-            of_everyone(summed[10].astype(jnp.bfloat16), "head").astype(jnp.float32),
-            of_everyone(summed[11].astype(jnp.bfloat16), "head").astype(jnp.float32),
-            of_everyone(summed[12].astype(jnp.bfloat16), "head").astype(jnp.float32),
-        )
-    stacked = tuple(
-        (
-            jnp.stack([layer_grads[layer_slot][member_slot] for layer_slot in range(LAYERS)])
-            for member_slot in range(13)
-        )
+            hidden,
+            mixed_rows,
+            first_low,
+            activated,
+            grad_joint_rows,
+            grad_branch,
+            grad_up,
+            grad_down,
+        )
+        vector_grads[layer_index] = (
+            grad_query_add,
+            grad_value_add,
+            grad_out_add,
+            grad_gain_first,
+            grad_shift_first,
+            grad_down_add,
+            grad_gain_second,
+            grad_shift_second,
+            grad_up_add,
+        )
+    vectors = jnp.concatenate(
+        [a.reshape(-1, 768) for layer in vector_grads for a in layer] + [jnp.zeros((8, 768), jnp.float32)]
+    )
+    joint_grad, out_grad, up_grad, down_grad, vectors = reduce_grads(layer_grads, vectors)
+    vectors = vectors[:24].reshape(LAYERS, 12, 768)
+    owner = lax.axis_index("batch") * blk_devices + lax.axis_index("blk")
+    own_rows = lax.dynamic_slice_in_dim(vectors[:, :8], owner * 24, 24, axis=2)
+    own_up = lax.dynamic_slice_in_dim(vectors[:, 8:].reshape(LAYERS, 3072), owner * 96, 96, axis=1)
+    stacked = (
+        joint_grad,
+        own_rows[:, 0],
+        own_rows[:, 1],
+        out_grad,
+        own_rows[:, 2],
+        own_rows[:, 3],
+        own_rows[:, 4],
+        up_grad,
+        own_up,
+        down_grad,
+        own_rows[:, 5],
+        own_rows[:, 6],
+        own_rows[:, 7],
     )
     activations = jnp.stack(outputs)
     input_grad = grad_rows.reshape(seq_count, tok_count, width)

time: 1160 us -> 684 us (0.59)
  blocking collectives: 308 us -> 31.5 us
  Pallas kernels: 0 us -> 200 us
  waiting for transfers between devices: 280 us -> 83.3 us
  starting transfers between devices: 117 us -> 33.8 us
  local copies, waits for them, and re-layouts: 152 us -> 83.1 us
  matrix products: 216 us -> 190 us
  other arithmetic: 61.2 us -> 37.8 us
    unnamed x2 -> x0, blocking collectives: 256 us -> none
    pallas_call x0 -> x2, Pallas kernels: none -> 200 us  [the longest x1 107 us: gather_weights(): pl.pallas_call(gather_kernel, out_shape=[jax.ShapeDtypeStruct((4, 2, 2, 2...]
    all_to_all x26 -> x0, waiting for transfers between devices: 134 us -> none  [sent_to_all(): lax.all_to_all(jnp.broadcast_to(array[None], (length, *array.shape)), axi...]
    all_gather x4 -> x0, waiting for transfers between devices: 114 us -> none  [in_one_piece(): whole, at, outs = (lax.all_gather(both, axis, axis=dim, tiled=True), 0, [])]
    all_to_all x26 -> x0, starting transfers between devices: 87 us -> none  [sent_to_all(): lax.all_to_all(jnp.broadcast_to(array[None], (length, *array.shape)), axi...]
    concatenate x4 -> x3, local copies, waits for them, and re-layouts: 35.4 us -> 3.48 us  [the longest x1 2.53 us: body(): jnp.concatenate([a.reshape(-1, 768) for layer in vector_grads for a in la...]
    all_to_all x1 -> x2, waiting for transfers between devices: 0.01 us -> 28 us  [sent_together(): lax.all_to_all(both, axis, split_axis=split_dim, concat_axis=concat_dim,...]
    all_gather x2, waiting for transfers between devices: 18 us -> 40.1 us  [sent_together_2(): whole = lax.all_gather(both, axis, axis=dim, tiled=True)]
  transfers between devices with their start and end apart: 42 -> 10, of which waited for: 33 -> 7; matrix products, arithmetic and copies ran while one was open for 30% -> 12% of each run, Pallas kernels for 0% -> 0%
where the time goes in v1:
time: 684 us; the launch traced here: 677 us
  Pallas kernels  200 us (29%)
  matrix products  190 us (28%)
  waiting for transfers between devices  83.3 us (12%)
  local copies, waits for them, and re-layouts  83.1 us (12%)
  other arithmetic  37.8 us (6%)
  starting transfers between devices  33.8 us (5%)
  blocking collectives  31.5 us (5%)
  between operations  17 us (2%)
    pallas_call x1, Pallas kernels, gather_weights(): pl.pallas_call(gather_kernel, out_shape=[jax.ShapeDtypeStruct((4, 2, 2, 2...  107 us
    pallas_call x1, Pallas kernels, reduce_grads(): pl.pallas_call(reduce_kernel, out_shape=[jax.ShapeDtypeStruct((2, 24, 230...  93.8 us
    dot_general x2, matrix products, attend_backward(): jnp.einsum('hqk,khe->qhe', grad_scores, key_heads, preferred_element_type...  48.3 us
    dot_general x2, matrix products, attend_backward(): jnp.einsum('hqk,qhe->khe', grad_scores, query_heads, preferred_element_ty...  41 us
    all_gather x2, waiting for transfers between devices, sent_together_2(): whole = lax.all_gather(both, axis, axis=dim, tiled=True)  40.1 us
    dot_general x8, matrix products, row_product(): return jnp.dot(operand, matrix, preferred_element_type=jnp.float32)  32.8 us
    all_to_all x2, blocking collectives, sent_together(): lax.all_to_all(both, axis, split_axis=split_dim, concat_axis=concat_dim,...  31.5 us
    dot_general x8, matrix products, times_transposed(): lax.dot_general(operand, matrix, (((1,), (1,)), ((), ())), preferred_elem...  30.3 us
  transfers between devices with their start and end apart: 10, of which 7 were waited for; matrix products, arithmetic and copies ran while one was open for 12% of the time, Pallas kernels for 0%

profile of v1, /device:TPU:0, one launch (start us, length us, event | category | flops | bytes accessed | tf_op | source)
XLA Modules:
  0.0 676.7 jit_solution(15441558496967695793)
XLA Ops:
  19.3 106.6 %gather_weights.1 = (bf16[4,2,2,2,24,3072]{5,4,3,2,1,0:T(8,128)(2,1)}, bf16[4,2,2,2,96,768]{5,4,3,2,1,0:T(8,128)(2,1)}, bf16[4,2,2,2,24,3072]{5,4,3,2,1,0:T(8,12...) custom-call(bf16[24,3072]{1,0:T(8,128)(2,1)} %get-tuple-element.260., ...), custom_call_target="tpu_custom_call" | custom-call | tf_op jit(solution)/shard_map/gather_weights/pallas_call | solution.py:216
  132.1 17.4 %all_to_all.130 = bf16[3,128,768]{1,0,2:T(4,128)(2,1)S(1)} all-to-all(bf16[3,128,768]{1,0,2:T(4,128)(2,1)S(1)} %copy.353), channel_id=1, replica_groups=mesh['batch'=8,'head'=4,'blk'=4] {'head'}, dimensions={2} | all-to-all | bytes 1179648 | tf_op jit(solution)/shard_map/all_to_all | solution.py:20
  152.5 18.8 %all-gather.3.cloned.1.call-done = bf16[2,2048,192]{1,2,0:T(8,128)(2,1)} async-done(((bf16[2,512,192]{1,2,0:T(8,128)(2,1)}), bf16[2,2048,192]{1,2,0:T(8,128)(2,1)}) %all-gather.3.cloned.1.call-update) | async-done | bytes 1572880 | tf_op jit(solution)/shard_map/all_gather | solution.py:27
  201.6 7.5 %fusion.101 = (bf16[3072,128]{0,1:T(8,128)(2,1)}, f32[128,3072]{1,0:T(8,128)S(1)}) fusion(f32[3072]{0:T(1024)S(1)} %reshape.870, bf16[768,3072]{1,0:T(8,128)(2,1)} %bitcast.422, f32[128,768]{1,0:T(8,128)S(1)} %get-tuple-element.244, f32[768]{0:T(1024)S(1)} %reshape.869, f32[768]{0:T(1024)S(1)} %reshape.868, f32[128]{0:T(128)S(1)} %fusion.215, ...), kind=kOutput, calls=%fused_computation.74 | convolution fusion | flops 630423552 | bytes 7490560 | tf_op jit(solution)/shard_map/dot_general | solution.py:55
  215.2 14.1 %all_to_all.131 = bf16[3,128,768]{1,0,2:T(4,128)(2,1)S(1)} all-to-all(bf16[3,128,768]{1,0,2:T(4,128)(2,1)S(1)} %copy.367), channel_id=1, replica_groups=mesh['batch'=8,'head'=4,'blk'=4] {'head'}, dimensions={2} | all-to-all | bytes 1179648 | tf_op jit(solution)/shard_map/all_to_all | solution.py:20
  230.5 21.2 %all-gather.5.cloned.1.call-done = bf16[2,2048,192]{1,2,0:T(8,128)(2,1)} async-done(((bf16[2,512,192]{1,2,0:T(8,128)(2,1)}), bf16[2,2048,192]{1,2,0:T(8,128)(2,1)}) %all-gather.5.cloned.1.call-update) | async-done | bytes 1572880 | tf_op jit(solution)/shard_map/all_gather | solution.py:27
  285.0 7.4 %fusion.104 = (bf16[3072,128]{0,1:T(8,128)(2,1)}, f32[128,3072]{1,0:T(8,128)S(1)}) fusion(f32[3072]{0:T(1024)S(1)} %copy-done.74, bf16[768,3072]{1,0:T(8,128)(2,1)} %bitcast.426, f32[128,768]{1,0:T(8,128)S(1)} %get-tuple-element.250, f32[768]{0:T(1024)S(1)} %copy-done.61, f32[768]{0:T(1024)S(1)} %copy-done.55, f32[128]{0:T(128)S(1)} %fusion.217, ...), kind=kOutput, calls=%fused_computation.77 | convolution fusion | flops 630423552 | bytes 7490560 | tf_op jit(solution)/shard_map/dot_general | solution.py:55
  292.5 6.2 fusion.266
  301.3 5.5 convert_reduce_fusion
  325.4 5.6 all-to-all-done.4
  331.4 6.4 fusion.267
  337.9 7.0 %fusion.94 = bf16[2048,3,64]{0,2,1:T(8,128)(2,1)} fusion(bf16[512,3,64]{0,2,1:T(8,128)(2,1)S(1)} %reshape.823, f32[3,512,2048]{2,1,0:T(8,128)} %copy-done.1, f32[3,512]{1,0:T(4,128)S(1)} %log_add_fusion.1, pred[2048]{0:T(1024)(128)(4,1)S(1)} %fusion.202), kind=kOutput, calls=%fused_computation.65 | convolution fusion | flops 415629312 | bytes 13574144 | tf_op jit(solution)/shard_map/while/body/eval_jaxpr/hqk,qhe->khe/dot_general | solution.py:606
  344.9 20.5 %fusion.85 = bf16[2048,3,64]{0,2,1:T(8,128)(2,1)S(1)} fusion(bf16[512,3,64]{0,2,1:T(8,128)(2,1)S(1)} %reshape.817, f32[3,512,2048]{2,1,0:T(8,128)} %fusion.267, f32[3,512,2048]{2,1,0:T(8,128)} %copy-done.1, f32[3,512]{1,0:T(4,128)S(1)} %log_add_fusion.1, pred[2048]{0:T(1024)(128)(4,1)S(1)} %fusion.202), kind=kOutput, calls=%fused_computation.62 | convolution fusion | flops 437652992 | bytes 26157056 | tf_op jit(solution)/shard_map/while/body/eval_jaxpr/hqk,qhe->khe/dot_general | solution.py:603
  373.6 24.4 %fusion.161 = bf16[3,64,512]{2,1,0:T(8,128)(2,1)S(1)} fusion(bf16[2048,3,64]{0,2,1:T(8,128)(2,1)} %bitcast.435, f32[3,512,2048]{2,1,0:T(8,128)} %fusion.267, f32[3,512,2048]{2,1,0:T(8,128)} %copy-done.1, f32[3,512]{1,0:T(4,128)} %copy-done.84, pred[2048]{0:T(1024)(128)(4,1)S(1)} %fusion.202), kind=kOutput, calls=%fused_computation.168 | convolution fusion | flops 437358080 | bytes 26157056 | tf_op jit(solution)/shard_map/while/body/eval_jaxpr/hqk,khe->qhe/dot_general | solution.py:600
  408.3 14.5 %all-to-all-done.6 = bf16[3,512,192]{2,0,1:T(4,128)(2,1)S(1)} async-done(((bf16[3,512,192]{2,0,1:T(4,128)(2,1)}), bf16[3,512,192]{2,0,1:T(4,128)(2,1)S(1)}, u32[]{:S(2)}, u32[]{:S(2)}) %all-to-all-start.6) | async-done | bytes 589856 | tf_op jit(solution)/shard_map/all_to_all | solution.py:20
  432.7 7.5 %convert_reduce_fusion.1 = (f32[3072]{0:T(1024)}, bf16[128,3072]{1,0:T(8,128)(2,1)S(1)}) fusion(f32[128,3072]{1,0:T(8,128)S(1)} %copy-done.101, bf16[128,768]{1,0:T(8,128)(2,1)S(1)} %get-tuple-element.171.refs_2_, bf16[3072,768]{1,0:T(8,128)(2,1)} %bitcast.514), kind=kOutput, calls=%fused_computation.91 | convolution fusion | flops 633074688 | bytes 7286784 | tf_op jit(solution)/shard_map/dot_general | solution.py:65
  453.6 5.5 all-to-all-done.7
  459.5 6.4 fusion.268
  465.9 6.2 fusion.91
  472.1 20.5 %fusion.88 = bf16[2048,3,64]{0,2,1:T(8,128)(2,1)S(1)} fusion(bf16[512,3,64]{0,2,1:T(8,128)(2,1)S(1)} %copy-done.20, f32[3,512,2048]{2,1,0:T(8,128)} %fusion.268, f32[3,512,2048]{2,1,0:T(8,128)} %copy-done, f32[3,512]{1,0:T(4,128)S(1)} %log_add_fusion, pred[2048]{0:T(1024)(128)(4,1)S(1)} %fusion.202), kind=kOutput, calls=%fused_computation.63 | convolution fusion | flops 437652992 | bytes 26157056 | tf_op jit(solution)/shard_map/while/body/eval_jaxpr/hqk,qhe->khe/dot_general | solution.py:603
  495.3 5.0 all-to-all-start.8
  513.2 24.0 %fusion.158 = bf16[3,64,512]{2,1,0:T(8,128)(2,1)S(1)} fusion(bf16[2048,3,64]{0,2,1:T(8,128)(2,1)S(1)} %bitcast.431, f32[3,512,2048]{2,1,0:T(8,128)} %fusion.268, f32[3,512,2048]{2,1,0:T(8,128)} %copy-done, f32[3,512]{1,0:T(4,128)} %copy-done.83, pred[2048]{0:T(1024)(128)(4,1)S(1)} %fusion.202), kind=kOutput, calls=%fused_computation.167 | convolution fusion | flops 437358080 | bytes 26157056 | tf_op jit(solution)/shard_map/while/body/eval_jaxpr/hqk,khe->qhe/dot_general | solution.py:600
  546.4 13.5 %all-to-all-done.9 = bf16[3,512,192]{2,0,1:T(4,128)(2,1)S(1)} async-done(((bf16[3,512,192]{2,0,1:T(4,128)(2,1)}), bf16[3,512,192]{2,0,1:T(4,128)(2,1)S(1)}, u32[]{:S(2)}, u32[]{:S(2)}) %all-to-all-start.9) | async-done | bytes 589856 | tf_op jit(solution)/shard_map/all_to_all | solution.py:20
  566.4 93.8 %reduce_grads.1 = (f32[2,24,2304]{2,1,0:T(8,128)}, f32[2,24,768]{2,1,0:T(8,128)}, f32[2,24,3072]{2,1,0:T(8,128)}, f32[2,96,768]{2,1,0:T(8,128)}, f32[32,768]{1,0:T(8,128)}) custom-call(bf16[2,2688,128]{2,1,0:T(8,128)(2,1)} %pad_maximum_fusion.2.refs_0_, bf16[128,3072]{1,0:T(8,128)(2,1)} %copy-done.9, bf16[128,768]{1,0:T(8,128)(2,1)} %copy-done.24, ...), custom_call_target="tpu_custom_call" | custom-call | tf_op jit(solution)/shard_map/reduce_grads/pallas_call | solution.py:445
  (500 shorter events, 194.2 us)
Async XLA Ops:
  7.2 164.2 %all-gather.3.cloned.1.call-start = ((), (), s32[]{:S(2)}) async-start(), calls=%async_computation.10 | async-start | bytes 1966080 | tf_op jit(solution)/shard_map/all_gather | solution.py:27
  16.9 111.2 %copy-start.26 = (bf16[1,128,768]{2,1,0:T(8,128)(2,1)S(1)}, bf16[1,128,768]{2,1,0:T(8,128)(2,1)}, u32[]{:S(2)}) copy-start(bf16[1,128,768]{2,1,0:T(8,128)(2,1)} %param.16) | copy-start | bytes 589828
  152.2 57.0 %copy-start.53 = (f32[768]{0:T(1024)}, f32[768]{0:T(1024)S(1)}, u32[]{:S(2)}) copy-start(f32[768]{0:T(1024)S(1)} %reshape.868) | copy-start | bytes 9220
  152.4 56.8 %copy-start.59 = (f32[768]{0:T(1024)}, f32[768]{0:T(1024)S(1)}, u32[]{:S(2)}) copy-start(f32[768]{0:T(1024)S(1)} %reshape.869) | copy-start | bytes 9220
  152.5 20.4 %copy-start.19 = (bf16[512,3,64]{0,2,1:T(8,128)(2,1)}, bf16[512,3,64]{0,2,1:T(8,128)(2,1)S(1)}, u32[]{:S(2)}) copy-start(bf16[512,3,64]{0,2,1:T(8,128)(2,1)S(1)} %reshape.807) | copy-start | bytes 589828
  187.4 10.6 %all-to-all-start.1 = ((bf16[4,2,12288]{2,1,0:T(2,128)(2,1)}), bf16[4,2,12288]{2,1,0:T(2,128)(2,1)S(1)}, u32[]{:S(2)}, u32[]{:S(2)}) async-start(bf16[4,2,12288]{2,1,0:T(2,128)(2,1)} %reshape.883), calls=%async_computation.1 | async-start | bytes 393216 | tf_op jit(solution)/shard_map/all_to_all | solution.py:659
  191.6 60.1 %all-gather.5.cloned.1.call-start = ((), (), s32[]{:S(2)}) async-start(), calls=%async_computation.11 | async-start | bytes 1966080 | tf_op jit(solution)/shard_map/all_gather | solution.py:27
  193.5 20.1 %copy-start.49 = (f32[768]{0:T(1024)}, f32[768]{0:T(1024)S(1)}, u32[]{:S(2)}) copy-start(f32[768]{0:T(1024)S(1)} %reshape.873) | copy-start | bytes 9220
  199.5 9.7 %slice-start.6 = ((s8[4718592]{0:T(1024)(128)(4,1)}), s8[4194304]{0:T(1024)(128)(4,1)S(1)}, s32[]{:S(2)}) async-start(s8[4718592]{0:T(1024)(128)(4,1)} %bitcast.515), calls=%async_computation.18 | async-start | bytes 8388608
  201.6 12.0 %slice-start.4 = ((s8[4718592]{0:T(1024)(128)(4,1)}), s8[4194304]{0:T(1024)(128)(4,1)S(1)}, s32[]{:S(2)}) async-start(s8[4718592]{0:T(1024)(128)(4,1)} %bitcast.497), calls=%async_computation.16 | async-start | bytes 8388608
  267.2 14.8 %all-to-all-start.3 = ((bf16[4,2,12288]{2,1,0:T(2,128)(2,1)}), bf16[4,2,12288]{2,1,0:T(2,128)(2,1)S(1)}, u32[]{:S(2)}, u32[]{:S(2)}) async-start(bf16[4,2,12288]{2,1,0:T(2,128)(2,1)} %reshape.885), calls=%async_computation.3 | async-start | bytes 393216 | tf_op jit(solution)/shard_map/all_to_all | solution.py:659
  282.9 9.5 %copy-start.13 = (bf16[1,128,4,192]{1,3,2,0:T(8,128)(2,1)}, bf16[1,128,4,192]{1,3,2,0:T(8,128)(2,1)S(1)}, u32[]{:S(2)}) copy-start(bf16[1,128,4,192]{1,3,2,0:T(8,128)(2,1)S(1)} %copy.374) | copy-start | bytes 589828
  292.5 14.3 %slice-start.2 = ((s8[4718592]{0:T(1024)(128)(4,1)}), s8[4194304]{0:T(1024)(128)(4,1)S(1)}, s32[]{:S(2)}) async-start(s8[4718592]{0:T(1024)(128)(4,1)} %bitcast.427), calls=%async_computation.14 | async-start | bytes 8388608
  319.8 11.1 %all-to-all-start.4 = ((bf16[4,2,12288]{2,1,0:T(2,128)(2,1)}), bf16[4,2,12288]{2,1,0:T(2,128)(2,1)S(1)}, u32[]{:S(2)}, u32[]{:S(2)}) async-start(bf16[4,2,12288]{2,1,0:T(2,128)(2,1)} %reshape.887), calls=%async_computation.4 | async-start | bytes 393216 | tf_op jit(solution)/shard_map/all_to_all | solution.py:748
  325.4 19.5 %copy-start.84 = (f32[3,512]{1,0:T(4,128)}, f32[3,512]{1,0:T(4,128)S(1)}, u32[]{:S(2)}) copy-start(f32[3,512]{1,0:T(4,128)S(1)} %log_add_fusion.1) | copy-start | bytes 18436
  369.8 28.9 %all-to-all-start.5 = ((bf16[4,1,512,384]{2,3,1,0:T(8,128)(2,1)}), bf16[4,1,512,384]{2,3,1,0:T(8,128)(2,1)S(1)}, u32[]{:S(2)}, u32[]{:S(2)}) async-start(bf16[4,1,512,384]{2,3,1,0:T(8,128)(2,1)} %pad_maximum_fusion), calls=%async_computation.5 | async-start | bytes 3145728 | tf_op jit(solution)/shard_map/all_to_all | solution.py:39
  403.1 19.6 %all-to-all-start.6 = ((bf16[3,512,192]{2,0,1:T(4,128)(2,1)}), bf16[3,512,192]{2,0,1:T(4,128)(2,1)S(1)}, u32[]{:S(2)}, u32[]{:S(2)}) async-start(bf16[3,512,192]{2,0,1:T(4,128)(2,1)} %copy.388), calls=%async_computation.6 | async-start | bytes 2097152 | tf_op jit(solution)/shard_map/all_to_all | solution.py:20
  408.3 63.8 %copy-start.83 = (f32[3,512]{1,0:T(4,128)}, f32[3,512]{1,0:T(4,128)S(1)}, u32[]{:S(2)}) copy-start(f32[3,512]{1,0:T(4,128)S(1)} %log_add_fusion) | copy-start | bytes 18436
  427.2 13.1 %slice-start = ((s8[4718592]{0:T(1024)(128)(4,1)}), s8[4194304]{0:T(1024)(128)(4,1)S(1)}, s32[]{:S(2)}) async-start(s8[4718592]{0:T(1024)(128)(4,1)} %bitcast.423), calls=%async_computation.12 | async-start | bytes 8388608
  449.2 9.9 %all-to-all-start.7 = ((bf16[4,2,12288]{2,1,0:T(2,128)(2,1)}), bf16[4,2,12288]{2,1,0:T(2,128)(2,1)S(1)}, u32[]{:S(2)}, u32[]{:S(2)}) async-start(bf16[4,2,12288]{2,1,0:T(2,128)(2,1)} %reshape.889), calls=%async_computation.7 | async-start | bytes 393216 | tf_op jit(solution)/shard_map/all_to_all | solution.py:748
  495.3 42.0 %all-to-all-start.8 = ((bf16[4,1,512,384]{2,3,1,0:T(8,128)(2,1)}), bf16[4,1,512,384]{2,3,1,0:T(8,128)(2,1)S(1)}, u32[]{:S(2)}, u32[]{:S(2)}) async-start(bf16[4,1,512,384]{2,3,1,0:T(8,128)(2,1)} %pad_maximum_fusion.1), calls=%async_computation.8 | async-start | bytes 3145728 | tf_op jit(solution)/shard_map/all_to_all | solution.py:39
  540.1 19.8 %all-to-all-start.9 = ((bf16[3,512,192]{2,0,1:T(4,128)(2,1)}), bf16[3,512,192]{2,0,1:T(4,128)(2,1)S(1)}, u32[]{:S(2)}, u32[]{:S(2)}) async-start(bf16[3,512,192]{2,0,1:T(4,128)(2,1)} %copy.402), calls=%async_computation.9 | async-start | bytes 2097152 | tf_op jit(solution)/shard_map/all_to_all | solution.py:20
  566.4 94.8 %copy-start.16 = (f32[128,768]{1,0:T(8,128)S(1)}, f32[128,768]{1,0:T(8,128)}, u32[]{:S(2)}) copy-start(f32[128,768]{1,0:T(8,128)} %copy-done.15) | copy-start | bytes 1179652
  566.4 94.8 %copy-start.97 = (f32[128]{0:T(128)S(1)}, f32[128]{0:T(128)}, u32[]{:S(2)}) copy-start(f32[128]{0:T(128)} %copy-done.96) | copy-start | bytes 1540
  (98 other events, 377.6 us)
Sparse Core Ops, SparseCore 0:
  151.4 19.9 all-gather.2
  230.4 21.2 all-gather.4

commit v2 on v1

--- a/solution.py
+++ b/solution.py
@@ -5,66 +5,11 @@
 from jax.experimental.pallas import tpu as pltpu
 from jax.sharding import PartitionSpec as P
 
-HEADS = 12
-HD = 64
 LAYERS = 2
 
 
 EPSILON = 1e-12
 MASKED = -1e30
-
-
-def sent_together(arrays, axis, split_dim, concat_dim, along):
-    widths = [a.shape[along] for a in arrays]
-    both = jnp.concatenate(arrays, axis=along)
-    whole = lax.all_to_all(both, axis, split_axis=split_dim, concat_axis=concat_dim, tiled=True)
-    return tuple(jnp.split(whole, [sum(widths[:k]) for k in range(1, len(widths))], axis=along))
-
-
-def sent_together_2(arrays, axis, dim, along):
-    widths = [a.shape[along] for a in arrays]
-    both = jnp.concatenate(arrays, axis=along)
-    whole = lax.all_gather(both, axis, axis=dim, tiled=True)
-    return tuple(jnp.split(whole, [sum(widths[:k]) for k in range(1, len(widths))], axis=along))
-
-
-def cut_along(array, dim, length):
-    dims = array.shape
-    blocks = array.reshape(*dims[:dim], length, dims[dim] // length, *dims[dim + 1 :])
-    return jnp.moveaxis(blocks, dim, 0)
-
-
-def sum_at_owner(array, axis, dim):
-    length = lax.axis_size(axis)
-    blocks = lax.all_to_all(cut_along(array, dim, length), axis, 0, 0, tiled=True)
-    return jnp.sum(blocks.astype(jnp.float32), axis=0)
-
-
-def layer_norm(values, gain, shift):
-    average = jnp.mean(values, axis=-1, keepdims=True)
-    centered = values - average
-    variance = jnp.mean(centered * centered, axis=-1, keepdims=True)
-    return centered * lax.rsqrt(variance + EPSILON) * gain + shift
-
-
-def exact_gelu(values):
-    return jax.nn.gelu(values, approximate=False)
-
-
-def row_product(operand, matrix):
-    return jnp.dot(operand, matrix, preferred_element_type=jnp.float32)
-
-
-def inner_rows(operand, other):
-    return lax.dot_general(
-        operand, other, (((0,), (0,)), ((), ())), preferred_element_type=jnp.float32
-    )
-
-
-def times_transposed(operand, matrix):
-    return lax.dot_general(
-        operand, matrix, (((1,), (1,)), ((), ())), preferred_element_type=jnp.float32
-    )
 
 
 MESH = pl.DeviceIdType.MESH
@@ -480,8 +425,473 @@
     )(*operands, vectors)
 
 
-def column_sums(values):
-    return jnp.sum(values.astype(jnp.float32), axis=tuple(range(values.ndim - 1)))
+FAR = (((1,), (1,)), ((), ()))
+NEAR = (((0,), (0,)), ((), ()))
+F32 = jnp.float32
+BF = jnp.bfloat16
+KEYS = 128
+
+
+def mxu(a, b, dims=None):
+    if dims is None:
+        return jnp.dot(a, b, preferred_element_type=F32)
+    return lax.dot_general(a, b, dims, preferred_element_type=F32)
+
+
+def normalized(values):
+    average = jnp.mean(values, axis=-1, keepdims=True)
+    centered = values - average
+    variance = jnp.mean(centered * centered, axis=-1, keepdims=True)
+    r = lax.rsqrt(variance + EPSILON)
+    return centered * r, r
+
+
+def norm_backward(values, gain, grad):
+    xhat, r = normalized(values)
+    g = grad * gain
+    back = r * (
+        g - jnp.mean(g, axis=-1, keepdims=True) - xhat * jnp.mean(g * xhat, axis=-1, keepdims=True)
+    )
+    gain_grad = jnp.sum(grad * xhat, axis=0, keepdims=True)
+    return back, gain_grad, jnp.sum(grad, axis=0, keepdims=True)
+
+
+def normal_cdf(u):
+    return 0.5 * (1.0 + lax.erf(u * 0.7071067811865476))
+
+
+def greet_sequence(me):
+    barrier = pltpu.get_barrier_semaphore()
+    peers = [peer_of(me, "x", s) for s in (1, 2, 3)]
+    peers += [peer_of(me, "c", 1), peer_of(me, "y", 2)]
+    for p in peers:
+        pl.semaphore_signal(barrier, inc=1, device_id=device_of(p), device_id_type=MESH)
+    pl.semaphore_wait(barrier, len(peers))
+
+
+def key_bias(length, block, xs):
+    limit = length - xs * 512 - block * 128
+    rows = lax.broadcasted_iota(jnp.int32, (KEYS, 128), 0)
+    return jnp.where(rows < limit, 0.0, MASKED)
+
+
+def forward_kernel(*refs):
+    hid, rows, up_add, lens, wj, wu, wd = refs[:7]
+    res, q_out, kv_out, log_out, att_out, mixed_out = refs[7:13]
+    before1_out, low_out, up_out, act_out, before2_out = refs[13:18]
+    vj, vu, vd, qs, qb, kvb, sc, acc, back, ab = refs[18:28]
+    wsem, osem, qsend, qrecv, xsend, xrecv, csend, crecv, ysend, yrecv, fsend, frecv = refs[28:40]
+    bsend, brecv = refs[40:]
+    me = my_place()
+    x, c = me["x"], me["c"]
+    yh = me["y"] // 2
+    k = yh * 2 + c
+    partner, across = peer_of(me, "c", 1), peer_of(me, "y", 2)
+    k_partner = yh * 2 + 1 - c
+    k_across = (1 - yh) * 2 + c
+    k_diag = (1 - yh) * 2 + 1 - c
+    loads = [
+        pltpu.make_async_copy(a, b, wsem.at[i])
+        for i, (a, b) in enumerate(((wj, vj), (wu, vu), (wd, vd)))
+    ]
+    for copy in loads:
+        copy.start()
+    greet_sequence(me)
+    sends = []
+
+    def send(src, dst, s, r, place):
+        copy = remote(src, dst, s, r, place)
+        copy.start()
+        sends.append(copy)
+
+    def arrived(slot, s, r, place):
+        remote(slot, slot, s, r, place).wait_recv()
+
+    loads[0].wait()
+    for j in (1, 2, 0):
+        p = mxu(hid[...], vj[:, 768 * j : 768 * j + 768])
+        if j == 0:
+            p = p + rows[0:1]
+        if j == 2:
+            p = p + rows[1:2]
+        p = p.astype(BF).astype(F32)
+        if j == 0:
+            p = p * 0.125
+        p = p.T.astype(BF)
+        for g in range(4):
+            qs[g, 192 * j : 192 * j + 192] = p[192 * g : 192 * g + 192]
+        if j == 2:
+            kvb[k, x] = qs[x, 192:576]
+            for s in (2, 1, 3):
+                peer = peer_of(me, "x", s)
+                send(
+                    qs.at[peer["x"], 192:576], kvb.at[k, x], xsend.at[s - 1], xrecv.at[s - 1], peer
+                )
+            send(kvb.at[k, x], kvb.at[k, x], ysend.at[0], yrecv.at[0], across)
+            send(kvb.at[k, x], kvb.at[k, x], csend.at[0], crecv.at[0], partner)
+    qb[x] = qs[x, 0:192]
+    for s in (2, 1, 3):
+        peer = peer_of(me, "x", s)
+        send(qs.at[peer["x"], 0:192], qb.at[x], qsend.at[s - 1], qrecv.at[s - 1], peer)
+    for s in (1, 3, 2):
+        source = peer_of(me, "x", 4 - s)
+        slot = kvb.at[k, source["x"]]
+        arrived(slot, xsend.at[s - 1], xrecv.at[s - 1], source)
+        send(slot, slot, ysend.at[s], yrecv.at[s], across)
+        send(slot, slot, csend.at[s], crecv.at[s], partner)
+    for s in (1, 3, 2):
+        source = peer_of(me, "x", 4 - s)
+        arrived(qb.at[source["x"]], qsend.at[s - 1], qrecv.at[s - 1], source)
+    for s in (0, 1, 3, 2):
+        arrived(kvb.at[k_partner, (x + 4 - s) % 4], csend.at[s], crecv.at[s], partner)
+
+    length = lens[0]
+    queries = [
+        jnp.concatenate([qb[xs, 64 * n : 64 * n + 64] for xs in range(4)], axis=1)
+        for n in range(3)
+    ]
+
+    def half(b0, b1, old):
+        def scores(i, peaks):
+            b = b0 + (b1 - b0) * (i // 4)
+            xs = i % 4
+            bias = key_bias(length, b, xs)
+            bias = jnp.concatenate([bias] * 4, axis=1)
+            new = []
+            for n in range(3):
+                keys = kvb[b, xs, 64 * n : 64 * n + 64, :]
+                st = mxu(keys, queries[n], NEAR) + bias
+                sc[n, pl.ds(pl.multiple_of(i * KEYS, KEYS), KEYS), :] = st
+                new.append(jnp.maximum(peaks[n], jnp.max(st.reshape(16, 8, 512), axis=0)))
+            return tuple(new)
+
+        start = tuple(jnp.full((8, 512), MASKED, F32) for _ in range(3))
+        peaks = lax.fori_loop(0, 8, scores, start)
+        peaks = [jnp.max(p, axis=0, keepdims=True) for p in peaks]
+        if old is not None:
+            peaks = [jnp.maximum(p, o[0]) for p, o in zip(peaks, old)]
+        totals = []
+        for n in range(3):
+            if old is None:
+                acc[n] = jnp.zeros((64, 512), F32)
+                totals.append(jnp.zeros((8, 512), F32))
+            else:
+                shrink = jnp.exp(old[n][0] - peaks[n])
+                acc[n] = acc[n] * shrink
+                totals.append(old[n][1] * shrink)
+
+        def mix(i, sums):
+            b = b0 + (b1 - b0) * (i // 2)
+            xs = (i % 2) * 2
+            new = []
+            for n in range(3):
+                at = pl.ds(pl.multiple_of(i * 256, 256), 256)
+                p = jnp.exp(sc[n, at, :] - peaks[n])
+                new.append(sums[n] + jnp.sum(p.reshape(32, 8, 512), axis=0))
+                v = slice(192 + 64 * n, 256 + 64 * n)
+                values = jnp.concatenate([kvb[b, xs, v, :], kvb[b, xs + 1, v, :]], axis=1)
+                acc[n] += mxu(values, p.astype(BF))
+            return tuple(new)
+
+        totals = lax.fori_loop(0, 4, mix, tuple(totals))
+        return list(zip(peaks, totals))
+
+    state = half(k, k_partner, None)
+    for s in (0, 1, 3, 2):
+        slot = kvb.at[k_across, (x + 4 - s) % 4]
+        arrived(slot, ysend.at[s], yrecv.at[s], across)
+        send(slot, slot, fsend.at[s], frecv.at[s], partner)
+    for s in (0, 1, 3, 2):
+        arrived(kvb.at[k_diag, (x + 4 - s) % 4], fsend.at[s], frecv.at[s], partner)
+    keep = pltpu.make_async_copy(kvb, kv_out, osem)
+    keep.start()
+    state = half(k_across, k_diag, state)
+    log_out[...] = jnp.zeros_like(log_out)
+    for n in range(3):
+        total = jnp.sum(state[n][1], axis=0, keepdims=True)
+        mixed = acc[n] / total
+        att_out[64 * n : 64 * n + 64, :] = mixed
+        log_out[n : n + 1, :] = state[n][0] + jnp.log(total)
+        for xs in range(4):
+            back[xs, 64 * n : 64 * n + 64, :] = mixed[:, 128 * xs : 128 * xs + 128].astype(BF)
+    ab[x] = back[x]
+    for s in (2, 1, 3):
+        peer = peer_of(me, "x", s)
+        send(back.at[peer["x"]], ab.at[x], bsend.at[s - 1], brecv.at[s - 1], peer)
+    q_out[...] = qb[...]
+    loads[1].wait()
+    loads[2].wait()
+    for s in (1, 3, 2):
+        source = peer_of(me, "x", 4 - s)
+        arrived(ab.at[source["x"]], bsend.at[s - 1], brecv.at[s - 1], source)
+    mixed = ab[...].reshape(768, 128).astype(F32).T.astype(BF)
+    mixed_out[...] = mixed
+    before = hid[...].astype(F32) + (mxu(mixed, vj[:, 2304:3072]) + rows[2:3])
+    before1_out[...] = before
+    first = normalized(before)[0] * rows[3:4] + rows[4:5]
+    low = first.astype(BF)
+    low_out[...] = low
+    second = first + rows[5:6]
+    for q in range(4):
+        at = slice(768 * q, 768 * q + 768)
+        u = mxu(low, vu[:, at]) + up_add[:, at]
+        up_out[:, at] = u
+        a = (u * normal_cdf(u)).astype(BF)
+        act_out[:, at] = a
+        second = second + mxu(a, vd[at, :])
+    before2_out[...] = second
+    res[...] = (normalized(second)[0] * rows[6:7] + rows[7:8]).astype(BF)
+    keep.wait()
+    for copy in sends:
+        copy.wait_send()
+
+
+def forward_layer(hidden, rows, up_add, lengths, wj, wu, wd):
+    vmem = pl.BlockSpec(memory_space=pltpu.VMEM)
+    anyspace = pl.BlockSpec(memory_space=pl.ANY)
+    dma = pltpu.SemaphoreType.DMA
+    out = jax.ShapeDtypeStruct
+    return pl.pallas_call(
+        forward_kernel,
+        out_shape=[
+            out((128, 768), BF),
+            out((4, 192, 128), BF),
+            out((4, 4, 384, 128), BF),
+            out((8, 512), F32),
+            out((192, 512), F32),
+            out((128, 768), BF),
+            out((128, 768), F32),
+            out((128, 768), BF),
+            out((128, 3072), F32),
+            out((128, 3072), BF),
+            out((128, 768), F32),
+        ],
+        in_specs=[vmem, vmem, vmem, pl.BlockSpec(memory_space=pltpu.SMEM)] + [anyspace] * 3,
+        out_specs=[vmem, vmem, anyspace] + [vmem] * 8,
+        scratch_shapes=[
+            pltpu.VMEM((768, 3072), BF),
+            pltpu.VMEM((768, 3072), BF),
+            pltpu.VMEM((3072, 768), BF),
+            pltpu.VMEM((4, 576, 128), BF),
+            pltpu.VMEM((4, 192, 128), BF),
+            pltpu.VMEM((4, 4, 384, 128), BF),
+            pltpu.VMEM((3, 1024, 512), F32),
+            pltpu.VMEM((3, 64, 512), F32),
+            pltpu.VMEM((4, 192, 128), BF),
+            pltpu.VMEM((4, 192, 128), BF),
+            dma((3,)),
+            dma,
+            dma((3,)),
+            dma((3,)),
+            dma((3,)),
+            dma((3,)),
+            dma((4,)),
+            dma((4,)),
+            dma((4,)),
+            dma((4,)),
+            dma((4,)),
+            dma((4,)),
+            dma((3,)),
+            dma((3,)),
+        ],
+        compiler_params=pltpu.CompilerParams(
+            collective_id=2, has_side_effects=True, vmem_limit_bytes=60 * 1024 * 1024
+        ),
+        name="forward_layer",
+    )(hidden, rows, up_add, lengths, wj, wu, wd)
+
+
+def backward_kernel(*refs):
+    dy, rows, up, before2, before1, qb, kvb, logs, att, lens, wj, wu, wd = refs[:13]
+    dh_out, dj_out, db_out, du_out, df_out, vec_out = refs[13:19]
+    vj, vu, vd, das, dab, dkv, rx, ry, rl, py, dq, sb, dj = refs[19:32]
+    wsem, asend, arecv, csend, crecv, jsend, jrecv = refs[32:]
+    me = my_place()
+    x, c = me["x"], me["c"]
+    yh = me["y"] // 2
+    partner, across = peer_of(me, "c", 1), peer_of(me, "y", 2)
+    loads = [
+        pltpu.make_async_copy(a, b, wsem.at[i])
+        for i, (a, b) in enumerate(((wd, vd), (wu, vu), (wj, vj)))
+    ]
+    for copy in loads:
+        copy.start()
+    greet_sequence(me)
+    sends = []
+
+    def send(src, dst, s, r, place):
+        copy = remote(src, dst, s, r, place)
+        copy.start()
+        sends.append(copy)
+
+    def arrived(slot, s, r, place):
+        remote(slot, slot, s, r, place).wait_recv()
+
+    def column_sum(a):
+        return jnp.sum(a.astype(F32), axis=0, keepdims=True)
+
+    vec_out[...] = jnp.zeros_like(vec_out)
+    d_second, gain_grad, shift_grad = norm_backward(before2[...], rows[6:7], dy[...])
+    vec_out[6:7] = gain_grad
+    vec_out[7:8] = shift_grad
+    df = d_second.astype(BF)
+    df_out[...] = df
+    vec_out[5:6] = column_sum(df)
+    loads[0].wait()
+    loads[1].wait()
+    d_first = d_second
+    for q in range(4):
+        at = slice(768 * q, 768 * q + 768)
+        u = up[:, at]
+        slope = normal_cdf(u) + u * (0.3989422804014327 * jnp.exp(-0.5 * u * u))
+        du = (mxu(df, vd[at, :], FAR) * slope).astype(BF)
+        du_out[:, at] = du
+        vec_out[8 + q : 9 + q] = column_sum(du)
+        d_first = d_first + mxu(du, vu[:, at], FAR)
+    d_sum, gain_grad, shift_grad = norm_backward(before1[...], rows[3:4], d_first)
+    vec_out[3:4] = gain_grad
+    vec_out[4:5] = shift_grad
+    db = d_sum.astype(BF)
+    db_out[...] = db
+    vec_out[2:3] = column_sum(db)
+    dh_out[...] = d_sum
+    loads[2].wait()
+    da = mxu(db, vj[:, 2304:3072], FAR).T.astype(BF)
+    for g in range(4):
+        das[g] = da[192 * g : 192 * g + 192]
+    dab[x] = das[x]
+    for s in (2, 1, 3):
+        peer = peer_of(me, "x", s)
+        send(das.at[peer["x"]], dab.at[x], asend.at[s - 1], arecv.at[s - 1], peer)
+    for s in (1, 3, 2):
+        source = peer_of(me, "x", 4 - s)
+        arrived(dab.at[source["x"]], asend.at[s - 1], arecv.at[s - 1], source)
+    length = lens[0]
+
+    def by_head(ref, n):
+        return jnp.concatenate([ref[xs, 64 * n : 64 * n + 64] for xs in range(4)], axis=1)
+
+    inner = []
+    for n in range(3):
+        dq[n] = jnp.zeros((64, 512), F32)
+        inner.append(
+            jnp.sum(
+                by_head(dab, n).astype(F32) * att[64 * n : 64 * n + 64, :], axis=0, keepdims=True
+            )
+        )
+
+    def half(which, base):
+        def step(i, carry):
+            core, xs = i // 4, i % 4
+            b = base + core
+            bias = key_bias(length, b, xs)
+            bias = jnp.concatenate([bias] * 2, axis=1)
+            for n in range(3):
+                own = slice(64 * n, 64 * n + 64)
+                keys = kvb[b, xs, own, :]
+                values = kvb[b, xs, slice(192 + 64 * n, 256 + 64 * n), :]
+                dk = dv = None
+                for h in range(2):
+                    at = slice(256 * h, 256 * h + 256)
+                    q_n = jnp.concatenate([qb[2 * h, own], qb[2 * h + 1, own]], axis=1)
+                    da_n = jnp.concatenate([dab[2 * h, own], dab[2 * h + 1, own]], axis=1)
+                    p = jnp.exp(mxu(keys, q_n, NEAR) + bias - logs[n : n + 1, at])
+                    dp = mxu(values, da_n, NEAR)
+                    ds = (p * (dp - inner[n][:, at])).astype(BF)
+                    dq[n, :, at] += mxu(keys, ds)
+                    k_term = mxu(q_n, ds, FAR)
+                    v_term = mxu(da_n, p.astype(BF), FAR)
+                    dk = k_term if dk is None else dk + k_term
+                    dv = v_term if dv is None else dv + v_term
+                dkv[which, core, xs, 64 * n : 64 * n + 64, :] = dk.astype(BF)
+                dkv[which, core, xs, 192 + 64 * n : 256 + 64 * n, :] = dv.astype(BF)
+            return carry
+
+        lax.fori_loop(0, 8, step, 0)
+
+    half(0, (1 - yh) * 2)
+    send(dkv.at[0, 1 - c], rx, csend.at[0], crecv.at[0], partner)
+    arrived(rx, csend.at[0], crecv.at[0], partner)
+    for xs in range(4):
+        py[xs] = (dkv[0, c, xs].astype(F32) + rx[xs].astype(F32)).astype(BF)
+    send(py, ry, csend.at[1], crecv.at[1], across)
+    half(1, yh * 2)
+    send(dkv.at[1, 1 - c], rl, csend.at[2], crecv.at[2], partner)
+    for xs in range(4):
+        for n in range(3):
+            part = dq[n, :, 128 * xs : 128 * xs + 128] * 0.125
+            sb[xs, 64 * n : 64 * n + 64, :] = part.astype(BF)
+    arrived(rl, csend.at[2], crecv.at[2], partner)
+    arrived(ry, csend.at[1], crecv.at[1], across)
+    for xs in range(4):
+        total = dkv[1, c, xs].astype(F32) + rl[xs].astype(F32) + ry[xs].astype(F32)
+        sb[xs, 192:576, :] = total.astype(BF)
+    dj[x] = sb[x]
+    for s in (2, 1, 3):
+        peer = peer_of(me, "x", s)
+        send(sb.at[peer["x"]], dj.at[x], jsend.at[s - 1], jrecv.at[s - 1], peer)
+    for s in (1, 3, 2):
+        source = peer_of(me, "x", 4 - s)
+        arrived(dj.at[source["x"]], jsend.at[s - 1], jrecv.at[s - 1], source)
+    dh = dh_out[...]
+    for j in range(3):
+        at = slice(768 * j, 768 * j + 768)
+        t = jnp.concatenate([dj[g, 192 * j : 192 * j + 192] for g in range(4)], axis=0)
+        t = t.astype(F32).T.astype(BF)
+        dj_out[:, at] = t
+        if j != 1:
+            row = 0 if j == 0 else 1
+            vec_out[row : row + 1] = column_sum(t)
+        dh = dh + mxu(t, vj[:, at], FAR)
+    dh_out[...] = dh
+    for copy in sends:
+        copy.wait_send()
+
+
+def backward_layer(dy, rows, up, before2, before1, q, kv, logs, att, lengths, wj, wu, wd):
+    vmem = pl.BlockSpec(memory_space=pltpu.VMEM)
+    anyspace = pl.BlockSpec(memory_space=pl.ANY)
+    dma = pltpu.SemaphoreType.DMA
+    out = jax.ShapeDtypeStruct
+    return pl.pallas_call(
+        backward_kernel,
+        out_shape=[
+            out((128, 768), F32),
+            out((128, 2304), BF),
+            out((128, 768), BF),
+            out((128, 3072), BF),
+            out((128, 768), BF),
+            out((16, 768), F32),
+        ],
+        in_specs=[vmem] * 9 + [pl.BlockSpec(memory_space=pltpu.SMEM)] + [anyspace] * 3,
+        out_specs=[vmem] * 6,
+        scratch_shapes=[
+            pltpu.VMEM((768, 3072), BF),
+            pltpu.VMEM((768, 3072), BF),
+            pltpu.VMEM((3072, 768), BF),
+            pltpu.VMEM((4, 192, 128), BF),
+            pltpu.VMEM((4, 192, 128), BF),
+            pltpu.VMEM((2, 2, 4, 384, 128), BF),
+            pltpu.VMEM((4, 384, 128), BF),
+            pltpu.VMEM((4, 384, 128), BF),
+            pltpu.VMEM((4, 384, 128), BF),
+            pltpu.VMEM((4, 384, 128), BF),
+            pltpu.VMEM((3, 64, 512), F32),
+            pltpu.VMEM((4, 576, 128), BF),
+            pltpu.VMEM((4, 576, 128), BF),
+            dma((3,)),
+            dma((3,)),
+            dma((3,)),
+            dma((3,)),
+            dma((3,)),
+            dma((3,)),
+            dma((3,)),
+        ],
+        compiler_params=pltpu.CompilerParams(
+            collective_id=3, has_side_effects=True, vmem_limit_bytes=60 * 1024 * 1024
+        ),
+        name="backward_layer",
+    )(dy, rows, up, before2, before1, q, kv, logs, att, lengths, wj, wu, wd)
 
 
 def body(
@@ -528,271 +938,35 @@
     weights_of = []
     for layer_index in range(LAYERS):
         up_full, down_full, joint_out = gathered[3 * layer_index : 3 * layer_index + 3]
-        up_full = up_full.reshape(768, 3072)
-        down_full = down_full.reshape(3072, 768)
-        joint_out = joint_out.reshape(768, 3072)
-        rows = rows_all[layer_index]
         weights_of.append(
-            (
-                joint_out[:, :2304],
-                rows[0],
-                rows[1],
-                joint_out[:, 2304:],
-                rows[2],
-                rows[3],
-                rows[4],
-                up_full,
-                up_adds[layer_index],
-                down_full,
-                rows[5],
-                rows[6],
-                rows[7],
-            )
+            (joint_out.reshape(768, 3072), up_full.reshape(768, 3072), down_full.reshape(3072, 768))
         )
-    seq_count, tok_count, width = inputs.shape
-    row_count = seq_count * tok_count
-    head_devices = lax.axis_size("head")
-    blk_devices = lax.axis_size("blk")
-    group_heads = HEADS // head_devices
-    score_scale = HD ** (-0.5)
-    block_rows = head_devices * tok_count
-    places = jnp.arange(blk_devices * block_rows, dtype=jnp.int32)
-    block_index = places // block_rows
-    within = places % block_rows
-    key_places = (within // tok_count * blk_devices + block_index) * tok_count + within % tok_count
-
-    def masked_scores(query, key_rows, length):
-        query_heads = query.reshape(query.shape[0], group_heads, HD)
-        key_heads = key_rows.reshape(key_rows.shape[0], group_heads, HD)
-        raw_scores = jnp.einsum(
-            "qhe,khe->hqk", query_heads, key_heads, preferred_element_type=jnp.float32
+    rows_all = rows_all.astype(F32)
+    up_adds = up_adds.astype(F32)
+    hidden = inputs.reshape(128, 768)
+    kept, outputs = [], []
+    for l in range(LAYERS):
+        result = forward_layer(
+            hidden, rows_all[l], up_adds[l : l + 1], lengths, *weights_of[l]
         )
-        key_valid = key_places < length
-        return jnp.where(key_valid[None, None, :], raw_scores * score_scale, MASKED)
-
-    def attend_forward(sequence_items):
-        query, key_rows, value_rows, length = sequence_items
-        scores = masked_scores(query, key_rows, length)
-        row_peak = jnp.max(scores, axis=-1, keepdims=True)
-        shifted = jnp.exp(scores - row_peak)
-        row_total = jnp.sum(shifted, axis=-1, keepdims=True)
-        probabilities = (shifted / row_total).astype(jnp.bfloat16)
-        value_heads = value_rows.reshape(value_rows.shape[0], group_heads, HD)
-        mixed_heads = jnp.einsum(
-            "hqk,khe->qhe", probabilities, value_heads, preferred_element_type=jnp.float32
-        )
-        log_total = row_peak[..., 0] + jnp.log(row_total[..., 0])
-        return (mixed_heads.reshape(query.shape[0], -1).astype(jnp.bfloat16), log_total)
-
-    def attend_backward(sequence_items):
-        query, key_rows, value_rows, length, log_total, grad_mixed = sequence_items
-        scores = masked_scores(query, key_rows, length)
-        probabilities = jnp.exp(scores - log_total[..., None])
-        query_heads = query.reshape(query.shape[0], group_heads, HD)
-        key_heads = key_rows.reshape(key_rows.shape[0], group_heads, HD)
-        value_heads = value_rows.reshape(value_rows.shape[0], group_heads, HD)
-        grad_heads = grad_mixed.reshape(grad_mixed.shape[0], group_heads, HD)
-        grad_probs = jnp.einsum(
-            "qhe,khe->hqk", grad_heads, value_heads, preferred_element_type=jnp.float32
-        )
-        row_inner = jnp.sum(probabilities * grad_probs, axis=-1, keepdims=True)
-        grad_scores = (probabilities * (grad_probs - row_inner) * score_scale).astype(jnp.bfloat16)
-        grad_query = jnp.einsum(
-            "hqk,khe->qhe", grad_scores, key_heads, preferred_element_type=jnp.float32
-        )
-        key_term = jnp.einsum(
-            "hqk,qhe->khe", grad_scores, query_heads, preferred_element_type=jnp.float32
-        )
-        value_term = jnp.einsum(
-            "hqk,qhe->khe",
-            probabilities.astype(jnp.bfloat16),
-            grad_heads,
-            preferred_element_type=jnp.float32,
-        )
-        key_total = key_rows.shape[0]
-        pair_term = jnp.concatenate(
-            [key_term.reshape(key_total, -1), value_term.reshape(key_total, -1)], axis=-1
-        )
-        return (grad_query.reshape(query.shape[0], -1).astype(jnp.bfloat16), pair_term)
-
-    hidden = inputs.reshape(row_count, width)
-    kept = []
-    outputs = []
-    for layer_index in range(LAYERS):
-        weights = weights_of[layer_index]
-        (
-            joint_full,
-            query_add,
-            value_add,
-            out_full,
-            out_add,
-            gain_first,
-            shift_first,
-            up_full,
-            up_add,
-            down_full,
-            down_add,
-            gain_second,
-            shift_second,
-        ) = weights
-        projected = row_product(hidden, joint_full)
-        query = (
-            (projected[:, :width] + query_add)
-            .astype(jnp.bfloat16)
-            .reshape(seq_count, tok_count, width)
-        )
-        key_rows = (
-            projected[:, width : 2 * width]
-            .astype(jnp.bfloat16)
-            .reshape(seq_count, tok_count, width)
-        )
-        value_rows = (
-            (projected[:, 2 * width :] + value_add)
-            .astype(jnp.bfloat16)
-            .reshape(seq_count, tok_count, width)
-        )
-        query_group, key_group, value_group = sent_together(
-            (query, key_rows, value_rows), "head", 2, 1, 0
-        )
-        key_all, value_all = sent_together_2((key_group, value_group), "blk", 1, 0)
-        mixed_group, log_total = lax.map(attend_forward, (query_group, key_all, value_all, lengths))
-        mixed_rows = lax.all_to_all(
-            mixed_group, "head", split_axis=1, concat_axis=2, tiled=True
-        ).reshape(row_count, width)
-        branch = row_product(mixed_rows, out_full) + out_add
-        before_first = hidden.astype(jnp.float32) + branch
-        first_norm = layer_norm(before_first, gain_first, shift_first)
-        first_low = first_norm.astype(jnp.bfloat16)
-        upward = row_product(first_low, up_full) + up_add
-        activated = exact_gelu(upward).astype(jnp.bfloat16)
-        before_second = first_norm + (row_product(activated, down_full) + down_add)
-        result = layer_norm(before_second, gain_second, shift_second)
-        result_low = result.astype(jnp.bfloat16)
-        outputs.append(result_low.reshape(seq_count, tok_count, width))
-        kept.append(
-            (
-                hidden,
-                query_group,
-                key_all,
-                value_all,
-                log_total,
-                mixed_rows,
-                before_first,
-                first_low,
-                upward,
-                activated,
-                before_second,
-            )
-        )
-        hidden = result_low
-    grad_rows = cotangent.reshape(row_count, width).astype(jnp.float32)
+        kept.append((hidden, *result[1:]))
+        hidden = result[0]
+        outputs.append(hidden.reshape(1, 128, 768))
+    grad_rows = cotangent.reshape(128, 768).astype(F32)
     layer_grads = [None] * LAYERS
     vector_grads = [None] * LAYERS
-    for layer_index in reversed(range(LAYERS)):
-        (
-            hidden,
-            query_group,
-            key_all,
-            value_all,
-            log_total,
-            mixed_rows,
-            before_first,
-            first_low,
-            upward,
-            activated,
-            before_second,
-        ) = kept[layer_index]
-        weights = weights_of[layer_index]
-        (
-            joint_full,
-            query_add,
-            value_add,
-            out_full,
-            out_add,
-            gain_first,
-            shift_first,
-            up_full,
-            up_add,
-            down_full,
-            down_add,
-            gain_second,
-            shift_second,
-        ) = weights
-        _, second_pull = jax.vjp(
-            layer_norm,
-            before_second,
-            gain_second.astype(jnp.float32),
-            shift_second.astype(jnp.float32),
+    for l in reversed(range(LAYERS)):
+        hidden, q, kv, logs, att, mixed, before1, low, up, acts, before2 = kept[l]
+        grad_rows, d_joint, d_branch, d_up, d_down, vector_grads[l] = backward_layer(
+            grad_rows, rows_all[l], up, before2, before1, q, kv, logs, att, lengths, *weights_of[l]
         )
-        grad_second, grad_gain_second, grad_shift_second = second_pull(grad_rows)
-        grad_down = grad_second.astype(jnp.bfloat16)
-        grad_down_add = column_sums(grad_down)
-        _, gelu_pull = jax.vjp(exact_gelu, upward)
-        grad_up = gelu_pull(times_transposed(grad_down, down_full))[0].astype(jnp.bfloat16)
-        grad_up_add = column_sums(grad_up)
-        grad_first = grad_second + times_transposed(grad_up, up_full)
-        _, first_pull = jax.vjp(
-            layer_norm,
-            before_first,
-            gain_first.astype(jnp.float32),
-            shift_first.astype(jnp.float32),
-        )
-        grad_before, grad_gain_first, grad_shift_first = first_pull(grad_first)
-        grad_branch = grad_before.astype(jnp.bfloat16)
-        grad_out_add = column_sums(grad_branch)
-        grad_mixed = (
-            times_transposed(grad_branch, out_full)
-            .astype(jnp.bfloat16)
-            .reshape(seq_count, tok_count, width)
-        )
-        grad_group = lax.all_to_all(grad_mixed, "head", split_axis=2, concat_axis=1, tiled=True)
-        grad_query_group, pair_terms = lax.map(
-            attend_backward, (query_group, key_all, value_all, lengths, log_total, grad_group)
-        )
-        pair_sums = sum_at_owner(pair_terms.astype(jnp.bfloat16), "blk", 1).astype(jnp.bfloat16)
-        group_width = pair_sums.shape[-1] // 2
-        grad_query, grad_key, grad_value = sent_together(
-            (grad_query_group, pair_sums[..., :group_width], pair_sums[..., group_width:]),
-            "head",
-            1,
-            2,
-            0,
-        )
-        grad_joint_rows = jnp.concatenate([grad_query, grad_key, grad_value], axis=-1).reshape(
-            row_count, 3 * width
-        )
-        grad_query_add = column_sums(grad_query)
-        grad_value_add = column_sums(grad_value)
-        grad_rows = grad_before + times_transposed(grad_joint_rows, joint_full)
-        layer_grads[layer_index] = (
-            hidden,
-            mixed_rows,
-            first_low,
-            activated,
-            grad_joint_rows,
-            grad_branch,
-            grad_up,
-            grad_down,
-        )
-        vector_grads[layer_index] = (
-            grad_query_add,
-            grad_value_add,
-            grad_out_add,
-            grad_gain_first,
-            grad_shift_first,
-            grad_down_add,
-            grad_gain_second,
-            grad_shift_second,
-            grad_up_add,
-        )
-    vectors = jnp.concatenate(
-        [a.reshape(-1, 768) for layer in vector_grads for a in layer] + [jnp.zeros((8, 768), jnp.float32)]
-    )
+        layer_grads[l] = (hidden, mixed, low, acts, d_joint, d_branch, d_up, d_down)
+    vectors = jnp.concatenate(vector_grads)
     joint_grad, out_grad, up_grad, down_grad, vectors = reduce_grads(layer_grads, vectors)
-    vectors = vectors[:24].reshape(LAYERS, 12, 768)
-    owner = lax.axis_index("batch") * blk_devices + lax.axis_index("blk")
+    vectors = vectors.reshape(LAYERS, 16, 768)
+    owner = lax.axis_index("batch") * 4 + lax.axis_index("blk")
     own_rows = lax.dynamic_slice_in_dim(vectors[:, :8], owner * 24, 24, axis=2)
-    own_up = lax.dynamic_slice_in_dim(vectors[:, 8:].reshape(LAYERS, 3072), owner * 96, 96, axis=1)
+    own_up = lax.dynamic_slice_in_dim(vectors[:, 8:12].reshape(LAYERS, 3072), owner * 96, 96, axis=1)
     stacked = (
         joint_grad,
         own_rows[:, 0],
@@ -809,7 +983,7 @@
         own_rows[:, 7],
     )
     activations = jnp.stack(outputs)
-    input_grad = grad_rows.reshape(seq_count, tok_count, width)
+    input_grad = grad_rows.reshape(1, 128, 768)
     return (
         activations,
         input_grad,

time: 684 us -> 410 us (0.60)
  matrix products: 190 us -> 0 us
  Pallas kernels: 200 us -> 375 us
  waiting for transfers between devices: 83.3 us -> 0 us
  local copies, waits for them, and re-layouts: 83.1 us -> 26.4 us
  starting transfers between devices: 33.8 us -> 0 us
  other arithmetic: 37.8 us -> 5.45 us
  blocking collectives: 31.5 us -> 0 us
  between operations: 17 us -> 1.67 us
    dot_general x28 -> x0, matrix products: 190 us -> none  [the longest x2 48.3 us: attend_backward(): jnp.einsum('hqk,khe->qhe', grad_scores, key_heads, preferred_element_type...]
    pallas_call x0 -> x4, Pallas kernels: none -> 175 us  [the longest x2 107 us: backward_layer(): pl.pallas_call(backward_kernel, out_shape=[out((128, 768), F32), out((128...]
    all_to_all x8 -> x0, waiting for transfers between devices: 43.2 us -> none  [the longest x2 28 us: sent_together(): lax.all_to_all(both, axis, split_axis=split_dim, concat_axis=concat_dim,...]
    all_gather x2 -> x0, waiting for transfers between devices: 40.1 us -> none  [sent_together_2(): whole = lax.all_gather(both, axis, axis=dim, tiled=True)]
    all_to_all x8 -> x0, starting transfers between devices: 33.3 us -> none  [the longest x2 8.71 us: body(): lax.all_to_all(mixed_group, 'head', split_axis=1, concat_axis=2, tiled=True)]
    all_to_all x2 -> x0, blocking collectives: 31.5 us -> none  [sent_together(): lax.all_to_all(both, axis, split_axis=split_dim, concat_axis=concat_dim,...]
    convert_element_type x42 -> x0, local copies, waits for them, and re-layouts: 15.9 us -> none  [the longest x16 6.48 us: layer_norm(): return centered * lax.rsqrt(variance + EPSILON) * gain + shift]
    reduce_sum x20 -> x0, other arithmetic: 15.4 us -> none  [the longest x2 5.63 us: attend_forward(): row_total = jnp.sum(shifted, axis=-1, keepdims=True)]
  transfers between devices with their start and end apart: 10 -> 0, of which waited for: 7 -> 0; matrix products, arithmetic and copies ran while one was open for 12% -> 0% of each run, Pallas kernels for 0% -> 0%
where the time goes in v2:
time: 410 us; the launch traced here: 408 us
  Pallas kernels  375 us (91%)
  local copies, waits for them, and re-layouts  26.4 us (6%)
  other arithmetic  5.45 us (1%)
    pallas_call x2, Pallas kernels, backward_layer(): pl.pallas_call(backward_kernel, out_shape=[out((128, 768), F32), out((128...  107 us
    pallas_call x1, Pallas kernels, gather_weights(): pl.pallas_call(gather_kernel, out_shape=[jax.ShapeDtypeStruct((4, 2, 2, 2...  107 us
    pallas_call x1, Pallas kernels, reduce_grads(): pl.pallas_call(reduce_kernel, out_shape=[jax.ShapeDtypeStruct((2, 24, 230...  92.8 us
    pallas_call x2, Pallas kernels, forward_layer(): pl.pallas_call(forward_kernel, out_shape=[out((128, 768), BF), out((4, 19...  68.6 us

profile of v2, /device:TPU:0, one launch (start us, length us, event | category | flops | bytes accessed | tf_op | source)
XLA Modules:
  0.0 408.4 jit_solution(2877463866819104649)
XLA Ops:
  0.6 1.0 constant_dynamic-update-slice_fusion.1
  1.6 0.9 constant_dynamic-update-slice_fusion
  2.5 1.8 slice_bitcast_fusion
  4.3 1.7 slice_bitcast_fusion.2
  6.0 0.7 reshape.134
  12.7 106.6 %gather_weights.1 = (bf16[4,2,2,2,24,3072]{5,4,3,2,1,0:T(8,128)(2,1)}, bf16[4,2,2,2,96,768]{5,4,3,2,1,0:T(8,128)(2,1)}, bf16[4,2,2,2,24,3072]{5,4,3,2,1,0:T(8,12...) custom-call(bf16[24,3072]{1,0:T(8,128)(2,1)} %get-tuple-element.125., ...), custom_call_target="tpu_custom_call" | custom-call | tf_op jit(solution)/shard_map/gather_weights/pallas_call | solution.py:161
  119.3 1.0 slice.106
  121.5 0.7 slice.90.refs_2_
  122.8 33.5 %forward_layer.2 = (bf16[128,768]{1,0:T(8,128)(2,1)}, bf16[4,192,128]{2,1,0:T(8,128)(2,1)}, bf16[4,4,384,128]{3,2,1,0:T(8,128)(2,1)}, f32[8,512]{1,0:T(8,128)}, ...) custom-call(bf16[128,768]{1,0:T(8,128)(2,1)} %bitcast.130, ...), custom_call_target="tpu_custom_call" | custom-call | tf_op jit(solution)/shard_map/forward_layer/pallas_call | solution.py:654
  158.0 35.1 %forward_layer.3 = (bf16[128,768]{1,0:T(8,128)(2,1)}, bf16[4,192,128]{2,1,0:T(8,128)(2,1)}, bf16[4,4,384,128]{3,2,1,0:T(8,128)(2,1)}, f32[8,512]{1,0:T(8,128)}, ...) custom-call(bf16[128,768]{1,0:T(8,128)(2,1)} %get-tuple-element.65.r, ...), custom_call_target="tpu_custom_call" | custom-call | tf_op jit(solution)/shard_map/forward_layer/pallas_call | solution.py:654
  193.2 0.8 bitcast_convert_fusion.refs_0_
  193.9 53.4 %backward_layer.2 = (f32[128,768]{1,0:T(8,128)}, bf16[128,2304]{1,0:T(8,128)(2,1)}, bf16[128,768]{1,0:T(8,128)(2,1)}, bf16[128,3072]{1,0:T(8,128)(2,1)}, bf16[128,768]{1,0:T(8,128)(2,1)}, /*index=5*/f32[16,768]{1,0:T(8,128)}) custom-call(f32[128,768]{1,0:T(8,128)} %bitcast_convert_fusion.refs_0_, f32[8,768]{1,0:T(8,128)} %squeeze.57.refs_1_, ...), custom_call_target="tpu_custom_call" | custom-call | tf_op jit(solution)/shard_map/backward_layer/pallas_call | solution.py:856
  247.4 53.4 %backward_layer.3 = (f32[128,768]{1,0:T(8,128)}, bf16[128,2304]{1,0:T(8,128)(2,1)}, bf16[128,768]{1,0:T(8,128)(2,1)}, bf16[128,3072]{1,0:T(8,128)(2,1)}, bf16[128,768]{1,0:T(8,128)(2,1)}, /*index=5*/f32[16,768]{1,0:T(8,128)}) custom-call(f32[128,768]{1,0:T(8,128)} %get-tuple-element.77.refs_0_, f32[8,768]{1,0:T(8,128)} %squeeze.56.refs_1_, ...), custom_call_target="tpu_custom_call" | custom-call | tf_op jit(solution)/shard_map/backward_layer/pallas_call | solution.py:856
  300.8 1.5 pad_maximum_fusion.3.refs_10_
  303.4 1.2 pad_maximum_fusion.1.refs_5_
  305.7 1.2 pad_maximum_fusion.refs_0_
  306.9 92.8 %reduce_grads.1 = (f32[2,24,2304]{2,1,0:T(8,128)}, f32[2,24,768]{2,1,0:T(8,128)}, f32[2,24,3072]{2,1,0:T(8,128)}, f32[2,96,768]{2,1,0:T(8,128)}, f32[32,768]{1,0:T(8,128)}) custom-call(bf16[2,2688,128]{2,1,0:T(8,128)(2,1)} %pad_maximum_fusion.refs_0_, bf16[128,3072]{1,0:T(8,128)(2,1)} %get-tuple-element.89.refs_1_, ...), custom_call_target="tpu_custom_call" | custom-call | tf_op jit(solution)/shard_map/reduce_grads/pallas_call | solution.py:390
  399.8 0.9 slice.113
  401.3 0.8 slice_bitcast_fusion.6
  402.8 0.8 pad_maximum_fusion.2
  403.6 0.7 copy.127
  404.3 1.8 copy.128
  406.8 0.8 copy.130
  407.6 0.8 copy.131
  (73 shorter events, 12.8 us)
Async XLA Ops:
  158.0 35.1 %copy-start.11 = (bf16[1,128,768]{2,1,0:T(8,128)(2,1)S(1)}, bf16[1,128,768]{2,1,0:T(8,128)(2,1)}, u32[]{:S(2)}) copy-start(bf16[1,128,768]{2,1,0:T(8,128)(2,1)} %param.31) | copy-start | bytes 589828
  247.4 53.4 %copy-start.14 = (f32[16,768]{1,0:T(8,128)S(1)}, f32[16,768]{1,0:T(8,128)}, u32[]{:S(2)}) copy-start(f32[16,768]{1,0:T(8,128)} %get-tuple-element.101) | copy-start | bytes 147460
  247.4 54.9 %copy-start.3 = (bf16[128,3072]{1,0:T(8,128)(2,1)S(1)}, bf16[128,3072]{1,0:T(8,128)(2,1)}, u32[]{:S(2)}) copy-start(bf16[128,3072]{1,0:T(8,128)(2,1)} %get-tuple-element.94) | copy-start | bytes 2359300
  300.8 2.0 copy-start.10
  300.8 2.2 copy-start.9
  300.8 2.4 copy-start
  302.8 1.8 copy-start.2
  303.4 1.7 copy-start.8
  303.4 1.9 copy-start.7
  304.6 0.9 copy-start.1
  306.9 95.9 %copy-start.12 = (bf16[128,768]{1,0:T(8,128)(2,1)S(1)}, bf16[128,768]{1,0:T(8,128)(2,1)}, u32[]{:S(2)}) copy-start(bf16[128,768]{1,0:T(8,128)(2,1)} %get-tuple-element.69) | copy-start | bytes 589828
  306.9 96.6 %copy-start.6 = (f32[128,768]{1,0:T(8,128)S(1)}, f32[128,768]{1,0:T(8,128)}, u32[]{:S(2)}) copy-start(f32[128,768]{1,0:T(8,128)} %get-tuple-element.85) | copy-start | bytes 1179652
  399.7 6.4 %copy-start.13 = (f32[2,24,768]{2,1,0:T(8,128)S(1)}, f32[2,24,768]{2,1,0:T(8,128)}, u32[]{:S(2)}) copy-start(f32[2,24,768]{2,1,0:T(8,128)} %get-tuple-element.147) | copy-start | bytes 442372
  399.7 7.1 %copy-start.5 = (f32[2,24,3072]{2,1,0:T(8,128)S(1)}, f32[2,24,3072]{2,1,0:T(8,128)}, u32[]{:S(2)}) copy-start(f32[2,24,3072]{2,1,0:T(8,128)} %get-tuple-element.151) | copy-start | bytes 1769476
  399.7 7.9 %copy-start.4 = (f32[2,96,768]{2,1,0:T(8,128)S(1)}, f32[2,96,768]{2,1,0:T(8,128)}, u32[]{:S(2)}) copy-start(f32[2,96,768]{2,1,0:T(8,128)} %get-tuple-element.153) | copy-start | bytes 1769476

commit v3 on v2

--- a/solution.py
+++ b/solution.py
@@ -1,3 +1,5 @@
+import functools
+
 import jax
 import jax.numpy as jnp
 from jax import lax
@@ -55,124 +57,158 @@
     )
 
 
-PIECES = (
-    (0, ("z", "y", "x")),
-    (1, ("z", "y")),
-    (2, ("y", "z")),
-    (3, ("z", "y", "x")),
-    (4, ("z", "y")),
-    (5, ("y", "z")),
-    (6, ("y", "z")),
-)
-
-
-def gather_kernel(*refs):
-    n = len(PIECES)
-    ins, outs = refs[:n], refs[n : 2 * n]
-    send, recv, fsend, frecv, local = refs[2 * n :]
-    me = my_place()
-    partner = peer_of(me, "c", 1)
-
-    def region(i, phase, place):
-        array, order = PIECES[i]
+class Gather:
+    def __init__(self, me, pieces, ins, outs, sems):
+        self.me, self.pieces, self.ins, self.outs = me, pieces, ins, outs
+        self.send, self.recv, self.fsend, self.frecv, self.local = sems
+        self.partner = peer_of(me, "c", 1)
+        self.started, self.locals = [], {}
+
+    def order(self, i):
+        return self.pieces[i][3]
+
+    def direct(self, i, phase):
+        return phase in self.pieces[i][5]
+
+    def region(self, i, phase, place, half=None):
+        array, start, width, order, by_rows, _ = self.pieces[i]
         done = order[:phase]
         z = ALL if "z" in done else place["z"]
         y = (ALL, ALL) if "y" in done else (place["y"] % 2, place["y"] // 2)
-        cols = ALL
+        lines = ALL
         if "x" in order and "x" not in done:
-            cols = pl.ds(pl.multiple_of(place["x"] * 768, 128), 768)
-        return outs[i].at[z, y[0], y[1], place["c"], ALL, cols]
-
-    def own(i):
-        if "x" in PIECES[i][1]:
-            return ins[i].at[ALL, pl.ds(pl.multiple_of(me["x"] * 768, 128), 768)]
-        return ins[i]
-
-    def step(i, phase, s):
-        axis = PIECES[i][1][phase]
-        src = own(i) if phase == 0 else region(i, phase, me)
-        return remote(
-            src,
-            region(i, phase, me),
-            send.at[i, phase, s - 1],
-            recv.at[i, phase, s - 1],
-            peer_of(me, axis, s),
+            width = width // 4
+            start = start + place["x"] * width
+        if half is not None:
+            if by_rows:
+                count = self.outs[array].shape[-2] // 2
+                lines = pl.ds(count * half, count)
+            else:
+                width = width // 2
+                start = start + half * width
+        columns = self.columns(array, start, width)
+        return self.outs[array].at[z, y[0], y[1], place["c"], lines, columns]
+
+    def columns(self, array, start, width):
+        if width == self.outs[array].shape[-1]:
+            return ALL
+        return pl.ds(start if isinstance(start, int) else pl.multiple_of(start, 128), width)
+
+    def own(self, i):
+        array, start, width, order, _, _ = self.pieces[i]
+        if "x" in order:
+            width = width // 4
+            start = start + self.me["x"] * width
+        columns = self.columns(array, start, width)
+        return self.ins[array].at[ALL, columns]
+
+    def copy(self, src, dst, s, r, place):
+        copy = remote(src, dst, s, r, place)
+        copy.start()
+        self.started.append(copy)
+
+    def near(self, i, phase):
+        axis = self.order(i)[phase]
+        return peer_of(self.me, axis, 1), peer_of(self.me, axis, 3), peer_of(self.me, axis, 2)
+
+    def start(self, i, phase):
+        right, left, opposite = self.near(i, phase)
+        dst = self.region(i, phase, self.me)
+        if phase == 0:
+            copy = pltpu.make_async_copy(self.own(i), dst, self.local.at[i])
+            copy.start()
+            self.locals[i] = copy
+        src = self.own(i) if phase == 0 else dst
+        places = [(0, right), (1, left)]
+        if self.direct(i, phase):
+            places = [(2, opposite)] + places
+        for j, place in places:
+            self.copy(src, dst, self.send.at[i, phase, j], self.recv.at[i, phase, j], place)
+        if phase == 0:
+            self.copy(src, dst, self.fsend.at[i, 3, 0], self.frecv.at[i, 3, 0], self.partner)
+
+    def arrived(self, slot, i, phase, j, place):
+        remote(
+            slot, slot, self.send.at[i, phase, j], self.recv.at[i, phase, j], place
+        ).wait_recv()
+
+    def pass_on(self, i, phase, j, place):
+        slot = self.region(i, phase, place)
+        self.copy(
+            slot, slot, self.fsend.at[i, phase, j], self.frecv.at[i, phase, j], self.partner
         )
 
-    def landed(i, phase, s):
-        axis = PIECES[i][1][phase]
-        place = peer_of(me, axis, 4 - s)
-        r = region(i, phase, place)
-        return remote(r, r, send.at[i, phase, s - 1], recv.at[i, phase, s - 1], place)
-
-    def forward(i, phase, s):
-        axis = PIECES[i][1][phase]
-        r = region(i, phase, peer_of(me, axis, 4 - s))
-        return remote(r, r, fsend.at[i, phase, s - 1], frecv.at[i, phase, s - 1], partner)
-
-    def forwarded(i, phase, s):
-        axis = PIECES[i][1][phase]
-        r = region(i, phase, peer_of(partner, axis, 4 - s))
-        return remote(r, r, fsend.at[i, phase, s - 1], frecv.at[i, phase, s - 1], partner)
-
-    greet_all(me)
-    copies, sends, fwds = [], [], []
-    for i in range(n):
-        for s in (2, 1, 3):
-            c = step(i, 0, s)
-            c.start()
-            sends.append(c)
-        c = pltpu.make_async_copy(own(i), region(i, 0, me), local.at[i])
-        c.start()
-        copies.append(c)
-        c = remote(own(i), region(i, 0, me), fsend.at[i, 3, 0], frecv.at[i, 3, 0], partner)
-        c.start()
-        fwds.append(c)
-    for c in copies:
-        c.wait()
-    for phase in range(3):
-        for i in range(n):
-            order = PIECES[i][1]
-            if phase >= len(order):
-                continue
-            for s in (1, 3, 2):
-                landed(i, phase, s).wait_recv()
-                c = forward(i, phase, s)
-                c.start()
-                fwds.append(c)
-            if phase + 1 < len(order):
-                for s in (2, 1, 3):
-                    c = step(i, phase + 1, s)
-                    c.start()
-                    sends.append(c)
-    for i in range(n):
-        r = region(i, 0, partner)
-        remote(r, r, fsend.at[i, 3, 0], frecv.at[i, 3, 0], partner).wait_recv()
-        for phase in range(len(PIECES[i][1])):
-            for s in (1, 2, 3):
-                forwarded(i, phase, s).wait_recv()
-    for c in sends + fwds:
-        c.wait_send()
-
-
-def gather_weights(pieces):
-    n = len(pieces)
-    anyspace = pl.BlockSpec(memory_space=pl.ANY)
-    return pl.pallas_call(
-        gather_kernel,
-        out_shape=[jax.ShapeDtypeStruct((4, 2, 2, 2, *p.shape), p.dtype) for p in pieces],
-        in_specs=[anyspace] * n,
-        out_specs=[anyspace] * n,
-        scratch_shapes=[
-            pltpu.SemaphoreType.DMA((n, 3, 3)),
-            pltpu.SemaphoreType.DMA((n, 3, 3)),
-            pltpu.SemaphoreType.DMA((n, 4, 3)),
-            pltpu.SemaphoreType.DMA((n, 4, 3)),
-            pltpu.SemaphoreType.DMA((n,)),
-        ],
-        compiler_params=pltpu.CompilerParams(collective_id=0, has_side_effects=True),
-        name="gather_weights",
-    )(*pieces)
+    def relay(self, i, phase):
+        right, left, _ = self.near(i, phase)
+        for j, source, target in ((0, left, right), (1, right, left)):
+            self.arrived(self.region(i, phase, source), i, phase, j, source)
+            if not self.direct(i, phase):
+                part = self.region(i, phase, source, j)
+                self.copy(
+                    part, part, self.send.at[i, phase, 2 + j], self.recv.at[i, phase, 2 + j], target
+                )
+            self.pass_on(i, phase, j, source)
+
+    def close(self, i, phase):
+        right, left, opposite = self.near(i, phase)
+        if self.direct(i, phase):
+            self.arrived(self.region(i, phase, opposite), i, phase, 2, opposite)
+        else:
+            for j, source in ((0, left), (1, right)):
+                self.arrived(self.region(i, phase, opposite, j), i, phase, 2 + j, source)
+        self.pass_on(i, phase, 2, opposite)
+        if phase == 0:
+            self.locals[i].wait()
+
+    def complete(self, i):
+        slots = [((3, 0), self.region(i, 0, self.partner))]
+        for phase, axis in enumerate(self.order(i)):
+            for j, s in ((0, 3), (1, 1), (2, 2)):
+                slots.append(((phase, j), self.region(i, phase, peer_of(self.partner, axis, s))))
+        for at, slot in slots:
+            remote(
+                slot, slot, self.fsend.at[i, *at], self.frecv.at[i, *at], self.partner
+            ).wait_recv()
+
+    def end(self):
+        for copy in self.started:
+            copy.wait_send()
+
+
+    def relay_all(self, phase, *group):
+        for i in group:
+            self.relay(i, phase)
+
+    def close_all(self, phase, *group):
+        for i in group:
+            self.close(i, phase)
+            if phase + 1 < len(self.order(i)):
+                self.start(i, phase + 1)
+
+
+def joint_pieces(array, direct):
+    return (
+        (array, 0, 1536, ("y", "z"), False, direct),
+        (array, 1536, 1536, ("z", "y"), False, direct),
+    )
+
+
+def feed_pieces(array, order, direct):
+    return (
+        (array, 0, 3072, order, False, direct),
+        (array + 1, 0, 384, ("y", "z"), True, direct),
+        (array + 1, 384, 384, ("y", "z"), True, direct),
+    )
+
+
+NEVER = ()
+FIRST_PIECES = (
+    feed_pieces(0, ("y", "z", "x"), NEVER)
+    + joint_pieces(2, NEVER)
+    + joint_pieces(3, NEVER)
+    + ((4, 0, 256, ("y", "z"), True, NEVER),)
+)
+SECOND_PIECES = feed_pieces(0, ("y", "z", "x"), NEVER)
 
 
 THIRDS = (("x", "y", "z"), ("y", "z", "x"), ("z", "x", "y"))
@@ -181,8 +217,8 @@
 def reduce_kernel(*refs):
     ins = refs[:11]
     joint_out, out_out, up_out, down_out, vec_out = refs[11:16]
-    lhs, rhs, g, r1, s1, r2, s2, r3, last, vc, va = refs[16:27]
-    csend, crecv, lsem, ps, pr, vs, vr = refs[27:]
+    lhs, rhs, g, o1, r1, s1, o2, r2, s2, r3, last, vc, va = refs[16:29]
+    csend, crecv, lsem, ps, pr, qs, qr, vs, vr = refs[29:]
     vec_in = ins[10]
     me = my_place()
     partner = peer_of(me, "c", 1)
@@ -281,7 +317,61 @@
                 peer_of(me, axis, s),
             ).wait_recv()
 
-    dims = (((0,), (0,)), ((), ()))
+    def ring_copy(phase, t, l, j, src, dst, peer):
+        copy = remote(src, dst, qs.at[phase, t, l, j], qr.at[phase, t, l, j], peer)
+        copy.start()
+        sends.append(copy)
+
+    def ring_wait(phase, t, l, j, slot, peer):
+        remote(slot, slot, qs.at[phase, t, l, j], qr.at[phase, t, l, j], peer).wait_recv()
+
+    def ring_refs(phase, t, l):
+        axis = THIRDS[t][phase]
+        places = [peer_of(me, axis, s) for s in (1, 3, 2)]
+        held, over, got = ((g, o1, r1), (s1, o2, r2))[phase]
+        return axis, places, held.at[t, l], over.at[t, l], got.at[t, l]
+
+    low_half, high_half = pl.ds(0, 2), pl.ds(2, 2)
+
+    def ring_start(phase, t, l):
+        axis, (right, left, far), held, over, got = ring_refs(phase, t, l)
+        ring_copy(phase, t, l, 0, held.at[far[axis], low_half], over.at[0], right)
+        ring_copy(phase, t, l, 1, held.at[far[axis], high_half], over.at[1], left)
+        ring_copy(
+            phase, t, l, 2, held.at[right[axis], high_half], got.at[0, high_half], right
+        )
+        ring_copy(phase, t, l, 3, held.at[left[axis], low_half], got.at[1, low_half], left)
+
+    def ring_middle(phase, t, l):
+        axis, (right, left, far), held, over, got = ring_refs(phase, t, l)
+        for j, source, target in ((0, left, right), (1, right, left)):
+            ring_wait(phase, t, l, j, over.at[j], source)
+            for a in range(2):
+                at = target[axis]
+                if phase == 0:
+
+                    def merge(b, carry, a=a, j=j, at=at):
+                        total = held[at, 2 * j + a, b].astype(f32) + over[j, a, b].astype(f32)
+                        held[at, 2 * j + a, b] = total.astype(jnp.bfloat16)
+                        return carry
+
+                    lax.fori_loop(0, 4, merge, 0)
+                else:
+                    total = held[at, 2 * j + a].astype(f32) + over[j, a].astype(f32)
+                    held[at, 2 * j + a] = total.astype(jnp.bfloat16)
+            part = (low_half, high_half)[j]
+            ring_copy(
+                phase, t, l, 4 + j, held.at[target[axis], part], got.at[j, part], target
+            )
+
+    def ring_finish(phase, t, l):
+        axis, (right, left, far), held, over, got = ring_refs(phase, t, l)
+        ring_wait(phase, t, l, 2, got.at[0, high_half], left)
+        ring_wait(phase, t, l, 3, got.at[1, low_half], right)
+        ring_wait(phase, t, l, 4, got.at[0, low_half], left)
+        ring_wait(phase, t, l, 5, got.at[1, high_half], right)
+
+    f32 = jnp.float32
     for l in layers:
         away, here = exchanged[l]
         for copy in here:
@@ -301,36 +391,37 @@
                     z, y = i // 4, (i % 2) * 2 + (i // 2) % 2
                     at = ((q, y, z), (y, z, q), (z, q, y))[t]
                     g[t, l, at[0], at[1], at[2]] = block[24 * i : 24 * i + 24].astype(jnp.bfloat16)
-            send_chunks(
-                0, t, l, lambda a, t=t, l=l: g.at[t, l, a], lambda s, t=t, l=l: r1.at[t, l, s - 1]
-            )
+            ring_start(0, t, l)
     vec_start(1, vec_finish(0))
-    f32 = jnp.float32
+    for l in layers:
+        for t in range(3):
+            ring_middle(0, t, l)
     for l in layers:
         for t in range(3):
             mine = me[THIRDS[t][0]]
-            await_chunks(0, t, l, lambda s, t=t, l=l: r1.at[t, l, s - 1])
+            ring_finish(0, t, l)
 
             def add1(i, carry, t=t, l=l, mine=mine):
                 a, b = i // 4, i % 4
                 total = g[t, l, mine, a, b].astype(f32)
-                for s in range(3):
+                for s in range(2):
                     total = total + r1[t, l, s, a, b].astype(f32)
                 s1[t, l, a, b] = total.astype(jnp.bfloat16)
                 return carry
 
             lax.fori_loop(0, 16, add1, 0)
-            send_chunks(
-                1, t, l, lambda a, t=t, l=l: s1.at[t, l, a], lambda s, t=t, l=l: r2.at[t, l, s - 1]
-            )
+            ring_start(1, t, l)
     vec_start(2, vec_finish(1))
     for l in layers:
         for t in range(3):
+            ring_middle(1, t, l)
+    for l in layers:
+        for t in range(3):
             mine = me[THIRDS[t][1]]
-            await_chunks(1, t, l, lambda s, t=t, l=l: r2.at[t, l, s - 1])
+            ring_finish(1, t, l)
             for a in range(4):
                 total = s1[t, l, mine, a].astype(f32)
-                for s in range(3):
+                for s in range(2):
                     total = total + r2[t, l, s, a].astype(f32)
                 s2[t, l, a] = total.astype(jnp.bfloat16)
             send_chunks(
@@ -402,9 +493,11 @@
             pltpu.VMEM((2, 2688, 256), bf),
             pltpu.VMEM((2, 256, 6912), bf),
             pltpu.VMEM((3, 2, 4, 4, 4, 24, 768), bf),
-            pltpu.VMEM((3, 2, 3, 4, 4, 24, 768), bf),
+            pltpu.VMEM((3, 2, 2, 2, 4, 24, 768), bf),
+            pltpu.VMEM((3, 2, 2, 4, 4, 24, 768), bf),
             pltpu.VMEM((3, 2, 4, 4, 24, 768), bf),
-            pltpu.VMEM((3, 2, 3, 4, 24, 768), bf),
+            pltpu.VMEM((3, 2, 2, 2, 24, 768), bf),
+            pltpu.VMEM((3, 2, 2, 4, 24, 768), bf),
             pltpu.VMEM((3, 2, 4, 24, 768), bf),
             pltpu.VMEM((3, 2, 3, 24, 768), bf),
             pltpu.VMEM((3, 2, 4, 24, 768), bf),
@@ -415,6 +508,8 @@
             dma((2, 5)),
             dma((4, 3, 2, 3)),
             dma((4, 3, 2, 3)),
+            dma((2, 3, 2, 6)),
+            dma((2, 3, 2, 6)),
             dma((4, 3)),
             dma((4, 3)),
         ],
@@ -475,14 +570,38 @@
     return jnp.where(rows < limit, 0.0, MASKED)
 
 
-def forward_kernel(*refs):
-    hid, rows, up_add, lens, wj, wu, wd = refs[:7]
-    res, q_out, kv_out, log_out, att_out, mixed_out = refs[7:13]
-    before1_out, low_out, up_out, act_out, before2_out = refs[13:18]
-    vj, vu, vd, qs, qb, kvb, sc, acc, back, ab = refs[18:28]
-    wsem, osem, qsend, qrecv, xsend, xrecv, csend, crecv, ysend, yrecv, fsend, frecv = refs[28:40]
-    bsend, brecv = refs[40:]
+def forward_kernel(first, *refs):
+    refs = list(refs)
+
+    def take(count):
+        out = refs[:count]
+        del refs[:count]
+        return out
+
+    hid, lens = take(2)
+    if first:
+        small_in = take(9)
+        up, down, joint_in = take(3)
+        shards = [up.at[0], down.at[0], joint_in.at[0], joint_in.at[1]]
+    else:
+        rows, up_add, wj = take(3)
+        up, down = take(2)
+        shards = [up.at[1], down.at[1]]
+    res, q_out, kv_out, log_out, att_out, mixed_out = take(6)
+    before1_out, low_out, up_out, act_out, before2_out = take(5)
+    if first:
+        rows_out, add_out = take(2)
+    gathered = take(4 if first else 2)
+    vj, vu, vd, qs, qb, kvb, sc, acc, back, ab, vv, rsum, usum = take(13)
+    wsem, osem, qsend, qrecv, xsend, xrecv, csend, crecv, ysend, yrecv, fsend, frecv = take(12)
+    bsend, brecv = take(2)
+    flat, own_small = take(2)
     me = my_place()
+    if first:
+        shards.append(own_small)
+    lands = [vu, vd, vj, gathered[3], vv] if first else [vu, vd]
+    plan = Gather(me, FIRST_PIECES if first else SECOND_PIECES, shards, lands, refs)
+    feed, joint, later, small = (0, 1, 2), (3, 4), (5, 6), (7,)
     x, c = me["x"], me["c"]
     yh = me["y"] // 2
     k = yh * 2 + c
@@ -490,13 +609,61 @@
     k_partner = yh * 2 + 1 - c
     k_across = (1 - yh) * 2 + c
     k_diag = (1 - yh) * 2 + 1 - c
-    loads = [
-        pltpu.make_async_copy(a, b, wsem.at[i])
-        for i, (a, b) in enumerate(((wj, vj), (wu, vu), (wd, vd)))
-    ]
-    for copy in loads:
+    greet_all(me)
+    loads = []
+
+    def load(src, dst):
+        copy = pltpu.make_async_copy(src, dst, wsem.at[len(loads)])
         copy.start()
-    greet_sequence(me)
+        loads.append(copy)
+
+    if first:
+        flat[...] = jnp.zeros_like(flat)
+        for j in range(9):
+            for l in range(2):
+                flat[16 * l + j : 16 * l + j + 1, 0 : small_in[j].shape[1]] = small_in[j][
+                    l : l + 1, :
+                ].astype(F32)
+        owner = lax.axis_index("batch") * 4 + lax.axis_index("blk")
+        lines = lax.broadcasted_iota(jnp.int32, (32, 256), 0) % 16
+        moved = pltpu.roll(flat[...], (owner * 24) % 128, axis=1)
+        moved_up = pltpu.roll(flat[...], (owner * 96) % 128, axis=1)
+        own_small[...] = jnp.where(lines == 8, moved_up, moved).astype(BF)
+        for i in small + joint + feed:
+            plan.start(i, 0)
+        plan.relay_all(0, *small, *joint)
+        plan.close_all(0, *small, *joint)
+        plan.relay_all(0, *feed)
+        plan.relay_all(1, *small, *joint)
+        plan.close_all(0, *feed)
+        plan.close_all(1, *small, *joint)
+        for i in small + joint:
+            plan.complete(i)
+        load(vj, gathered[2])
+        rsum[...] = jnp.zeros_like(rsum)
+        usum[...] = jnp.zeros_like(usum)
+        for o in range(32):
+            z, yl, yh, core = o // 8, (o // 4) % 2, (o // 2) % 2, o % 2
+            at, up_at = (24 * o) // 128 * 128, (96 * o) // 128 * 128
+            for l in range(2):
+                part = vv[z, yl, yh, core, 16 * l : 16 * l + 16, :].astype(F32)
+                rsum[l, :, at : at + 256] += part[0:8]
+                usum[l, 0:1, up_at : up_at + 256] += part[8:9]
+        for l in range(2):
+            rows_out[l] = rsum[l, :, 0:768]
+            add_out[l] = usum[l, :, 0:3072]
+        rows, up_add = rows_out.at[0], add_out.at[0]
+    else:
+        load(wj, vj)
+        for i in feed:
+            plan.start(i, 0)
+        plan.relay_all(0, 0)
+        plan.close_all(0, 0)
+        rows, up_add = rows.at[1], up_add.at[1]
+
+    def joint_columns(start):
+        return vj[:, :, :, :, :, start : start + 768].reshape(768, 768)
+
     sends = []
 
     def send(src, dst, s, r, place):
@@ -507,9 +674,10 @@
     def arrived(slot, s, r, place):
         remote(slot, slot, s, r, place).wait_recv()
 
-    loads[0].wait()
+    if not first:
+        loads[0].wait()
     for j in (1, 2, 0):
-        p = mxu(hid[...], vj[:, 768 * j : 768 * j + 768])
+        p = mxu(hid[...], joint_columns(768 * j))
         if j == 0:
             p = p + rows[0:1]
         if j == 2:
@@ -533,12 +701,25 @@
     for s in (2, 1, 3):
         peer = peer_of(me, "x", s)
         send(qs.at[peer["x"], 0:192], qb.at[x], qsend.at[s - 1], qrecv.at[s - 1], peer)
+    if first:
+        plan.relay_all(1, 0)
+        plan.close_all(1, 0)
+        for i in later:
+            plan.start(i, 0)
+    else:
+        plan.relay_all(1, 0)
+        plan.relay_all(0, 1, 2)
+        plan.close_all(1, 0)
+        plan.close_all(0, 1, 2)
     for s in (1, 3, 2):
         source = peer_of(me, "x", 4 - s)
         slot = kvb.at[k, source["x"]]
         arrived(slot, xsend.at[s - 1], xrecv.at[s - 1], source)
         send(slot, slot, ysend.at[s], yrecv.at[s], across)
         send(slot, slot, csend.at[s], crecv.at[s], partner)
+    if first:
+        plan.relay_all(1, 1, 2)
+        plan.relay_all(0, *later)
     for s in (1, 3, 2):
         source = peer_of(me, "x", 4 - s)
         arrived(qb.at[source["x"]], qsend.at[s - 1], qrecv.at[s - 1], source)
@@ -597,6 +778,13 @@
         return list(zip(peaks, totals))
 
     state = half(k, k_partner, None)
+    if first:
+        plan.close_all(0, *later)
+        plan.close_all(1, 1, 2)
+        plan.relay_all(2, 0)
+    else:
+        plan.relay_all(1, 1, 2)
+        plan.relay_all(2, 0)
     for s in (0, 1, 3, 2):
         slot = kvb.at[k_across, (x + 4 - s) % 4]
         arrived(slot, ysend.at[s], yrecv.at[s], across)
@@ -619,40 +807,58 @@
         peer = peer_of(me, "x", s)
         send(back.at[peer["x"]], ab.at[x], bsend.at[s - 1], brecv.at[s - 1], peer)
     q_out[...] = qb[...]
-    loads[1].wait()
-    loads[2].wait()
+    if first:
+        plan.relay_all(1, *later)
+    else:
+        plan.close_all(1, 1, 2)
+    plan.close_all(2, 0)
+    for i in feed:
+        plan.complete(i)
+    load(vu, gathered[0])
+    load(vd, gathered[1])
     for s in (1, 3, 2):
         source = peer_of(me, "x", 4 - s)
         arrived(ab.at[source["x"]], bsend.at[s - 1], brecv.at[s - 1], source)
     mixed = ab[...].reshape(768, 128).astype(F32).T.astype(BF)
     mixed_out[...] = mixed
-    before = hid[...].astype(F32) + (mxu(mixed, vj[:, 2304:3072]) + rows[2:3])
+    before = hid[...].astype(F32) + (mxu(mixed, joint_columns(2304)) + rows[2:3])
     before1_out[...] = before
-    first = normalized(before)[0] * rows[3:4] + rows[4:5]
-    low = first.astype(BF)
+    first_norm = normalized(before)[0] * rows[3:4] + rows[4:5]
+    low = first_norm.astype(BF)
     low_out[...] = low
-    second = first + rows[5:6]
+    second = first_norm + rows[5:6]
     for q in range(4):
         at = slice(768 * q, 768 * q + 768)
-        u = mxu(low, vu[:, at]) + up_add[:, at]
+        u = mxu(low, vu[:, :, :, :, :, at].reshape(768, 768)) + up_add[0:1, at]
         up_out[:, at] = u
         a = (u * normal_cdf(u)).astype(BF)
         act_out[:, at] = a
-        second = second + mxu(a, vd[at, :])
+        second = second + mxu(a, vd[q].reshape(768, 768))
     before2_out[...] = second
     res[...] = (normalized(second)[0] * rows[6:7] + rows[7:8]).astype(BF)
     keep.wait()
+    if first:
+        plan.close_all(1, *later)
+        for i in later:
+            plan.complete(i)
+    plan.end()
+    for copy in loads[0 if first else 1 :]:
+        copy.wait()
     for copy in sends:
         copy.wait_send()
 
 
-def forward_layer(hidden, rows, up_add, lengths, wj, wu, wd):
+def forward_layer(first, hidden, lengths, known, shards):
     vmem = pl.BlockSpec(memory_space=pltpu.VMEM)
     anyspace = pl.BlockSpec(memory_space=pl.ANY)
     dma = pltpu.SemaphoreType.DMA
     out = jax.ShapeDtypeStruct
+    n = len(FIRST_PIECES if first else SECOND_PIECES)
+    got = [(24, 3072), (96, 768)]
+    if first:
+        got += [(24, 3072), (24, 3072)]
     return pl.pallas_call(
-        forward_kernel,
+        functools.partial(forward_kernel, first),
         out_shape=[
             out((128, 768), BF),
             out((4, 192, 128), BF),
@@ -665,13 +871,19 @@
             out((128, 3072), F32),
             out((128, 3072), BF),
             out((128, 768), F32),
-        ],
-        in_specs=[vmem, vmem, vmem, pl.BlockSpec(memory_space=pltpu.SMEM)] + [anyspace] * 3,
-        out_specs=[vmem, vmem, anyspace] + [vmem] * 8,
+        ]
+        + ([out((2, 8, 768), F32), out((2, 8, 3072), F32)] if first else [])
+        + [out((4, 2, 2, 2, *s), BF) for s in got],
+        in_specs=[vmem, pl.BlockSpec(memory_space=pltpu.SMEM)]
+        + ([vmem] * 9 if first else [vmem, vmem, anyspace])
+        + [anyspace] * len(shards),
+        out_specs=[vmem, vmem, anyspace]
+        + [vmem] * (10 if first else 8)
+        + [anyspace] * len(got),
         scratch_shapes=[
-            pltpu.VMEM((768, 3072), BF),
-            pltpu.VMEM((768, 3072), BF),
-            pltpu.VMEM((3072, 768), BF),
+            pltpu.VMEM((4, 2, 2, 2, 24, 3072), BF),
+            pltpu.VMEM((4, 2, 2, 2, 24, 3072), BF),
+            pltpu.VMEM((4, 2, 2, 2, 96, 768), BF),
             pltpu.VMEM((4, 576, 128), BF),
             pltpu.VMEM((4, 192, 128), BF),
             pltpu.VMEM((4, 4, 384, 128), BF),
@@ -679,7 +891,10 @@
             pltpu.VMEM((3, 64, 512), F32),
             pltpu.VMEM((4, 192, 128), BF),
             pltpu.VMEM((4, 192, 128), BF),
-            dma((3,)),
+            pltpu.VMEM((4, 2, 2, 2, 32, 256), BF),
+            pltpu.VMEM((2, 8, 896), F32),
+            pltpu.VMEM((2, 8, 3200), F32),
+            dma((4,)),
             dma,
             dma((3,)),
             dma((3,)),
@@ -693,27 +908,39 @@
             dma((4,)),
             dma((3,)),
             dma((3,)),
+            pltpu.VMEM((32, 256), F32),
+            pltpu.VMEM((32, 256), BF),
+            dma((n, 3, 4)),
+            dma((n, 3, 4)),
+            dma((n, 4, 3)),
+            dma((n, 4, 3)),
+            dma((n,)),
         ],
         compiler_params=pltpu.CompilerParams(
-            collective_id=2, has_side_effects=True, vmem_limit_bytes=60 * 1024 * 1024
+            collective_id=2 if first else 0,
+            has_side_effects=True,
+            vmem_limit_bytes=60 * 1024 * 1024,
         ),
-        name="forward_layer",
-    )(hidden, rows, up_add, lengths, wj, wu, wd)
-
-
-def backward_kernel(*refs):
+        name="forward_first" if first else "forward_second",
+    )(hidden, lengths, *known, *shards)
+
+
+def backward_kernel(layer, *refs):
     dy, rows, up, before2, before1, qb, kvb, logs, att, lens, wj, wu, wd = refs[:13]
     dh_out, dj_out, db_out, du_out, df_out, vec_out = refs[13:19]
     vj, vu, vd, das, dab, dkv, rx, ry, rl, py, dq, sb, dj = refs[19:32]
     wsem, asend, arecv, csend, crecv, jsend, jrecv = refs[32:]
+    rows = rows.at[layer]
     me = my_place()
     x, c = me["x"], me["c"]
     yh = me["y"] // 2
     partner, across = peer_of(me, "c", 1), peer_of(me, "y", 2)
-    loads = [
-        pltpu.make_async_copy(a, b, wsem.at[i])
-        for i, (a, b) in enumerate(((wd, vd), (wu, vu), (wj, vj)))
-    ]
+    loads = []
+    for q in range(4):
+        at = slice(768 * q, 768 * q + 768)
+        for a, b in ((wd.at[at], vd.at[at]), (wu.at[:, at], vu.at[:, at])):
+            loads.append(pltpu.make_async_copy(a, b, wsem.at[len(loads)]))
+    loads.append(pltpu.make_async_copy(wj, vj, wsem.at[8]))
     for copy in loads:
         copy.start()
     greet_sequence(me)
@@ -737,10 +964,10 @@
     df = d_second.astype(BF)
     df_out[...] = df
     vec_out[5:6] = column_sum(df)
-    loads[0].wait()
-    loads[1].wait()
     d_first = d_second
     for q in range(4):
+        loads[2 * q].wait()
+        loads[2 * q + 1].wait()
         at = slice(768 * q, 768 * q + 768)
         u = up[:, at]
         slope = normal_cdf(u) + u * (0.3989422804014327 * jnp.exp(-0.5 * u * u))
@@ -755,7 +982,7 @@
     db_out[...] = db
     vec_out[2:3] = column_sum(db)
     dh_out[...] = d_sum
-    loads[2].wait()
+    loads[8].wait()
     da = mxu(db, vj[:, 2304:3072], FAR).T.astype(BF)
     for g in range(4):
         das[g] = da[192 * g : 192 * g + 192]
@@ -848,13 +1075,13 @@
         copy.wait_send()
 
 
-def backward_layer(dy, rows, up, before2, before1, q, kv, logs, att, lengths, wj, wu, wd):
+def backward_layer(layer, dy, rows, up, before2, before1, q, kv, logs, att, lengths, wj, wu, wd):
     vmem = pl.BlockSpec(memory_space=pltpu.VMEM)
     anyspace = pl.BlockSpec(memory_space=pl.ANY)
     dma = pltpu.SemaphoreType.DMA
     out = jax.ShapeDtypeStruct
     return pl.pallas_call(
-        backward_kernel,
+        functools.partial(backward_kernel, layer),
         out_shape=[
             out((128, 768), F32),
             out((128, 2304), BF),
@@ -879,7 +1106,7 @@
             pltpu.VMEM((3, 64, 512), F32),
             pltpu.VMEM((4, 576, 128), BF),
             pltpu.VMEM((4, 576, 128), BF),
-            dma((3,)),
+            dma((9,)),
             dma((3,)),
             dma((3,)),
             dma((3,)),
@@ -888,7 +1115,7 @@
             dma((3,)),
         ],
         compiler_params=pltpu.CompilerParams(
-            collective_id=3, has_side_effects=True, vmem_limit_bytes=60 * 1024 * 1024
+            collective_id=3 + layer, has_side_effects=True, vmem_limit_bytes=60 * 1024 * 1024
         ),
         name="backward_layer",
     )(dy, rows, up, before2, before1, q, kv, logs, att, lengths, wj, wu, wd)
@@ -912,53 +1139,44 @@
     second_shift,
     cotangent,
 ):
-    vectors = jnp.stack(
-        (
-            query_bias,
-            value_bias,
-            output_bias,
-            first_gain,
-            first_shift,
-            down_bias,
-            second_gain,
-            second_shift,
-        ),
-        axis=1,
+    small = (
+        query_bias,
+        value_bias,
+        output_bias,
+        first_gain,
+        first_shift,
+        down_bias,
+        second_gain,
+        second_shift,
+        up_bias,
     )
-    vectors = jnp.concatenate([vectors, up_bias.reshape(LAYERS, 4, 24)], axis=1)
-    vectors = jnp.pad(vectors.reshape(24, 24), ((0, 8), (0, 104)))
     joint_and_out = jnp.concatenate([joint_weight, output_weight], axis=-1)
-    pieces = []
-    for layer_index in range(LAYERS):
-        pieces += [up_weight[layer_index], down_weight[layer_index], joint_and_out[layer_index]]
-    *gathered, vectors_all = gather_weights((*pieces, vectors))
-    vectors_all = vectors_all.reshape(32, 32, 128)[:, :24, :24].reshape(32, LAYERS, 12, 24)
-    rows_all = vectors_all[:, :, :8].transpose(1, 2, 0, 3).reshape(LAYERS, 8, 768)
-    up_adds = vectors_all[:, :, 8:].transpose(1, 0, 2, 3).reshape(LAYERS, 3072)
-    weights_of = []
-    for layer_index in range(LAYERS):
-        up_full, down_full, joint_out = gathered[3 * layer_index : 3 * layer_index + 3]
-        weights_of.append(
-            (joint_out.reshape(768, 3072), up_full.reshape(768, 3072), down_full.reshape(3072, 768))
-        )
-    rows_all = rows_all.astype(F32)
-    up_adds = up_adds.astype(F32)
-    hidden = inputs.reshape(128, 768)
-    kept, outputs = [], []
-    for l in range(LAYERS):
-        result = forward_layer(
-            hidden, rows_all[l], up_adds[l : l + 1], lengths, *weights_of[l]
-        )
-        kept.append((hidden, *result[1:]))
-        hidden = result[0]
-        outputs.append(hidden.reshape(1, 128, 768))
+    hidden0 = inputs.reshape(128, 768)
+    got = forward_layer(
+        True,
+        hidden0,
+        lengths,
+        small,
+        (up_weight, down_weight, joint_and_out),
+    )
+    rows_all, up_adds, up0, down0, joint0, joint1 = got[11:]
+    more = forward_layer(
+        False, got[0], lengths, (rows_all, up_adds, joint1), (up_weight, down_weight)
+    )
+    up1, down1 = more[11:]
+    weights_of = [
+        (j.reshape(768, 3072), u.reshape(768, 3072), d.reshape(3072, 768))
+        for j, u, d in ((joint0, up0, down0), (joint1, up1, down1))
+    ]
+    kept = [(hidden0, *got[1:11]), (got[0], *more[1:11])]
+    outputs = [got[0].reshape(1, 128, 768), more[0].reshape(1, 128, 768)]
     grad_rows = cotangent.reshape(128, 768).astype(F32)
     layer_grads = [None] * LAYERS
     vector_grads = [None] * LAYERS
     for l in reversed(range(LAYERS)):
         hidden, q, kv, logs, att, mixed, before1, low, up, acts, before2 = kept[l]
         grad_rows, d_joint, d_branch, d_up, d_down, vector_grads[l] = backward_layer(
-            grad_rows, rows_all[l], up, before2, before1, q, kv, logs, att, lengths, *weights_of[l]
+            l, grad_rows, rows_all, up, before2, before1, q, kv, logs, att, lengths, *weights_of[l]
         )
         layer_grads[l] = (hidden, mixed, low, acts, d_joint, d_branch, d_up, d_down)
     vectors = jnp.concatenate(vector_grads)

time: 410 us -> 339 us (0.83)
  Pallas kernels: 375 us -> 320 us
  local copies, waits for them, and re-layouts: 26.4 us -> 10.9 us
    pallas_call x5 -> x4, Pallas kernels: 282 us -> 240 us  [the longest x2 135 us: forward_layer(): pl.pallas_call(functools.partial(forward_kernel, first), out_shape=[out((...]
    pallas_call x1, Pallas kernels: 92.8 us -> 80.3 us  [reduce_grads(): pl.pallas_call(reduce_kernel, out_shape=[jax.ShapeDtypeStruct((2, 24, 230...]
    another operation x8 -> x0, local copies, waits for them, and re-layouts: 5.26 us -> none  [body(): jnp.stack((query_bias, value_bias, output_bias, first_gain, first_shift,...]
    squeeze x4 -> x0, local copies, waits for them, and re-layouts: 4.97 us -> none  [the longest x1 1.8 us: body(): joint_and_out[layer_index]]
where the time goes in v3:
time: 339 us
  Pallas kernels  320 us (94%)
  local copies, waits for them, and re-layouts  10.9 us (3%)
  other arithmetic  6.41 us (2%)
    pallas_call x2, Pallas kernels, forward_layer(): pl.pallas_call(functools.partial(forward_kernel, first), out_shape=[out((...  135 us
    pallas_call x2, Pallas kernels, backward_layer(): pl.pallas_call(functools.partial(backward_kernel, layer), out_shape=[out(...  104 us
    pallas_call x1, Pallas kernels, reduce_grads(): pl.pallas_call(reduce_kernel, out_shape=[jax.ShapeDtypeStruct((2, 24, 230...  80.3 us

profile of v3, /device:TPU:0, one launch (start us, length us, event | category | flops | bytes accessed | tf_op | source)
XLA Modules:
  0.0 338.7 jit_solution(12435041818704511079)
XLA Ops:
  1.3 1.7 pad_maximum_fusion.3.refs_13_
  3.0 82.4 %forward_first.1 = (bf16[128,768]{1,0:T(8,128)(2,1)}, bf16[4,192,128]{2,1,0:T(8,128)(2,1)}, bf16[4,4,384,128]{3,2,1,0:T(8,128)(2,1)}, f32[8,512]{1,0:T(8,128)}, ...) custom-call(bf16[128,768]{1,0:T(8,128)(2,1)} %bitcast.100, ...), custom_call_target="tpu_custom_call" | custom-call | tf_op jit(solution)/shard_map/forward_first/pallas_call | solution.py:860
  85.4 53.1 %forward_second.1 = (bf16[128,768]{1,0:T(8,128)(2,1)}, bf16[4,192,128]{2,1,0:T(8,128)(2,1)}, bf16[4,4,384,128]{3,2,1,0:T(8,128)(2,1)}, f32[8,512]{1,0:T(8,128)},...) custom-call(bf16[128,768]{1,0:T(8,128)(2,1)} %get-tuple-element.62.r, ...), custom_call_target="tpu_custom_call" | custom-call | tf_op jit(solution)/shard_map/forward_second/pallas_call | solution.py:860
  138.5 0.8 bitcast_convert_fusion.refs_0_
  139.3 52.6 %backward_layer.2 = (f32[128,768]{1,0:T(8,128)}, bf16[128,2304]{1,0:T(8,128)(2,1)}, bf16[128,768]{1,0:T(8,128)(2,1)}, bf16[128,3072]{1,0:T(8,128)(2,1)}, bf16[128,768]{1,0:T(8,128)(2,1)}, /*index=5*/f32[16,768]{1,0:T(8,128)}) custom-call(f32[128,768]{1,0:T(8,128)} %bitcast_convert_fusion.refs_0_, f32[2,8,768]{2,1,0:T(8,128)} %get-tuple-element.63.refs_2_.refs_1_, ...), custom_call_target="tpu_custom_call" | custom-call | tf_op jit(solution)/shard_map/backward_layer/pallas_call | solution.py:1083
  191.9 51.5 %backward_layer.3 = (f32[128,768]{1,0:T(8,128)}, bf16[128,2304]{1,0:T(8,128)(2,1)}, bf16[128,768]{1,0:T(8,128)(2,1)}, bf16[128,3072]{1,0:T(8,128)(2,1)}, bf16[128,768]{1,0:T(8,128)(2,1)}, /*index=5*/f32[16,768]{1,0:T(8,128)}) custom-call(f32[128,768]{1,0:T(8,128)} %get-tuple-element.76.refs_0_, f32[2,8,768]{2,1,0:T(8,128)} %get-tuple-element.63.refs_2_.refs_1_, ...), custom_call_target="tpu_custom_call" | custom-call | tf_op jit(solution)/shard_map/backward_layer/pallas_call | solution.py:1083
  243.4 1.5 pad_maximum_fusion.4.refs_10_
  244.9 0.4 copy.50
  245.6 0.2 copy.54
  246.1 0.4 copy.42
  246.5 1.1 copy.40
  247.7 0.2 copy.46
  248.1 1.6 pad_maximum_fusion
  249.7 80.3 %reduce_grads.1 = (f32[2,24,2304]{2,1,0:T(8,128)}, f32[2,24,768]{2,1,0:T(8,128)}, f32[2,24,3072]{2,1,0:T(8,128)}, f32[2,96,768]{2,1,0:T(8,128)}, f32[32,768]{1,0:T(8,128)}) custom-call(bf16[2,2688,128]{2,1,0:T(8,128)(2,1)} %get-tuple-element.117.refs_0_, bf16[128,3072]{1,0:T(8,128)(2,1)} %get-tuple-element.91.refs_1_, ...), custom_call_target="tpu_custom_call" | custom-call | tf_op jit(solution)/shard_map/reduce_grads/pallas_call | solution.py:481
  330.0 0.9 slice.40
  330.9 0.7 constant_dynamic-slice_fusion.8
  331.6 0.8 slice_bitcast_fusion
  332.4 0.6 constant_dynamic-slice_fusion.7
  333.0 0.8 pad_maximum_fusion.2
  333.8 0.7 copy.74
  334.6 1.8 copy.75
  336.4 0.7 copy.76
  337.0 0.8 copy.77
  337.9 0.8 copy.78
  (40 shorter events, 0.9 us)
Async XLA Ops:
  85.4 53.1 %copy-start.10 = (bf16[1,128,768]{2,1,0:T(8,128)(2,1)S(1)}, bf16[1,128,768]{2,1,0:T(8,128)(2,1)}, u32[]{:S(2)}) copy-start(bf16[1,128,768]{2,1,0:T(8,128)(2,1)} %param.31) | copy-start | bytes 589828
  191.9 51.5 %copy-start.13 = (f32[16,768]{1,0:T(8,128)S(1)}, f32[16,768]{1,0:T(8,128)}, u32[]{:S(2)}) copy-start(f32[16,768]{1,0:T(8,128)} %get-tuple-element.103) | copy-start | bytes 147460
  191.9 53.0 %copy-start.3 = (bf16[128,3072]{1,0:T(8,128)(2,1)S(1)}, bf16[128,3072]{1,0:T(8,128)(2,1)}, u32[]{:S(2)}) copy-start(bf16[128,3072]{1,0:T(8,128)(2,1)} %get-tuple-element.96) | copy-start | bytes 2359300
  243.4 2.0 copy-start.9
  243.4 2.2 copy-start.8
  243.4 2.4 copy-start
  244.9 1.1 copy-start.2
  245.6 2.0 copy-start.7
  245.8 2.0 copy-start.1
  249.7 83.3 %copy-start.11 = (bf16[128,768]{1,0:T(8,128)(2,1)S(1)}, bf16[128,768]{1,0:T(8,128)(2,1)}, u32[]{:S(2)}) copy-start(bf16[128,768]{1,0:T(8,128)(2,1)} %get-tuple-element.66) | copy-start | bytes 589828
  249.7 84.1 %copy-start.6 = (f32[128,768]{1,0:T(8,128)S(1)}, f32[128,768]{1,0:T(8,128)}, u32[]{:S(2)}) copy-start(f32[128,768]{1,0:T(8,128)} %get-tuple-element.87) | copy-start | bytes 1179652
  330.0 6.4 %copy-start.12 = (f32[2,24,768]{2,1,0:T(8,128)S(1)}, f32[2,24,768]{2,1,0:T(8,128)}, u32[]{:S(2)}) copy-start(f32[2,24,768]{2,1,0:T(8,128)} %get-tuple-element.139) | copy-start | bytes 442372
  330.0 7.1 %copy-start.5 = (f32[2,24,3072]{2,1,0:T(8,128)S(1)}, f32[2,24,3072]{2,1,0:T(8,128)}, u32[]{:S(2)}) copy-start(f32[2,24,3072]{2,1,0:T(8,128)} %get-tuple-element.143) | copy-start | bytes 1769476
  330.0 7.9 %copy-start.4 = (f32[2,96,768]{2,1,0:T(8,128)S(1)}, f32[2,96,768]{2,1,0:T(8,128)}, u32[]{:S(2)}) copy-start(f32[2,96,768]{2,1,0:T(8,128)} %get-tuple-element.145) | copy-start | bytes 1769476

commit v4 on v3

--- a/solution.py
+++ b/solution.py
@@ -214,45 +214,164 @@
 THIRDS = (("x", "y", "z"), ("y", "z", "x"), ("z", "x", "y"))
 
 
+class Reducer:
+    low_half, high_half = pl.ds(0, 2), pl.ds(2, 2)
+
+    def __init__(self, me, ins, bufs, s2, sems):
+        self.me, self.ins, self.s2 = me, ins, s2
+        self.lhs, self.rhs, self.g, self.o1, self.r1, self.s1, self.o2, self.r2 = bufs
+        self.csend, self.crecv, self.lsem, self.qs, self.qr = sems
+        self.sends = []
+
+    def exchange(self):
+        me, c = self.me, self.me["c"]
+        partner = peer_of(me, "c", 1)
+        half = pl.ds(pl.multiple_of(c * 128, 128), 128)
+        lhs_in, rhs_in = self.ins[0], self.ins[1:]
+        dst = self.lhs.at[ALL, half]
+        self.away = [remote(lhs_in.at[1 - c], dst, self.csend.at[0], self.crecv.at[0], partner)]
+        self.here = [pltpu.make_async_copy(lhs_in.at[c], dst, self.lsem.at[0])]
+        starts, widths = (0, 3072, 3840, 6144), (3072, 768, 2304, 768)
+        for j in range(4):
+            dst = self.rhs.at[half, pl.ds(starts[j], widths[j])]
+            self.away.append(
+                remote(rhs_in[j], dst, self.csend.at[j + 1], self.crecv.at[j + 1], partner)
+            )
+            self.here.append(pltpu.make_async_copy(rhs_in[j], dst, self.lsem.at[j + 1]))
+        for copy in self.away + self.here:
+            copy.start()
+
+    def exchanged(self):
+        for copy in self.here:
+            copy.wait()
+        for copy in self.away:
+            copy.wait_recv()
+
+    def products(self, t):
+        for q in range(4):
+            unit = (0, 1 + q, 5 if q < 3 else 6)[t]
+            col = (q * 768, 3072, 3840 + q * 768)[t]
+            block = jnp.dot(
+                self.lhs[384 * unit : 384 * unit + 384, :],
+                self.rhs[:, col : col + 768],
+                preferred_element_type=jnp.float32,
+            )
+            for i in range(16):
+                z, y = i // 4, (i % 2) * 2 + (i // 2) % 2
+                at = ((q, y, z), (y, z, q), (z, q, y))[t]
+                part = block[24 * i : 24 * i + 24]
+                self.g[t, at[0], at[1], at[2]] = part.astype(jnp.bfloat16)
+        self.start(0, t)
+
+    def copy(self, phase, t, j, src, dst, peer):
+        copy = remote(src, dst, self.qs.at[phase, t, j], self.qr.at[phase, t, j], peer)
+        copy.start()
+        self.sends.append(copy)
+
+    def wait(self, phase, t, j, slot, peer):
+        remote(slot, slot, self.qs.at[phase, t, j], self.qr.at[phase, t, j], peer).wait_recv()
+
+    def refs(self, phase, t):
+        axis = THIRDS[t][phase]
+        places = [peer_of(self.me, axis, s) for s in (1, 3, 2)]
+        held, over, got = (
+            (self.g, self.o1, self.r1),
+            (self.s1, self.o2, self.r2),
+        )[phase]
+        return axis, places, held.at[t], over.at[t], got.at[t]
+
+    def start(self, phase, t):
+        axis, (right, left, far), held, over, got = self.refs(phase, t)
+        low, high = self.low_half, self.high_half
+        self.copy(phase, t, 0, held.at[far[axis], low], over.at[0], right)
+        self.copy(phase, t, 1, held.at[far[axis], high], over.at[1], left)
+        self.copy(phase, t, 2, held.at[right[axis], high], got.at[0, high], right)
+        self.copy(phase, t, 3, held.at[left[axis], low], got.at[1, low], left)
+
+    def middle(self, phase, t):
+        axis, (right, left, far), held, over, got = self.refs(phase, t)
+        f32 = jnp.float32
+        for j, source, target in ((0, left, right), (1, right, left)):
+            self.wait(phase, t, j, over.at[j], source)
+            at = target[axis]
+            for a in range(2):
+                if phase == 0:
+
+                    def merge(b, carry, a=a, j=j, at=at):
+                        total = held[at, 2 * j + a, b].astype(f32) + over[j, a, b].astype(f32)
+                        held[at, 2 * j + a, b] = total.astype(jnp.bfloat16)
+                        return carry
+
+                    lax.fori_loop(0, 4, merge, 0)
+                else:
+                    total = held[at, 2 * j + a].astype(f32) + over[j, a].astype(f32)
+                    held[at, 2 * j + a] = total.astype(jnp.bfloat16)
+            part = (self.low_half, self.high_half)[j]
+            self.copy(phase, t, 4 + j, held.at[at, part], got.at[j, part], target)
+
+    def finish(self, phase, t):
+        axis, (right, left, far), held, over, got = self.refs(phase, t)
+        low, high = self.low_half, self.high_half
+        self.wait(phase, t, 2, got.at[0, high], left)
+        self.wait(phase, t, 3, got.at[1, low], right)
+        self.wait(phase, t, 4, got.at[0, low], left)
+        self.wait(phase, t, 5, got.at[1, high], right)
+        mine = self.me[axis]
+        f32 = jnp.float32
+        if phase == 0:
+
+            def add(i, carry):
+                a, b = i // 4, i % 4
+                total = held[mine, a, b].astype(f32)
+                for s in range(2):
+                    total = total + got[s, a, b].astype(f32)
+                self.s1[t, a, b] = total.astype(jnp.bfloat16)
+                return carry
+
+            lax.fori_loop(0, 16, add, 0)
+            self.start(1, t)
+        else:
+            for a in range(4):
+                total = held[mine, a].astype(f32)
+                for s in range(2):
+                    total = total + got[s, a].astype(f32)
+                self.s2[t, a] = total.astype(jnp.bfloat16)
+
+    def end(self):
+        for copy in self.sends + self.away:
+            copy.wait_send()
+
+
+def reducer_buffers():
+    bf = jnp.bfloat16
+    return [
+        pltpu.VMEM((2688, 256), bf),
+        pltpu.VMEM((256, 6912), bf),
+        pltpu.VMEM((3, 4, 4, 4, 24, 768), bf),
+        pltpu.VMEM((3, 2, 2, 4, 24, 768), bf),
+        pltpu.VMEM((3, 2, 4, 4, 24, 768), bf),
+        pltpu.VMEM((3, 4, 4, 24, 768), bf),
+        pltpu.VMEM((3, 2, 2, 24, 768), bf),
+        pltpu.VMEM((3, 2, 4, 24, 768), bf),
+    ]
+
+
+def reducer_semaphores():
+    dma = pltpu.SemaphoreType.DMA
+    return [dma((5,)), dma((5,)), dma((5,)), dma((2, 3, 6)), dma((2, 3, 6))]
+
+
 def reduce_kernel(*refs):
-    ins = refs[:11]
-    joint_out, out_out, up_out, down_out, vec_out = refs[11:16]
-    lhs, rhs, g, o1, r1, s1, o2, r2, s2, r3, last, vc, va = refs[16:29]
-    csend, crecv, lsem, ps, pr, qs, qr, vs, vr = refs[29:]
-    vec_in = ins[10]
+    s2_in, vec_in = refs[5:7]
+    joint_out, out_out, up_out, down_out, vec_out = refs[7:12]
+    s2, r3, last, vc, va = refs[20:25]
+    ps, pr, vs, vr = refs[30:]
     me = my_place()
-    partner = peer_of(me, "c", 1)
-    c = me["c"]
+    layers = (1, 0)
+    f32 = jnp.float32
+    reducer = Reducer(me, refs[:5], refs[12:20], s2.at[0], refs[25:30])
     greet_all(me)
-    half = pl.ds(pl.multiple_of(c * 128, 128), 128)
-    other_half = pl.ds(pl.multiple_of((1 - c) * 128, 128), 128)
-    starts = (0, 3072, 3840, 6144)
-    widths = (3072, 768, 2304, 768)
-    layers = (1, 0)
-
-    def exchanges(l):
-        lhs_in, rhs_in = ins[5 * l], ins[5 * l + 1 : 5 * l + 5]
-        away = [
-            remote(
-                lhs_in.at[1 - c],
-                lhs.at[l, ALL, half],
-                csend.at[l, 0],
-                crecv.at[l, 0],
-                partner,
-            )
-        ]
-        here = [pltpu.make_async_copy(lhs_in.at[c], lhs.at[l, ALL, half], lsem.at[l, 0])]
-        for j in range(4):
-            dst = rhs.at[l, half, pl.ds(starts[j], widths[j])]
-            away.append(remote(rhs_in[j], dst, csend.at[l, j + 1], crecv.at[l, j + 1], partner))
-            here.append(pltpu.make_async_copy(rhs_in[j], dst, lsem.at[l, j + 1]))
-        return away, here
-
-    exchanged = {}
-    for l in layers:
-        exchanged[l] = exchanges(l)
-        for copy in exchanged[l][0] + exchanged[l][1]:
-            copy.start()
+    reducer.exchange()
 
     vec_axes = ("c", "x", "y", "z")
     vec_sends = []
@@ -317,122 +436,32 @@
                 peer_of(me, axis, s),
             ).wait_recv()
 
-    def ring_copy(phase, t, l, j, src, dst, peer):
-        copy = remote(src, dst, qs.at[phase, t, l, j], qr.at[phase, t, l, j], peer)
-        copy.start()
-        sends.append(copy)
-
-    def ring_wait(phase, t, l, j, slot, peer):
-        remote(slot, slot, qs.at[phase, t, l, j], qr.at[phase, t, l, j], peer).wait_recv()
-
-    def ring_refs(phase, t, l):
-        axis = THIRDS[t][phase]
-        places = [peer_of(me, axis, s) for s in (1, 3, 2)]
-        held, over, got = ((g, o1, r1), (s1, o2, r2))[phase]
-        return axis, places, held.at[t, l], over.at[t, l], got.at[t, l]
-
-    low_half, high_half = pl.ds(0, 2), pl.ds(2, 2)
-
-    def ring_start(phase, t, l):
-        axis, (right, left, far), held, over, got = ring_refs(phase, t, l)
-        ring_copy(phase, t, l, 0, held.at[far[axis], low_half], over.at[0], right)
-        ring_copy(phase, t, l, 1, held.at[far[axis], high_half], over.at[1], left)
-        ring_copy(
-            phase, t, l, 2, held.at[right[axis], high_half], got.at[0, high_half], right
-        )
-        ring_copy(phase, t, l, 3, held.at[left[axis], low_half], got.at[1, low_half], left)
-
-    def ring_middle(phase, t, l):
-        axis, (right, left, far), held, over, got = ring_refs(phase, t, l)
-        for j, source, target in ((0, left, right), (1, right, left)):
-            ring_wait(phase, t, l, j, over.at[j], source)
-            for a in range(2):
-                at = target[axis]
-                if phase == 0:
-
-                    def merge(b, carry, a=a, j=j, at=at):
-                        total = held[at, 2 * j + a, b].astype(f32) + over[j, a, b].astype(f32)
-                        held[at, 2 * j + a, b] = total.astype(jnp.bfloat16)
-                        return carry
-
-                    lax.fori_loop(0, 4, merge, 0)
-                else:
-                    total = held[at, 2 * j + a].astype(f32) + over[j, a].astype(f32)
-                    held[at, 2 * j + a] = total.astype(jnp.bfloat16)
-            part = (low_half, high_half)[j]
-            ring_copy(
-                phase, t, l, 4 + j, held.at[target[axis], part], got.at[j, part], target
-            )
-
-    def ring_finish(phase, t, l):
-        axis, (right, left, far), held, over, got = ring_refs(phase, t, l)
-        ring_wait(phase, t, l, 2, got.at[0, high_half], left)
-        ring_wait(phase, t, l, 3, got.at[1, low_half], right)
-        ring_wait(phase, t, l, 4, got.at[0, low_half], left)
-        ring_wait(phase, t, l, 5, got.at[1, high_half], right)
-
-    f32 = jnp.float32
-    for l in layers:
-        away, here = exchanged[l]
-        for copy in here:
-            copy.wait()
-        for copy in away:
-            copy.wait_recv()
-        for t in range(3):
-            for q in range(4):
-                unit = (0, 1 + q, 5 if q < 3 else 6)[t]
-                col = (q * 768, 3072, 3840 + q * 768)[t]
-                block = jnp.dot(
-                    lhs[l, 384 * unit : 384 * unit + 384, :],
-                    rhs[l, :, col : col + 768],
-                    preferred_element_type=jnp.float32,
-                )
-                for i in range(16):
-                    z, y = i // 4, (i % 2) * 2 + (i // 2) % 2
-                    at = ((q, y, z), (y, z, q), (z, q, y))[t]
-                    g[t, l, at[0], at[1], at[2]] = block[24 * i : 24 * i + 24].astype(jnp.bfloat16)
-            ring_start(0, t, l)
+    def third_phase(l, t):
+        send_chunks(2, t, l, lambda a: s2.at[l, t, a], lambda s: r3.at[t, l, s - 1])
+
+    s2[1] = s2_in[...]
+    for t in range(3):
+        third_phase(1, t)
+    reducer.exchanged()
+    for t in range(3):
+        reducer.products(t)
     vec_start(1, vec_finish(0))
-    for l in layers:
-        for t in range(3):
-            ring_middle(0, t, l)
-    for l in layers:
-        for t in range(3):
-            mine = me[THIRDS[t][0]]
-            ring_finish(0, t, l)
-
-            def add1(i, carry, t=t, l=l, mine=mine):
-                a, b = i // 4, i % 4
-                total = g[t, l, mine, a, b].astype(f32)
-                for s in range(2):
-                    total = total + r1[t, l, s, a, b].astype(f32)
-                s1[t, l, a, b] = total.astype(jnp.bfloat16)
-                return carry
-
-            lax.fori_loop(0, 16, add1, 0)
-            ring_start(1, t, l)
+    for t in range(3):
+        reducer.middle(0, t)
+    for t in range(3):
+        reducer.finish(0, t)
     vec_start(2, vec_finish(1))
-    for l in layers:
-        for t in range(3):
-            ring_middle(1, t, l)
-    for l in layers:
-        for t in range(3):
-            mine = me[THIRDS[t][1]]
-            ring_finish(1, t, l)
-            for a in range(4):
-                total = s1[t, l, mine, a].astype(f32)
-                for s in range(2):
-                    total = total + r2[t, l, s, a].astype(f32)
-                s2[t, l, a] = total.astype(jnp.bfloat16)
-            send_chunks(
-                2, t, l, lambda a, t=t, l=l: s2.at[t, l, a], lambda s, t=t, l=l: r3.at[t, l, s - 1]
-            )
+    for t in range(3):
+        reducer.middle(1, t)
+    for t in range(3):
+        reducer.finish(1, t)
+        third_phase(0, t)
     vec_start(3, vec_finish(2))
     for l in layers:
         for t in range(3):
             mine = me[THIRDS[t][2]]
             await_chunks(2, t, l, lambda s, t=t, l=l: r3.at[t, l, s - 1])
-            total = s2[t, l, mine].astype(f32)
+            total = s2[l, t, mine].astype(f32)
             for s in range(3):
                 total = total + r3[t, l, s].astype(f32)
             last[t, l, me["x"]] = total.astype(jnp.bfloat16)
@@ -457,7 +486,8 @@
                     joint_out[l, :, 768 * q : 768 * q + 768] = part
                 else:
                     out_out[l] = part
-    for copy in sends + vec_sends + [a for l in layers for a in exchanged[l][0]]:
+    reducer.end()
+    for copy in sends + vec_sends:
         copy.wait_send()
 
 
@@ -468,13 +498,12 @@
     return t.reshape(2, n * 384, tokens)
 
 
-def reduce_grads(per_layer, vectors):
-    operands = []
-    for hidden, mixed, first, acts, d_joint, d_branch, d_up, d_down in per_layer:
-        operands.append(
-            jnp.concatenate([for_owner_cores(a) for a in (first, acts, hidden, mixed)], axis=1)
-        )
-        operands += [d_up, d_down, d_joint, d_branch]
+def reducer_operands(hidden, mixed, first, acts, d_joint, d_branch, d_up, d_down):
+    lhs = jnp.concatenate([for_owner_cores(a) for a in (first, acts, hidden, mixed)], axis=1)
+    return lhs, d_up, d_down, d_joint, d_branch
+
+
+def reduce_grads(operands, later, vectors):
     anyspace = pl.BlockSpec(memory_space=pl.ANY)
     vmem = pl.BlockSpec(memory_space=pltpu.VMEM)
     bf, dma = jnp.bfloat16, pltpu.SemaphoreType.DMA
@@ -487,37 +516,23 @@
             jax.ShapeDtypeStruct((2, 96, 768), jnp.float32),
             jax.ShapeDtypeStruct((32, 768), jnp.float32),
         ],
-        in_specs=[anyspace] * 10 + [vmem],
+        in_specs=[anyspace] * 5 + [vmem] * 2,
         out_specs=[vmem] * 5,
-        scratch_shapes=[
-            pltpu.VMEM((2, 2688, 256), bf),
-            pltpu.VMEM((2, 256, 6912), bf),
-            pltpu.VMEM((3, 2, 4, 4, 4, 24, 768), bf),
-            pltpu.VMEM((3, 2, 2, 2, 4, 24, 768), bf),
-            pltpu.VMEM((3, 2, 2, 4, 4, 24, 768), bf),
-            pltpu.VMEM((3, 2, 4, 4, 24, 768), bf),
-            pltpu.VMEM((3, 2, 2, 2, 24, 768), bf),
-            pltpu.VMEM((3, 2, 2, 4, 24, 768), bf),
-            pltpu.VMEM((3, 2, 4, 24, 768), bf),
+        scratch_shapes=reducer_buffers()
+        + [
+            pltpu.VMEM((2, 3, 4, 24, 768), bf),
             pltpu.VMEM((3, 2, 3, 24, 768), bf),
             pltpu.VMEM((3, 2, 4, 24, 768), bf),
             pltpu.VMEM((2, 32, 768), bf),
             pltpu.VMEM((3, 4, 32, 768), bf),
-            dma((2, 5)),
-            dma((2, 5)),
-            dma((2, 5)),
-            dma((4, 3, 2, 3)),
-            dma((4, 3, 2, 3)),
-            dma((2, 3, 2, 6)),
-            dma((2, 3, 2, 6)),
-            dma((4, 3)),
-            dma((4, 3)),
-        ],
+        ]
+        + reducer_semaphores()
+        + [dma((4, 3, 2, 3)), dma((4, 3, 2, 3)), dma((4, 3)), dma((4, 3))],
         compiler_params=pltpu.CompilerParams(
-            collective_id=1, has_side_effects=True, vmem_limit_bytes=62 * 1024 * 1024
+            collective_id=1, has_side_effects=True, vmem_limit_bytes=60 * 1024 * 1024
         ),
         name="reduce_grads",
-    )(*operands, vectors)
+    )(*operands, later, vectors)
 
 
 FAR = (((1,), (1,)), ((), ()))
@@ -926,10 +941,20 @@
 
 
 def backward_kernel(layer, *refs):
-    dy, rows, up, before2, before1, qb, kvb, logs, att, lens, wj, wu, wd = refs[:13]
-    dh_out, dj_out, db_out, du_out, df_out, vec_out = refs[13:19]
-    vj, vu, vd, das, dab, dkv, rx, ry, rl, py, dq, sb, dj = refs[19:32]
-    wsem, asend, arecv, csend, crecv, jsend, jrecv = refs[32:]
+    refs = list(refs)
+
+    def take(count):
+        out = refs[:count]
+        del refs[:count]
+        return out
+
+    beside = layer == 0
+    dy, rows, up, before2, before1, qb, kvb, logs, att, lens, wj, wu, wd = take(13)
+    operands = take(5) if beside else None
+    dh_out, dj_out, db_out, du_out, df_out, vec_out = take(6)
+    sums_out = take(1)[0] if beside else None
+    vj, vu, vd, das, dab, dkv, rx, ry, rl, py, dq, sb, dj = take(13)
+    wsem, asend, arecv, csend, crecv, jsend, jrecv = take(7)
     rows = rows.at[layer]
     me = my_place()
     x, c = me["x"], me["c"]
@@ -943,7 +968,12 @@
     loads.append(pltpu.make_async_copy(wj, vj, wsem.at[8]))
     for copy in loads:
         copy.start()
-    greet_sequence(me)
+    if beside:
+        reducer = Reducer(me, operands, refs[:8], sums_out, refs[8:])
+        greet_all(me)
+        reducer.exchange()
+    else:
+        greet_sequence(me)
     sends = []
 
     def send(src, dst, s, r, place):
@@ -990,6 +1020,10 @@
     for s in (2, 1, 3):
         peer = peer_of(me, "x", s)
         send(das.at[peer["x"]], dab.at[x], asend.at[s - 1], arecv.at[s - 1], peer)
+    if beside:
+        reducer.exchanged()
+        for third in range(3):
+            reducer.products(third)
     for s in (1, 3, 2):
         source = peer_of(me, "x", 4 - s)
         arrived(dab.at[source["x"]], asend.at[s - 1], arecv.at[s - 1], source)
@@ -1042,8 +1076,14 @@
     for xs in range(4):
         py[xs] = (dkv[0, c, xs].astype(F32) + rx[xs].astype(F32)).astype(BF)
     send(py, ry, csend.at[1], crecv.at[1], across)
+    if beside:
+        for third in range(3):
+            reducer.middle(0, third)
     half(1, yh * 2)
     send(dkv.at[1, 1 - c], rl, csend.at[2], crecv.at[2], partner)
+    if beside:
+        for third in range(3):
+            reducer.finish(0, third)
     for xs in range(4):
         for n in range(3):
             part = dq[n, :, 128 * xs : 128 * xs + 128] * 0.125
@@ -1057,6 +1097,9 @@
     for s in (2, 1, 3):
         peer = peer_of(me, "x", s)
         send(sb.at[peer["x"]], dj.at[x], jsend.at[s - 1], jrecv.at[s - 1], peer)
+    if beside:
+        for third in range(3):
+            reducer.middle(1, third)
     for s in (1, 3, 2):
         source = peer_of(me, "x", 4 - s)
         arrived(dj.at[source["x"]], jsend.at[s - 1], jrecv.at[s - 1], source)
@@ -1071,11 +1114,15 @@
             vec_out[row : row + 1] = column_sum(t)
         dh = dh + mxu(t, vj[:, at], FAR)
     dh_out[...] = dh
+    if beside:
+        for third in range(3):
+            reducer.finish(1, third)
+        reducer.end()
     for copy in sends:
         copy.wait_send()
 
 
-def backward_layer(layer, dy, rows, up, before2, before1, q, kv, logs, att, lengths, wj, wu, wd):
+def backward_layer(layer, dy, rows, up, before2, before1, q, kv, logs, att, lengths, wj, wu, wd, later):
     vmem = pl.BlockSpec(memory_space=pltpu.VMEM)
     anyspace = pl.BlockSpec(memory_space=pl.ANY)
     dma = pltpu.SemaphoreType.DMA
@@ -1089,9 +1136,12 @@
             out((128, 3072), BF),
             out((128, 768), BF),
             out((16, 768), F32),
-        ],
-        in_specs=[vmem] * 9 + [pl.BlockSpec(memory_space=pltpu.SMEM)] + [anyspace] * 3,
-        out_specs=[vmem] * 6,
+        ]
+        + ([out((3, 4, 24, 768), BF)] if layer == 0 else []),
+        in_specs=[vmem] * 9
+        + [pl.BlockSpec(memory_space=pltpu.SMEM)]
+        + [anyspace] * (3 + len(later)),
+        out_specs=[vmem] * (7 if layer == 0 else 6),
         scratch_shapes=[
             pltpu.VMEM((768, 3072), BF),
             pltpu.VMEM((768, 3072), BF),
@@ -1113,12 +1163,13 @@
             dma((3,)),
             dma((3,)),
             dma((3,)),
-        ],
+        ]
+        + (reducer_buffers() + reducer_semaphores() if layer == 0 else []),
         compiler_params=pltpu.CompilerParams(
             collective_id=3 + layer, has_side_effects=True, vmem_limit_bytes=60 * 1024 * 1024
         ),
         name="backward_layer",
-    )(dy, rows, up, before2, before1, q, kv, logs, att, lengths, wj, wu, wd)
+    )(dy, rows, up, before2, before1, q, kv, logs, att, lengths, wj, wu, wd, *later)
 
 
 def body(
@@ -1171,16 +1222,28 @@
     kept = [(hidden0, *got[1:11]), (got[0], *more[1:11])]
     outputs = [got[0].reshape(1, 128, 768), more[0].reshape(1, 128, 768)]
     grad_rows = cotangent.reshape(128, 768).astype(F32)
-    layer_grads = [None] * LAYERS
     vector_grads = [None] * LAYERS
+    later = ()
     for l in reversed(range(LAYERS)):
         hidden, q, kv, logs, att, mixed, before1, low, up, acts, before2 = kept[l]
-        grad_rows, d_joint, d_branch, d_up, d_down, vector_grads[l] = backward_layer(
-            l, grad_rows, rows_all, up, before2, before1, q, kv, logs, att, lengths, *weights_of[l]
+        grad_rows, d_joint, d_branch, d_up, d_down, vector_grads[l], *sums = backward_layer(
+            l,
+            grad_rows,
+            rows_all,
+            up,
+            before2,
+            before1,
+            q,
+            kv,
+            logs,
+            att,
+            lengths,
+            *weights_of[l],
+            later,
         )
-        layer_grads[l] = (hidden, mixed, low, acts, d_joint, d_branch, d_up, d_down)
+        later = reducer_operands(hidden, mixed, low, acts, d_joint, d_branch, d_up, d_down)
     vectors = jnp.concatenate(vector_grads)
-    joint_grad, out_grad, up_grad, down_grad, vectors = reduce_grads(layer_grads, vectors)
+    joint_grad, out_grad, up_grad, down_grad, vectors = reduce_grads(later, sums[0], vectors)
     vectors = vectors.reshape(LAYERS, 16, 768)
     owner = lax.axis_index("batch") * 4 + lax.axis_index("blk")
     own_rows = lax.dynamic_slice_in_dim(vectors[:, :8], owner * 24, 24, axis=2)

time: 339 us -> 328 us (0.968)
  Pallas kernels: 320 us -> 307 us
    pallas_call x1, Pallas kernels: 80.3 us -> 57.8 us  [reduce_grads(): pl.pallas_call(reduce_kernel, out_shape=[jax.ShapeDtypeStruct((2, 24, 230...]
    pallas_call x2, Pallas kernels: 104 us -> 114 us  [backward_layer(): pl.pallas_call(functools.partial(backward_kernel, layer), out_shape=[out(...]
where the time goes in v4:
time: 328 us; the launch traced here: 327 us
  Pallas kernels  307 us (94%)
  local copies, waits for them, and re-layouts  11.1 us (3%)
  other arithmetic  7.12 us (2%)
    pallas_call x2, Pallas kernels, forward_layer(): pl.pallas_call(functools.partial(forward_kernel, first), out_shape=[out((...  135 us
    pallas_call x2, Pallas kernels, backward_layer(): pl.pallas_call(functools.partial(backward_kernel, layer), out_shape=[out(...  114 us
    pallas_call x1, Pallas kernels, reduce_grads(): pl.pallas_call(reduce_kernel, out_shape=[jax.ShapeDtypeStruct((2, 24, 230...  57.8 us

profile of v4, /device:TPU:0, one launch (start us, length us, event | category | flops | bytes accessed | tf_op | source)
XLA Modules:
  0.0 327.2 jit_solution(13844787675635764269)
XLA Ops:
  1.3 1.7 pad_maximum_fusion.3.refs_13_
  3.0 82.4 %forward_first.1 = (bf16[128,768]{1,0:T(8,128)(2,1)}, bf16[4,192,128]{2,1,0:T(8,128)(2,1)}, bf16[4,4,384,128]{3,2,1,0:T(8,128)(2,1)}, f32[8,512]{1,0:T(8,128)}, ...) custom-call(bf16[128,768]{1,0:T(8,128)(2,1)} %bitcast.94, ...), custom_call_target="tpu_custom_call" | custom-call | tf_op jit(solution)/shard_map/forward_first/pallas_call | solution.py:875
  85.4 53.0 %forward_second.1 = (bf16[128,768]{1,0:T(8,128)(2,1)}, bf16[4,192,128]{2,1,0:T(8,128)(2,1)}, bf16[4,4,384,128]{3,2,1,0:T(8,128)(2,1)}, f32[8,512]{1,0:T(8,128)},...) custom-call(bf16[128,768]{1,0:T(8,128)(2,1)} %get-tuple-element.63.r, ...), custom_call_target="tpu_custom_call" | custom-call | tf_op jit(solution)/shard_map/forward_second/pallas_call | solution.py:875
  138.5 1.6 copy.42
  140.1 0.2 copy.40
  140.7 1.2 pad_maximum_fusion.refs_13_
  141.9 0.8 bitcast_convert_fusion.refs_0_
  142.7 52.5 %backward_layer.2 = (f32[128,768]{1,0:T(8,128)}, bf16[128,2304]{1,0:T(8,128)(2,1)}, bf16[128,768]{1,0:T(8,128)(2,1)}, bf16[128,3072]{1,0:T(8,128)(2,1)}, bf16[128,768]{1,0:T(8,128)(2,1)}, /*index=5*/f32[16,768]{1,0:T(8,128)}) custom-call(f32[128,768]{1,0:T(8,128)} %bitcast_convert_fusion.refs_0_, f32[2,8,768]{2,1,0:T(8,128)} %get-tuple-element.64.refs_2_.refs_1_, ...), custom_call_target="tpu_custom_call" | custom-call | tf_op jit(solution)/shard_map/backward_layer/pallas_call | solution.py:1130
  195.3 61.6 %backward_layer.3 = (f32[128,768]{1,0:T(8,128)}, bf16[128,2304]{1,0:T(8,128)(2,1)}, bf16[128,768]{1,0:T(8,128)(2,1)}, bf16[128,3072]{1,0:T(8,128)(2,1)}, bf16[12...) custom-call(f32[128,768]{1,0:T(8,128)} %get-tuple-element.77.refs_0_, ...), custom_call_target="tpu_custom_call" | custom-call | tf_op jit(solution)/shard_map/backward_layer/pallas_call | solution.py:1130
  256.9 1.5 pad_maximum_fusion.4.refs_6_
  258.4 0.4 copy.50
  259.1 0.2 copy.54
  259.5 1.2 pad_maximum_fusion.1.refs_0_
  260.7 57.8 %reduce_grads.1 = (f32[2,24,2304]{2,1,0:T(8,128)}, f32[2,24,768]{2,1,0:T(8,128)}, f32[2,24,3072]{2,1,0:T(8,128)}, f32[2,96,768]{2,1,0:T(8,128)}, f32[32,768]{1,0:T(8,128)}) custom-call(bf16[2,2688,128]{2,1,0:T(8,128)(2,1)} %pad_maximum_fusion.1.refs_0_, bf16[128,3072]{1,0:T(8,128)(2,1)} %get-tuple-element.99.refs_1_, ...), custom_call_target="tpu_custom_call" | custom-call | tf_op jit(solution)/shard_map/reduce_grads/pallas_call | solution.py:510
  318.5 0.9 slice.40
  319.4 0.7 constant_dynamic-slice_fusion.8
  320.1 0.8 slice_bitcast_fusion
  320.9 0.6 constant_dynamic-slice_fusion.7
  321.5 0.8 pad_maximum_fusion.2
  322.3 0.7 copy.74
  323.1 1.8 copy.75
  324.9 0.7 copy.76
  325.5 0.8 copy.77
  326.3 0.8 copy.78
  (41 shorter events, 1.0 us)
Async XLA Ops:
  138.4 1.7 copy-start.9
  138.4 1.9 copy-start.8
  138.4 2.1 copy-start
  140.1 1.8 copy-start.10
  195.2 61.6 %copy-start.13 = (f32[16,768]{1,0:T(8,128)S(1)}, f32[16,768]{1,0:T(8,128)}, u32[]{:S(2)}) copy-start(f32[16,768]{1,0:T(8,128)} %get-tuple-element.105) | copy-start | bytes 147460
  195.3 63.1 %copy-start.2 = (bf16[128,3072]{1,0:T(8,128)(2,1)S(1)}, bf16[128,3072]{1,0:T(8,128)(2,1)}, u32[]{:S(2)}) copy-start(bf16[128,3072]{1,0:T(8,128)(2,1)} %get-tuple-element.97) | copy-start | bytes 2359300
  256.8 2.0 copy-start.7
  256.8 2.2 copy-start.6
  256.9 2.4 copy-start.1
  259.5 62.1 %copy-start.11 = (bf16[128,768]{1,0:T(8,128)(2,1)S(1)}, bf16[128,768]{1,0:T(8,128)(2,1)}, u32[]{:S(2)}) copy-start(bf16[128,768]{1,0:T(8,128)(2,1)} %get-tuple-element.67) | copy-start | bytes 589828
  260.7 61.6 %copy-start.5 = (f32[128,768]{1,0:T(8,128)S(1)}, f32[128,768]{1,0:T(8,128)}, u32[]{:S(2)}) copy-start(f32[128,768]{1,0:T(8,128)} %get-tuple-element.95) | copy-start | bytes 1179652
  318.5 6.4 %copy-start.12 = (f32[2,24,768]{2,1,0:T(8,128)S(1)}, f32[2,24,768]{2,1,0:T(8,128)}, u32[]{:S(2)}) copy-start(f32[2,24,768]{2,1,0:T(8,128)} %get-tuple-element.139) | copy-start | bytes 442372
  318.5 7.1 %copy-start.4 = (f32[2,24,3072]{2,1,0:T(8,128)S(1)}, f32[2,24,3072]{2,1,0:T(8,128)}, u32[]{:S(2)}) copy-start(f32[2,24,3072]{2,1,0:T(8,128)} %get-tuple-element.143) | copy-start | bytes 1769476
  318.5 7.9 %copy-start.3 = (f32[2,96,768]{2,1,0:T(8,128)S(1)}, f32[2,96,768]{2,1,0:T(8,128)}, u32[]{:S(2)}) copy-start(f32[2,96,768]{2,1,0:T(8,128)} %get-tuple-element.145) | copy-start | bytes 1769476

commit v5 on v4

--- a/solution.py
+++ b/solution.py
@@ -204,7 +204,11 @@
 NEVER = ()
 FIRST_PIECES = (
     feed_pieces(0, ("y", "z", "x"), NEVER)
-    + joint_pieces(2, NEVER)
+    + (
+        (2, 0, 1280, ("y", "z"), False, NEVER),
+        (2, 1280, 1024, ("z", "y"), False, NEVER),
+        (2, 2304, 768, ("z", "y"), False, NEVER),
+    )
     + joint_pieces(3, NEVER)
     + ((4, 0, 256, ("y", "z"), True, NEVER),)
 )
@@ -241,13 +245,10 @@
         for copy in self.away + self.here:
             copy.start()
 
-    def exchanged(self):
-        for copy in self.here:
-            copy.wait()
-        for copy in self.away:
-            copy.wait_recv()
-
     def products(self, t):
+        for j in ((0, 1), (2,), (3, 4))[t]:
+            self.here[j].wait()
+            self.away[j].wait_recv()
         for q in range(4):
             unit = (0, 1 + q, 5 if q < 3 else 6)[t]
             col = (q * 768, 3072, 3840 + q * 768)[t]
@@ -362,14 +363,16 @@
 
 
 def reduce_kernel(*refs):
-    s2_in, vec_in = refs[5:7]
+    operands = refs[:5]
+    s2_in, vec_first, vec_last = refs[5:8]
+    refs = refs[1:]
     joint_out, out_out, up_out, down_out, vec_out = refs[7:12]
     s2, r3, last, vc, va = refs[20:25]
     ps, pr, vs, vr = refs[30:]
     me = my_place()
     layers = (1, 0)
     f32 = jnp.float32
-    reducer = Reducer(me, refs[:5], refs[12:20], s2.at[0], refs[25:30])
+    reducer = Reducer(me, operands, refs[12:20], s2.at[0], refs[25:30])
     greet_all(me)
     reducer.exchange()
 
@@ -406,7 +409,7 @@
             total = part if total is None else total + part
         return total
 
-    vec_start(0, vec_in[...])
+    vec_start(0, jnp.concatenate([vec_first[...], vec_last[...]], axis=0))
 
     sends = []
 
@@ -442,7 +445,6 @@
     s2[1] = s2_in[...]
     for t in range(3):
         third_phase(1, t)
-    reducer.exchanged()
     for t in range(3):
         reducer.products(t)
     vec_start(1, vec_finish(0))
@@ -516,7 +518,7 @@
             jax.ShapeDtypeStruct((2, 96, 768), jnp.float32),
             jax.ShapeDtypeStruct((32, 768), jnp.float32),
         ],
-        in_specs=[anyspace] * 5 + [vmem] * 2,
+        in_specs=[anyspace] * 5 + [vmem] * 3,
         out_specs=[vmem] * 5,
         scratch_shapes=reducer_buffers()
         + [
@@ -532,7 +534,7 @@
             collective_id=1, has_side_effects=True, vmem_limit_bytes=60 * 1024 * 1024
         ),
         name="reduce_grads",
-    )(*operands, later, vectors)
+    )(*operands, later, *vectors)
 
 
 FAR = (((1,), (1,)), ((), ()))
@@ -616,7 +618,8 @@
         shards.append(own_small)
     lands = [vu, vd, vj, gathered[3], vv] if first else [vu, vd]
     plan = Gather(me, FIRST_PIECES if first else SECOND_PIECES, shards, lands, refs)
-    feed, joint, later, small = (0, 1, 2), (3, 4), (5, 6), (7,)
+    joint, later, small = (3, 4), (6, 7), (8,)
+    feed = (0, 1, 2, 5) if first else (0, 1, 2)
     x, c = me["x"], me["c"]
     yh = me["y"] // 2
     k = yh * 2 + c
@@ -654,19 +657,26 @@
         plan.close_all(1, *small, *joint)
         for i in small + joint:
             plan.complete(i)
-        load(vj, gathered[2])
         rsum[...] = jnp.zeros_like(rsum)
         usum[...] = jnp.zeros_like(usum)
-        for o in range(32):
-            z, yl, yh, core = o // 8, (o // 4) % 2, (o // 2) % 2, o % 2
-            at, up_at = (24 * o) // 128 * 128, (96 * o) // 128 * 128
-            for l in range(2):
+
+        def small_rows(l):
+            for o in range(32):
+                z, yl, yh, core = o // 8, (o // 4) % 2, (o // 2) % 2, o % 2
+                at = (24 * o) // 128 * 128
                 part = vv[z, yl, yh, core, 16 * l : 16 * l + 16, :].astype(F32)
                 rsum[l, :, at : at + 256] += part[0:8]
-                usum[l, 0:1, up_at : up_at + 256] += part[8:9]
-        for l in range(2):
             rows_out[l] = rsum[l, :, 0:768]
+
+        def small_adds(l):
+            for o in range(32):
+                z, yl, yh, core = o // 8, (o // 4) % 2, (o // 2) % 2, o % 2
+                at = (96 * o) // 128 * 128
+                part = vv[z, yl, yh, core, 16 * l : 16 * l + 16, :].astype(F32)
+                usum[l, 0:1, at : at + 256] += part[8:9]
             add_out[l] = usum[l, :, 0:3072]
+
+        small_rows(0)
         rows, up_add = rows_out.at[0], add_out.at[0]
     else:
         load(wj, vj)
@@ -717,6 +727,9 @@
         peer = peer_of(me, "x", s)
         send(qs.at[peer["x"], 0:192], qb.at[x], qsend.at[s - 1], qrecv.at[s - 1], peer)
     if first:
+        small_rows(1)
+        small_adds(0)
+        small_adds(1)
         plan.relay_all(1, 0)
         plan.close_all(1, 0)
         for i in later:
@@ -733,7 +746,7 @@
         send(slot, slot, ysend.at[s], yrecv.at[s], across)
         send(slot, slot, csend.at[s], crecv.at[s], partner)
     if first:
-        plan.relay_all(1, 1, 2)
+        plan.relay_all(1, 1, 2, 5)
         plan.relay_all(0, *later)
     for s in (1, 3, 2):
         source = peer_of(me, "x", 4 - s)
@@ -795,7 +808,7 @@
     state = half(k, k_partner, None)
     if first:
         plan.close_all(0, *later)
-        plan.close_all(1, 1, 2)
+        plan.close_all(1, 1, 2, 5)
         plan.relay_all(2, 0)
     else:
         plan.relay_all(1, 1, 2)
@@ -829,6 +842,8 @@
     plan.close_all(2, 0)
     for i in feed:
         plan.complete(i)
+    if first:
+        load(vj, gathered[2])
     load(vu, gathered[0])
     load(vd, gathered[1])
     for s in (1, 3, 2):
@@ -988,7 +1003,7 @@
         return jnp.sum(a.astype(F32), axis=0, keepdims=True)
 
     vec_out[...] = jnp.zeros_like(vec_out)
-    d_second, gain_grad, shift_grad = norm_backward(before2[...], rows[6:7], dy[...])
+    d_second, gain_grad, shift_grad = norm_backward(before2[...], rows[6:7], dy[...].astype(F32))
     vec_out[6:7] = gain_grad
     vec_out[7:8] = shift_grad
     df = d_second.astype(BF)
@@ -1021,7 +1036,6 @@
         peer = peer_of(me, "x", s)
         send(das.at[peer["x"]], dab.at[x], asend.at[s - 1], arecv.at[s - 1], peer)
     if beside:
-        reducer.exchanged()
         for third in range(3):
             reducer.products(third)
     for s in (1, 3, 2):
@@ -1221,7 +1235,7 @@
     ]
     kept = [(hidden0, *got[1:11]), (got[0], *more[1:11])]
     outputs = [got[0].reshape(1, 128, 768), more[0].reshape(1, 128, 768)]
-    grad_rows = cotangent.reshape(128, 768).astype(F32)
+    grad_rows = cotangent.reshape(128, 768)
     vector_grads = [None] * LAYERS
     later = ()
     for l in reversed(range(LAYERS)):
@@ -1242,8 +1256,9 @@
             later,
         )
         later = reducer_operands(hidden, mixed, low, acts, d_joint, d_branch, d_up, d_down)
-    vectors = jnp.concatenate(vector_grads)
-    joint_grad, out_grad, up_grad, down_grad, vectors = reduce_grads(later, sums[0], vectors)
+    joint_grad, out_grad, up_grad, down_grad, vectors = reduce_grads(
+        later, sums[0], vector_grads
+    )
     vectors = vectors.reshape(LAYERS, 16, 768)
     owner = lax.axis_index("batch") * 4 + lax.axis_index("blk")
     own_rows = lax.dynamic_slice_in_dim(vectors[:, :8], owner * 24, 24, axis=2)

time: 328 us -> 324 us (0.988)
  no operation moved by 1% of the time
where the time goes in v5:
time: 324 us; the launch traced here: 323 us
  Pallas kernels  305 us (94%)
  local copies, waits for them, and re-layouts  11.5 us (4%)
  other arithmetic  4.85 us (1%)
    pallas_call x2, Pallas kernels, forward_layer(): pl.pallas_call(functools.partial(forward_kernel, first), out_shape=[out((...  135 us
    pallas_call x2, Pallas kernels, backward_layer(): pl.pallas_call(functools.partial(backward_kernel, layer), out_shape=[out(...  113 us
    pallas_call x1, Pallas kernels, reduce_grads(): pl.pallas_call(reduce_kernel, out_shape=[jax.ShapeDtypeStruct((2, 24, 230...  57.5 us

profile of v5, /device:TPU:0, one launch (start us, length us, event | category | flops | bytes accessed | tf_op | source)
XLA Modules:
  0.0 322.9 jit_solution(9218966073322081575)
XLA Ops:
  1.3 1.7 pad_maximum_fusion.3.refs_13_
  3.0 81.7 %forward_first.1 = (bf16[128,768]{1,0:T(8,128)(2,1)}, bf16[4,192,128]{2,1,0:T(8,128)(2,1)}, bf16[4,4,384,128]{3,2,1,0:T(8,128)(2,1)}, f32[8,512]{1,0:T(8,128)}, ...) custom-call(bf16[128,768]{1,0:T(8,128)(2,1)} %bitcast.92, ...), custom_call_target="tpu_custom_call" | custom-call | tf_op jit(solution)/shard_map/forward_first/pallas_call | solution.py:890
  84.7 52.9 %forward_second.1 = (bf16[128,768]{1,0:T(8,128)(2,1)}, bf16[4,192,128]{2,1,0:T(8,128)(2,1)}, bf16[4,4,384,128]{3,2,1,0:T(8,128)(2,1)}, f32[8,512]{1,0:T(8,128)},...) custom-call(bf16[128,768]{1,0:T(8,128)(2,1)} %get-tuple-element.63.r, ...), custom_call_target="tpu_custom_call" | custom-call | tf_op jit(solution)/shard_map/forward_second/pallas_call | solution.py:890
  137.6 1.6 copy.42
  139.3 0.2 copy.40
  139.5 0.2 copy.46
  139.9 1.2 pad_maximum_fusion.refs_13_
  141.1 51.0 %backward_layer.2 = (f32[128,768]{1,0:T(8,128)}, bf16[128,2304]{1,0:T(8,128)(2,1)}, bf16[128,768]{1,0:T(8,128)(2,1)}, bf16[128,3072]{1,0:T(8,128)(2,1)}, bf16[128,768]{1,0:T(8,128)(2,1)}, /*index=5*/f32[16,768]{1,0:T(8,128)}) custom-call(bf16[128,768]{1,0:T(8,128)(2,1)} %bitcast.109, f32[2,8,768]{2,1,0:T(8,128)} %get-tuple-element.64.refs_2_.refs_1_, ...), custom_call_target="tpu_custom_call" | custom-call | tf_op jit(solution)/shard_map/backward_layer/pallas_call | solution.py:1144
  192.1 61.9 %backward_layer.3 = (f32[128,768]{1,0:T(8,128)}, bf16[128,2304]{1,0:T(8,128)(2,1)}, bf16[128,768]{1,0:T(8,128)(2,1)}, bf16[128,3072]{1,0:T(8,128)(2,1)}, bf16[12...) custom-call(f32[128,768]{1,0:T(8,128)} %get-tuple-element.77.refs_0_, ...), custom_call_target="tpu_custom_call" | custom-call | tf_op jit(solution)/shard_map/backward_layer/pallas_call | solution.py:1144
  254.1 0.4 copy.50
  254.5 0.4 copy-done.7
  255.1 0.2 copy.54
  255.5 1.2 pad_maximum_fusion.1.refs_0_
  256.7 57.5 %reduce_grads.1 = (f32[2,24,2304]{2,1,0:T(8,128)}, f32[2,24,768]{2,1,0:T(8,128)}, f32[2,24,3072]{2,1,0:T(8,128)}, f32[2,96,768]{2,1,0:T(8,128)}, f32[32,768]{1,0:T(8,128)}) custom-call(bf16[2,2688,128]{2,1,0:T(8,128)(2,1)} %pad_maximum_fusion.1.refs_0_, bf16[128,3072]{1,0:T(8,128)(2,1)} %get-tuple-element.99.refs_1_, ...), custom_call_target="tpu_custom_call" | custom-call | tf_op jit(solution)/shard_map/reduce_grads/pallas_call | solution.py:512
  314.3 0.9 slice.40
  315.2 0.7 constant_dynamic-slice_fusion.8
  315.8 0.8 slice_bitcast_fusion
  316.7 0.6 constant_dynamic-slice_fusion.7
  317.3 0.8 pad_maximum_fusion.2
  318.1 0.7 copy.74
  318.8 1.8 copy.75
  320.6 0.7 copy.76
  321.3 0.8 copy.77
  322.1 0.8 copy.78
  (35 shorter events, 0.9 us)
Async XLA Ops:
  137.6 1.7 copy-start.9
  137.6 1.9 copy-start.8
  137.6 2.1 copy-start
  192.1 61.9 %copy-start.2 = (bf16[128,3072]{1,0:T(8,128)(2,1)S(1)}, bf16[128,3072]{1,0:T(8,128)(2,1)}, u32[]{:S(2)}) copy-start(bf16[128,3072]{1,0:T(8,128)(2,1)} %get-tuple-element.97) | copy-start | bytes 2359300
  254.0 0.9 copy-start.7
  254.0 1.1 copy-start.6
  254.0 1.3 copy-start.1
  255.5 61.8 %copy-start.10 = (bf16[128,768]{1,0:T(8,128)(2,1)S(1)}, bf16[128,768]{1,0:T(8,128)(2,1)}, u32[]{:S(2)}) copy-start(bf16[128,768]{1,0:T(8,128)(2,1)} %get-tuple-element.67) | copy-start | bytes 589828
  256.7 61.4 %copy-start.5 = (f32[128,768]{1,0:T(8,128)S(1)}, f32[128,768]{1,0:T(8,128)}, u32[]{:S(2)}) copy-start(f32[128,768]{1,0:T(8,128)} %get-tuple-element.95) | copy-start | bytes 1179652
  314.2 6.4 %copy-start.11 = (f32[2,24,768]{2,1,0:T(8,128)S(1)}, f32[2,24,768]{2,1,0:T(8,128)}, u32[]{:S(2)}) copy-start(f32[2,24,768]{2,1,0:T(8,128)} %get-tuple-element.139) | copy-start | bytes 442372
  314.2 7.1 %copy-start.4 = (f32[2,24,3072]{2,1,0:T(8,128)S(1)}, f32[2,24,3072]{2,1,0:T(8,128)}, u32[]{:S(2)}) copy-start(f32[2,24,3072]{2,1,0:T(8,128)} %get-tuple-element.143) | copy-start | bytes 1769476
  314.3 7.9 %copy-start.3 = (f32[2,96,768]{2,1,0:T(8,128)S(1)}, f32[2,96,768]{2,1,0:T(8,128)}, u32[]{:S(2)}) copy-start(f32[2,96,768]{2,1,0:T(8,128)} %get-tuple-element.145) | copy-start | bytes 1769476
